TPU v7x, 32 devices: a whole 2x2x4 slice. The times are simulated.
32 devices in a mesh: dp: 8 (over z, x), tensor: 4 (over y, core).
Axes of the slice: x: 2, y: 2, z: 4, core: 2. Of those that a mesh axis runs over, the one named last changes fastest.
Arguments:
- resid: bfloat16 [8192, 1536], P(('dp', 'tensor')), may hold values from -6 to 6
- segment_ids: int32 [8192], P('dp'), may hold values from 0 to 127, as said below
- cotangent: float32 [8192, 1536], P(('dp', 'tensor')), may hold values from -6 to 6
- w_z: bfloat16 [2, 1536, 3072], P(None, 'dp', 'tensor'), may hold values from -0.15625 to 0.15625
- w_x: bfloat16 [2, 1536, 3072], P(None, 'dp', 'tensor'), may hold values from -0.15625 to 0.15625
- w_bc: bfloat16 [2, 1536, 256], P(None, ('dp', 'tensor')), may hold values from -0.15625 to 0.15625
- w_dt: bfloat16 [2, 1536, 48], P(None, 'dp', 'tensor'), may hold values from -0.15625 to 0.15625
- w_out: bfloat16 [2, 3072, 1536], P(None, 'tensor', 'dp'), may hold values from -0.109375 to 0.109375
- norm_gain: float32 [2, 1536], replicated, may hold values from 0.5 to 1.5
- conv_x: float32 [2, 4, 3072], P(None, None, 'tensor'), may hold values from -3 to 3
- conv_bc: float32 [2, 4, 256], replicated, may hold values from -3 to 3
- a_log: float32 [2, 48], P(None, 'tensor'), may hold values from -4 to 1.5
- dt_bias: float32 [2, 48], P(None, 'tensor'), may hold values from -4.5 to -2.5
- d_skip: float32 [2, 48], P(None, 'tensor'), may hold values from 0.5 to 1.5
- gated_gain: float32 [2, 3072], P(None, 'tensor'), may hold values from 0.5 to 1.5
Outputs:
- hidden_out: float32 [8192, 1536], P(('dp', 'tensor'))
- grad_resid: float32 [8192, 1536], P(('dp', 'tensor'))
- grad_w_z: float32 [2, 1536, 3072], P(None, 'dp', 'tensor')
- grad_w_x: float32 [2, 1536, 3072], P(None, 'dp', 'tensor')
- grad_w_bc: float32 [2, 1536, 256], P(None, ('dp', 'tensor'))
- grad_w_dt: float32 [2, 1536, 48], P(None, 'dp', 'tensor')
- grad_w_out: float32 [2, 3072, 1536], P(None, 'tensor', 'dp')
- grad_norm_gain: float32 [2, 1536], replicated
- grad_conv_x: float32 [2, 4, 3072], P(None, None, 'tensor')
- grad_conv_bc: float32 [2, 4, 256], replicated
- grad_a_log: float32 [2, 48], P(None, 'tensor')
- grad_dt_bias: float32 [2, 48], P(None, 'tensor')
- grad_d_skip: float32 [2, 48], P(None, 'tensor')
- grad_gated_gain: float32 [2, 3072], P(None, 'tensor')
Inputs may be any that keep to these rules, and one draw needn't show every extreme that they name: `segment_ids`: within each sequence (aligned run of 1024 tokens) the ids never fall; each document (run of equal ids) has 102 to 999 tokens except the last of a sequence, which may be shorter; the ids of sequence i lie in 16 i to 16 i + 15, and its last document has id 16 i + 15.
All inputs are finite; a program needn't handle non-finite values.
Results may differ from a plain program's by a relative error of at most 0.019.
Values may be sent and summed in bfloat16 or wider, within the bound.
A program may use at most 192 MiB of HBM per device.

v0:
```python
import jax
import jax.numpy as jnp
from jax import lax
from jax.sharding import PartitionSpec as P

P_SIZE = 64
N = 128
LEN = 1024


highest = lax.Precision.HIGHEST
epsilon = 1e-05


def silu_slope(values):
    sigma = jax.nn.sigmoid(values)
    return sigma * (1.0 + values * (1.0 - sigma))


def document_filter(values, kernel, labels):
    width = kernel.shape[0]
    length = values.shape[0]
    total = kernel[width - 1] * values
    for steps in range(1, width):
        moved = jnp.pad(values, ((steps, 0), (0, 0)))[:length]
        earlier = jnp.pad(labels, (steps, 0), constant_values=-1)[:length]
        keep_rows = (earlier == labels).astype(values.dtype)
        total = total + kernel[width - 1 - steps] * moved * keep_rows[:, None]
    return total


def head_split(values, sequences, heads):
    return jnp.moveaxis(values.reshape(sequences, LEN, heads, -1), 2, 0)


def head_merge(values):
    heads, sequences, length, width = values.shape
    return jnp.moveaxis(values, 0, 2).reshape(sequences * length, heads * width)


def decay_table(running, visible):
    gap = jnp.where(visible, running[:, :, None] - running[:, None, :], 0.0)
    return jnp.where(visible, jnp.exp(gap), 0.0)


def contract_rows(left, right):
    return lax.dot_general(
        left, right, (((0,), (0,)), ((), ())), preferred_element_type=jnp.float32
    )


def on_device(
    resid,
    segment_ids,
    cotangent,
    w_z,
    w_x,
    w_bc,
    w_dt,
    w_out,
    norm_gain,
    conv_x,
    conv_bc,
    a_log,
    dt_bias,
    d_skip,
    gated_gain,
):
    tensor_size = lax.axis_size("tensor")
    local_rows = resid.shape[0]
    group_rows = segment_ids.shape[0]
    sequences = group_rows // LEN
    heads = a_log.shape[1]
    inner = heads * P_SIZE
    inner_all = inner * tensor_size
    layers = a_log.shape[0]
    place = jnp.arange(LEN)
    grouped = segment_ids.reshape(sequences, LEN)
    visible = (grouped[:, :, None] == grouped[:, None, :]) & (place[:, None] >= place[None, :])[
        None
    ]
    state = resid.astype(jnp.float32)
    saved = []
    for layer in range(layers):
        weight_gate, weight_inner, weight_step, weight_out = (
            lax.all_gather(w_z[layer], "dp", axis=0, tiled=True),
            lax.all_gather(w_x[layer], "dp", axis=0, tiled=True),
            lax.all_gather(w_dt[layer], "dp", axis=0, tiled=True),
            lax.all_gather(w_out[layer], "dp", axis=1, tiled=True),
        )
        weight_shared = lax.all_gather(w_bc[layer], ("dp", "tensor"), axis=0, tiled=True)
        scale_in = lax.rsqrt(jnp.mean(state * state, axis=1, keepdims=True) + epsilon)
        normed = (state * scale_in * norm_gain[layer]).astype(jnp.bfloat16)
        rows_all = lax.all_gather(normed, "tensor", axis=0, tiled=True)
        gate_raw = jnp.dot(rows_all, weight_gate, preferred_element_type=jnp.float32)
        inner_raw = jnp.dot(rows_all, weight_inner, preferred_element_type=jnp.float32)
        step_raw = jnp.dot(rows_all, weight_step, preferred_element_type=jnp.float32)
        shared_raw = jnp.dot(rows_all, weight_shared, preferred_element_type=jnp.float32)
        inner_conv = document_filter(inner_raw, conv_x[layer], segment_ids)
        inner_act = jax.nn.silu(inner_conv)
        shared_conv = document_filter(shared_raw, conv_bc[layer], segment_ids)
        shared_act = jax.nn.silu(shared_conv)
        inner_low = inner_act.astype(jnp.bfloat16)
        keys_low = shared_act[:, :N].astype(jnp.bfloat16).reshape(sequences, LEN, N)
        query_low = shared_act[:, N:].astype(jnp.bfloat16).reshape(sequences, LEN, N)
        step_size = jax.nn.softplus(step_raw + dt_bias[layer])
        rate = -jnp.exp(a_log[layer])
        cumulative = jnp.cumsum((step_size * rate).reshape(sequences, LEN, heads), axis=1)
        coupling = jnp.einsum(
            "sqn,skn->sqk", query_low, keys_low, preferred_element_type=jnp.float32
        )
        decay_heads = jnp.moveaxis(cumulative, 2, 0)
        step_heads = jnp.moveaxis(step_size.reshape(sequences, LEN, heads), 2, 0)
        inner_heads = head_split(inner_low, sequences, heads)

        def mix_one(item, coupling=coupling):
            decay_one, step_one, inner_one = item
            decay = decay_table(decay_one, visible)
            weights = (coupling * decay * step_one[:, None, :]).astype(jnp.bfloat16)
            return jnp.einsum(
                "sqk,skp->sqp", weights, inner_one, preferred_element_type=jnp.float32
            )

        mixed = head_merge(lax.map(mix_one, (decay_heads, step_heads, inner_heads)))
        skip_wide = jnp.repeat(d_skip[layer], P_SIZE)
        output_full = mixed + inner_act * skip_wide
        gate_act = jax.nn.silu(gate_raw)
        gated = output_full * gate_act
        squares = lax.psum(jnp.sum(gated * gated, axis=1), "tensor")
        scale_out = lax.rsqrt(squares / inner_all + epsilon)[:, None]
        out_low = (gated * scale_out * gated_gain[layer]).astype(jnp.bfloat16)

        def project(start, count, out_low=out_low, weight_out=weight_out):
            return jnp.dot(out_low, weight_out, preferred_element_type=jnp.float32)

        branch = lax.psum_scatter(
            project(jnp.int32(0), lax.axis_size("tensor") * local_rows),
            "tensor",
            scatter_dimension=0,
            tiled=True,
        )
        saved.append(
            {
                "state": state,
                "scale_in": scale_in,
                "rows_all": rows_all,
                "gate_raw": gate_raw,
                "inner_raw": inner_raw,
                "inner_conv": inner_conv,
                "inner_act": inner_act,
                "shared_raw": shared_raw,
                "shared_conv": shared_conv,
                "keys_low": keys_low,
                "query_low": query_low,
                "step_raw": step_raw,
                "step_size": step_size,
                "rate": rate,
                "coupling": coupling,
                "decay_heads": decay_heads,
                "step_heads": step_heads,
                "inner_heads": inner_heads,
                "skip_wide": skip_wide,
                "output_full": output_full,
                "gate_act": gate_act,
                "gated": gated,
                "scale_out": scale_out,
                "out_low": out_low,
                "weight_gate": weight_gate,
                "weight_inner": weight_inner,
                "weight_step": weight_step,
                "weight_out": weight_out,
                "weight_shared": weight_shared,
            }
        )
        state = state + branch
    grad_state = cotangent
    grad_gate_list = [None] * layers
    grad_inner_list = [None] * layers
    grad_shared_list = [None] * layers
    grad_step_list = [None] * layers
    grad_out_list = [None] * layers
    grad_norm_list = [None] * layers
    grad_conv_inner_list = [None] * layers
    grad_conv_shared_list = [None] * layers
    grad_alog_list = [None] * layers
    grad_bias_list = [None] * layers
    grad_skip_list = [None] * layers
    grad_gain_list = [None] * layers
    for layer in reversed(range(layers)):
        keep = saved[layer]
        weight_gate, weight_inner, weight_step, weight_out = (
            lax.all_gather(w_z[layer], "dp", axis=0, tiled=True),
            lax.all_gather(w_x[layer], "dp", axis=0, tiled=True),
            lax.all_gather(w_dt[layer], "dp", axis=0, tiled=True),
            lax.all_gather(w_out[layer], "dp", axis=1, tiled=True),
        )
        weight_shared = lax.all_gather(w_bc[layer], ("dp", "tensor"), axis=0, tiled=True)
        gated = keep["gated"]
        scale_out = keep["scale_out"]
        rows_all = keep["rows_all"]
        branch_low = grad_state.astype(jnp.bfloat16)
        grad_all = lax.all_gather(branch_low, "tensor", axis=0, tiled=True)
        grad_weight_out = contract_rows(keep["out_low"], grad_all)
        grad_normed_out = lax.dot_general(
            grad_all, weight_out, (((1,), (1,)), ((), ())), preferred_element_type=jnp.float32
        )
        gained = grad_normed_out * gated_gain[layer]
        grad_gain_list[layer] = jnp.sum(grad_normed_out * gated * scale_out, axis=0)
        cross = lax.psum(jnp.sum(gained * gated, axis=1), "tensor")
        grad_gated = scale_out * gained - gated * scale_out**3 * (cross / inner_all)[:, None]
        grad_output = (grad_gated * keep["gate_act"]).astype(jnp.bfloat16)
        grad_gate = (grad_gated * keep["output_full"] * silu_slope(keep["gate_raw"])).astype(
            jnp.bfloat16
        )
        inner_act = keep["inner_act"]
        grad_skip_list[layer] = jnp.sum(
            (grad_output.astype(jnp.float32) * inner_act).reshape(group_rows, heads, P_SIZE),
            axis=(0, 2),
        )
        grad_heads = head_split(grad_output, sequences, heads)
        coupling = keep["coupling"]

        def mix_back(total, item, coupling=coupling):
            decay_one, step_one, inner_one, grad_one = item
            decay = decay_table(decay_one, visible)
            weights = (coupling * decay * step_one[:, None, :]).astype(jnp.bfloat16)
            grad_weights = jnp.einsum(
                "sqp,skp->sqk", grad_one, inner_one, preferred_element_type=jnp.float32
            )
            grad_inner = jnp.einsum(
                "sqk,sqp->skp", weights, grad_one, preferred_element_type=jnp.float32
            )
            through = grad_weights * coupling * decay
            spread = through * step_one[:, None, :]
            grad_step = jnp.sum(through, axis=1)
            grad_running = jnp.sum(spread, axis=2) - jnp.sum(spread, axis=1)
            grad_coupling = (grad_weights * decay * step_one[:, None, :]).astype(jnp.bfloat16)
            return (
                total + grad_coupling.astype(jnp.float32),
                (grad_inner, grad_step, grad_running),
            )

        empty = jnp.zeros((sequences, LEN, LEN), jnp.float32)
        grad_coupling_sum, (grad_inner_heads, grad_step_heads, grad_running_heads) = lax.scan(
            mix_back,
            empty,
            (keep["decay_heads"], keep["step_heads"], keep["inner_heads"], grad_heads),
        )
        keys_wide = keep["keys_low"].astype(jnp.float32)
        query_wide = keep["query_low"].astype(jnp.float32)
        grad_query = jnp.einsum("sqk,skn->sqn", grad_coupling_sum, keys_wide, precision=highest)
        grad_keys = jnp.einsum("sqk,sqn->skn", grad_coupling_sum, query_wide, precision=highest)
        grad_shared_act = jnp.concatenate(
            [grad_keys.reshape(group_rows, N), grad_query.reshape(group_rows, N)], axis=1
        )
        grad_inner_act = (
            head_merge(grad_inner_heads) + grad_output.astype(jnp.float32) * keep["skip_wide"]
        )
        grad_running_all = jnp.moveaxis(grad_running_heads, 0, 2)
        grad_rate_term = lax.cumsum(grad_running_all, axis=1, reverse=True).reshape(
            group_rows, heads
        )
        rate = keep["rate"]
        step_size = keep["step_size"]
        grad_step_total = (
            jnp.moveaxis(grad_step_heads, 0, 2).reshape(group_rows, heads) + grad_rate_term * rate
        )
        grad_alog_list[layer] = jnp.sum(grad_rate_term * step_size, axis=0) * rate
        grad_step_raw = grad_step_total * jax.nn.sigmoid(keep["step_raw"] + dt_bias[layer])
        grad_bias_list[layer] = jnp.sum(grad_step_raw, axis=0)
        grad_step_low = grad_step_raw.astype(jnp.bfloat16)
        inner_pull = jax.vjp(
            lambda values, kernel: document_filter(values, kernel, segment_ids),
            keep["inner_raw"],
            conv_x[layer],
        )[1]
        grad_inner_raw, grad_conv_inner_list[layer] = inner_pull(
            grad_inner_act * silu_slope(keep["inner_conv"])
        )
        grad_inner_low = grad_inner_raw.astype(jnp.bfloat16)
        shared_pull = jax.vjp(
            lambda values, kernel: document_filter(values, kernel, segment_ids),
            keep["shared_raw"],
            conv_bc[layer],
        )[1]
        grad_shared_raw, grad_conv_shared_list[layer] = shared_pull(
            grad_shared_act * silu_slope(keep["shared_conv"])
        )
        grad_weight_gate = contract_rows(rows_all, grad_gate)
        grad_weight_inner = contract_rows(rows_all, grad_inner_low)
        grad_weight_step = contract_rows(rows_all, grad_step_low)
        grad_weight_shared = lax.dot_general(
            rows_all.astype(jnp.float32),
            grad_shared_raw,
            (((0,), (0,)), ((), ())),
            precision=highest,
        )
        shared_wide = weight_shared.astype(jnp.float32)

        def pull_rows(
            start,
            count,
            grad_gate=grad_gate,
            grad_inner_low=grad_inner_low,
            grad_step_low=grad_step_low,
            grad_shared_raw=grad_shared_raw,
            weight_gate=weight_gate,
            weight_inner=weight_inner,
            weight_step=weight_step,
            shared_wide=shared_wide,
        ):

            def transpose_product(values, weight):
                return lax.dot_general(
                    values, weight, (((1,), (1,)), ((), ())), preferred_element_type=jnp.float32
                )

            total = transpose_product(grad_gate, weight_gate) + transpose_product(
                grad_inner_low, weight_inner
            )
            total = total + transpose_product(grad_step_low, weight_step)
            return total + lax.dot_general(
                grad_shared_raw, shared_wide, (((1,), (1,)), ((), ())), precision=highest
            )

        grad_normed = lax.psum_scatter(
            pull_rows(jnp.int32(0), lax.axis_size("tensor") * local_rows).astype(jnp.bfloat16),
            "tensor",
            scatter_dimension=0,
            tiled=True,
        ).astype(jnp.float32)
        state_in = keep["state"]
        scale_in = keep["scale_in"]
        gained_in = grad_normed * norm_gain[layer]
        grad_norm_list[layer] = jnp.sum(grad_normed * state_in * scale_in, axis=0)
        grad_state = (
            grad_state
            + scale_in * gained_in
            - state_in * scale_in**3 * jnp.mean(gained_in * state_in, axis=1, keepdims=True)
        )
        (
            grad_gate_list[layer],
            grad_inner_list[layer],
            grad_step_list[layer],
            grad_out_list[layer],
        ) = (
            lax.psum_scatter(
                grad_weight_gate.astype(jnp.bfloat16), "dp", scatter_dimension=0, tiled=True
            ).astype(jnp.float32),
            lax.psum_scatter(
                grad_weight_inner.astype(jnp.bfloat16), "dp", scatter_dimension=0, tiled=True
            ).astype(jnp.float32),
            lax.psum_scatter(
                grad_weight_step.astype(jnp.bfloat16), "dp", scatter_dimension=0, tiled=True
            ).astype(jnp.float32),
            lax.psum_scatter(
                grad_weight_out.astype(jnp.bfloat16), "dp", scatter_dimension=1, tiled=True
            ).astype(jnp.float32),
        )
        grad_shared_list[layer] = lax.psum_scatter(
            grad_weight_shared, ("dp", "tensor"), scatter_dimension=0, tiled=True
        )
    small = lax.psum(
        (
            jnp.stack(grad_conv_inner_list),
            jnp.stack(grad_gain_list),
            jnp.stack(grad_alog_list),
            jnp.stack(grad_bias_list),
            jnp.stack(grad_skip_list),
        ),
        "dp",
    )
    common = lax.psum(
        (jnp.stack(grad_norm_list), jnp.stack(grad_conv_shared_list)), ("dp", "tensor")
    )
    return (
        state,
        grad_state,
        jnp.stack(grad_gate_list),
        jnp.stack(grad_inner_list),
        jnp.stack(grad_shared_list),
        jnp.stack(grad_step_list),
        jnp.stack(grad_out_list),
        common[0],
        small[0],
        common[1],
        small[2],
        small[3],
        small[4],
        small[1],
    )


def solution(mesh):
    placed = (
        P(("dp", "tensor"), None),
        P("dp"),
        P(("dp", "tensor"), None),
        P(None, "dp", "tensor"),
        P(None, "dp", "tensor"),
        P(None, ("dp", "tensor"), None),
        P(None, "dp", "tensor"),
        P(None, "tensor", "dp"),
        P(),
        P(None, None, "tensor"),
        P(),
        P(None, "tensor"),
        P(None, "tensor"),
        P(None, "tensor"),
        P(None, "tensor"),
    )
    return jax.shard_map(
        on_device,
        mesh=mesh,
        in_specs=placed,
        out_specs=(
            P(("dp", "tensor"), None),
            P(("dp", "tensor"), None),
            P(None, "dp", "tensor"),
            P(None, "dp", "tensor"),
            P(None, ("dp", "tensor"), None),
            P(None, "dp", "tensor"),
            P(None, "tensor", "dp"),
            P(),
            P(None, None, "tensor"),
            P(),
            P(None, "tensor"),
            P(None, "tensor"),
            P(None, "tensor"),
            P(None, "tensor"),
        ),
        check_vma=False,
    )
```

profile of v0, /device:TPU:0, one launch (start us, length us, event | category | flops | bytes accessed | tf_op | source)
XLA Modules:
  0.0 1894.0 jit_solution(6706540450940822522)
XLA Ops:
  15.4 45.9 %all-gather.1 = bf16[1,1536,256]{2,1,0:T(8,128)(2,1)S(1)} all-gather(bf16[1,48,256]{2,1,0:T(8,128)(2,1)S(1)} %get-tuple-element.727), channel_id=3, replica_groups=mesh['dp'=8,'tensor'=4] {'dp','tensor'}, dimensions={1}, use_global_device_ids=true | all-gather | bytes 811008 | tf_op jit(solution)/shard_map/all_gather | solution.py:91
  61.8 34.1 %all-gather = bf16[1,1536,12]{2,0,1:T(2,128)(2,1)S(1)} all-gather(bf16[1,192,12]{2,0,1:T(2,128)(2,1)S(1)} %copy.205), channel_id=2, replica_groups=mesh['dp'=8,'tensor'=4] {'dp'}, dimensions={1}, use_global_device_ids=true | all-gather | bytes 41472 | tf_op jit(solution)/shard_map/all_gather | solution.py:88
  132.1 52.6 %while.56 = (s32[]{:T(128)}, f32[12,1,1024,64]{2,3,1,0:T(8,128)}, f32[12,1,1024]{2,1,0:T(1,128)S(1)}, f32[1,1024,1024]{2,1,0:T(8,128)}, f32[12,1,1024]{2,1,0:T(1...) while((s32[]{:T(128)}, f32[12,1,1024,64]{2,3,1,0:T(8,128)}, ...), condition=%wide.region_4.5_spmd.clone, body=%wide.region_3.4_spmd.clone.sunk | while | flops 143654912 | bytes 4756569 | solution.py:124
  188.3 8.2 multiply_reduce_fusion.17
  196.4 6.3 psum.77
  203.3 12.2 all-gather.33.cloned.1.call-done
  215.6 7.9 fusion.114
  223.6 57.1 %reduce-scatter.19.cloned.1.call-done = f32[256,1536]{1,0:T(8,128)} async-done(((f32[1024,1536]{1,0:T(8,128)}), f32[256,1536]{1,0:T(8,128)}) %reduce-scatter.19.cloned.1.call-update) | async-done | bytes 1572880 | tf_op jit(solution)/shard_map/reduce_scatter | solution.py:136
  288.2 32.4 %all-gather.5 = bf16[1,1536,12]{2,0,1:T(2,128)(2,1)S(1)} all-gather(bf16[1,192,12]{2,0,1:T(2,128)(2,1)S(1)} %copy.206), channel_id=7, replica_groups=mesh['dp'=8,'tensor'=4] {'dp'}, dimensions={1}, use_global_device_ids=true | all-gather | bytes 41472 | tf_op jit(solution)/shard_map/all_gather | solution.py:88
  321.0 47.7 %all-gather.6 = bf16[1,1536,256]{2,1,0:T(8,128)(2,1)} all-gather(bf16[1,48,256]{2,1,0:T(8,128)(2,1)S(1)} %get-tuple-element.726), channel_id=8, replica_groups=mesh['dp'=8,'tensor'=4] {'dp','tensor'}, dimensions={1}, use_global_device_ids=true | all-gather | bytes 811008 | tf_op jit(solution)/shard_map/all_gather | solution.py:91
  399.7 52.4 %while.57 = (s32[]{:T(128)}, f32[12,1,1024,64]{2,3,1,0:T(8,128)}, f32[12,1,1024]{2,1,0:T(1,128)S(1)}, f32[1,1024,1024]{2,1,0:T(8,128)}, f32[12,1,1024]{2,1,0:T(1...) while((s32[]{:T(128)}, f32[12,1,1024,64]{2,3,1,0:T(8,128)}, ...), condition=%wide.region_12.13_spmd.clone, body=%wide.region_11.12_spmd.clone.sunk | while | flops 143654912 | bytes 4756569 | solution.py:124
  455.6 8.1 multiply_reduce_fusion.16
  463.7 6.4 psum.78
  476.3 29.2 %all-gather.25.cloned.1.call-done = bf16[1024,1536]{1,0:T(8,128)(2,1)} async-done(((bf16[256,1536]{1,0:T(8,128)(2,1)}), bf16[1024,1536]{1,0:T(8,128)(2,1)}) %all-gather.25.cloned.1.call-update) | async-done | bytes 3145744 | tf_op jit(solution)/shard_map/all_gather | solution.py:202
  505.5 8.6 multiply_reduce_fusion.4
  514.1 6.3 psum.79
  520.4 8.9 fusion.92
  533.9 161.0 %while.58 = (s32[]{:T(128)}, f32[1,1024,1024]{2,1,0:T(8,128)}, f32[12,1,1024,64]{2,3,1,0:T(8,128)}, f32[12,1,1024]{2,0,1:T(8,128)S(1)}, f32[12,1,1024]{2,1,0:T(1...) while((s32[]{:T(128)}, f32[1,1024,1024]{2,1,0:T(8,128)}, ...), condition=%wide.region_22.23_spmd.clone, body=%wide.region_18.22_spmd.clone.sunk | while | flops 303036416 | bytes 42842288 | solution.py:244
  546.1 6.2 convert_add_fusion.6
  586.7 6.2 convert_add_fusion.6
  654.2 6.2 convert_add_fusion.6
  719.2 15.0 reduce-window.34
  753.6 6.9 add_convert_fusion.1
  761.3 7.9 fusion.102
  769.3 30.5 %reduce-scatter.23.cloned.1.call-done = bf16[256,1536]{1,0:T(8,128)(2,1)} async-done(((bf16[1024,1536]{1,0:T(8,128)(2,1)}), bf16[256,1536]{1,0:T(8,128)(2,1)}) %reduce-scatter.23.cloned.1.call-update) | async-done | bytes 786448 | tf_op jit(solution)/shard_map/reduce_scatter | solution.py:326
  801.9 58.7 %reduce-scatter.21.cloned.1.call-done = f32[256,1536]{1,0:T(8,128)} async-done(((f32[1024,1536]{1,0:T(8,128)}), f32[256,1536]{1,0:T(8,128)}) %reduce-scatter.21.cloned.1.call-update) | async-done | bytes 1572880 | tf_op jit(solution)/shard_map/reduce_scatter | solution.py:136
  867.7 26.6 %all-gather.27.cloned.1.call-done = bf16[1024,1536]{1,0:T(8,128)(2,1)} async-done(((bf16[256,1536]{1,0:T(8,128)(2,1)}), bf16[1024,1536]{1,0:T(8,128)(2,1)}) %all-gather.27.cloned.1.call-update) | async-done | bytes 3145744 | tf_op jit(solution)/shard_map/all_gather | solution.py:202
  894.4 8.0 multiply_reduce_fusion.5
  908.3 7.3 fusion.95
  920.3 167.9 %while.59 = (s32[]{:T(128)}, f32[1,1024,1024]{2,1,0:T(8,128)}, f32[12,1,1024,64]{2,3,1,0:T(8,128)}, f32[12,1,1024]{2,0,1:T(8,128)S(1)}, f32[12,1,1024]{2,1,0:T(1...) while((s32[]{:T(128)}, f32[1,1024,1024]{2,1,0:T(8,128)}, ...), condition=%wide.region_33.34_spmd.clone, body=%wide.region_29.33_spmd.clone.sunk | while | flops 303036416 | bytes 42842288 | solution.py:244
  1088.2 14.9 reduce-window.36
  1105.4 6.8 fusion.206
  1129.2 7.0 convolution_convert_fusion
  1136.3 7.0 convolution_convert_fusion.1
  1143.4 6.5 convolution_convert_fusion.2
  1154.0 16.7 multiply_reduce_fusion.9
  1178.0 6.5 convolution_convert_fusion.4
  1205.3 38.6 %all-reduce.44 = (f32[2,4,768]{2,1,0:T(4,128)}, f32[2,12]{1,0:T(2,128)}, f32[2,12]{1,0:T(2,128)}, f32[2,12]{1,0:T(2,128)}, f32[2,768]{1,0:T(2,128)}) all-reduce(f32[2,4,768]{2,1,0:T(4,128)S(1)} %pad_maximum_fusion.1, f32[2,12]{1,0:T(2,128)S(1)} %get-tuple-element.765, ...), channel_id=1, replica_groups=mesh['dp'=8,'tensor'=4] {'dp'}, use_global_device_ids=true, to_apply=%region_59.60 | all-reduce | flops 7752 | bytes 62016 | tf_op jit(solution)/shard_map/psum | solution.py:363
  1245.5 24.3 %reduce-scatter.37.cloned.1.call-done = f32[48,256]{1,0:T(8,128)} async-done(((f32[1536,256]{1,0:T(8,128)}), f32[48,256]{1,0:T(8,128)}) %reduce-scatter.37.cloned.1.call-update) | async-done | bytes 49168 | tf_op jit(solution)/shard_map/reduce_scatter | solution.py:360
  1269.8 102.0 %reduce-scatter.35.cloned.1.call-done = f32[48,256]{1,0:T(8,128)} async-done(((f32[1536,256]{1,0:T(8,128)}), f32[48,256]{1,0:T(8,128)}) %reduce-scatter.35.cloned.1.call-update) | async-done | bytes 49168 | tf_op jit(solution)/shard_map/reduce_scatter | solution.py:360
  1373.3 70.2 %reduce-scatter.41.cloned.1.call-done = bf16[768,192]{0,1:T(8,128)(2,1)} async-done(((bf16[768,1536]{0,1:T(8,128)(2,1)}), bf16[768,192]{0,1:T(8,128)(2,1)}) %reduce-scatter.41.cloned.1.call-update) | async-done | bytes 294928 | tf_op jit(solution)/shard_map/reduce_scatter | solution.py:356
  1443.5 72.0 %reduce-scatter.39.cloned.1.call-done = bf16[768,192]{0,1:T(8,128)(2,1)} async-done(((bf16[768,1536]{0,1:T(8,128)(2,1)}), bf16[768,192]{0,1:T(8,128)(2,1)}) %reduce-scatter.39.cloned.1.call-update) | async-done | bytes 294928 | tf_op jit(solution)/shard_map/reduce_scatter | solution.py:356
  1517.8 69.6 %reduce-scatter.33.cloned.1.call-done = bf16[192,768]{1,0:T(8,128)(2,1)} async-done(((bf16[1536,768]{1,0:T(8,128)(2,1)}), bf16[192,768]{1,0:T(8,128)(2,1)}) %reduce-scatter.33.cloned.1.call-update) | async-done | bytes 294928 | tf_op jit(solution)/shard_map/reduce_scatter | solution.py:350
  1587.4 71.9 %reduce-scatter.31.cloned.1.call-done = bf16[192,768]{1,0:T(8,128)(2,1)} async-done(((bf16[1536,768]{1,0:T(8,128)(2,1)}), bf16[192,768]{1,0:T(8,128)(2,1)}) %reduce-scatter.31.cloned.1.call-update) | async-done | bytes 294928 | tf_op jit(solution)/shard_map/reduce_scatter | solution.py:350
  1661.4 69.8 %reduce-scatter.29.cloned.1.call-done = bf16[192,768]{1,0:T(8,128)(2,1)} async-done(((bf16[1536,768]{1,0:T(8,128)(2,1)}), bf16[192,768]{1,0:T(8,128)(2,1)}) %reduce-scatter.29.cloned.1.call-update) | async-done | bytes 294928 | tf_op jit(solution)/shard_map/reduce_scatter | solution.py:347
  1731.2 72.0 %reduce-scatter.27.cloned.1.call-done = bf16[192,768]{1,0:T(8,128)(2,1)} async-done(((bf16[1536,768]{1,0:T(8,128)(2,1)}), bf16[192,768]{1,0:T(8,128)(2,1)}) %reduce-scatter.27.cloned.1.call-update) | async-done | bytes 294928 | tf_op jit(solution)/shard_map/reduce_scatter | solution.py:347
  1805.3 37.4 %reduce-scatter.25.cloned.1.call-done = bf16[256,1536]{1,0:T(8,128)(2,1)} async-done(((bf16[1024,1536]{1,0:T(8,128)(2,1)}), bf16[256,1536]{1,0:T(8,128)(2,1)}) %reduce-scatter.25.cloned.1.call-update) | async-done | bytes 786448 | tf_op jit(solution)/shard_map/reduce_scatter | solution.py:326
  1844.4 39.9 %all-reduce.43 = (f32[2,1536]{1,0:T(2,128)}, f32[2,4,256]{2,1,0:T(4,128)}) all-reduce(f32[2,1536]{1,0:T(2,128)S(1)} %pad_maximum_fusion.2, f32[2,4,256]{2,1,0:T(4,128)S(1)} %pad_maximum_fusion.3), channel_id=1, replica_groups=mesh['dp'=8,'tensor'=4] {'dp','tensor'}, use_global_device_ids=true, to_apply=%region_50.51 | all-reduce | flops 5120 | bytes 40960 | tf_op jit(solution)/shard_map/psum | solution.py:373
  (729 shorter events, 645.1 us)
Async XLA Ops:
  7.2 89.5 %all-gather.21.cloned.1.call-start = ((), (), s32[]{:S(2)}) async-start(), calls=%async_computation.14 | async-start | bytes 3932160 | tf_op jit(solution)/shard_map/all_gather | solution.py:94
  8.1 274.9 %copy-start.56 = (f32[1536]{0:T(1024)}, f32[1536]{0:T(1024)S(1)}, u32[]{:S(2)}) copy-start(f32[1536]{0:T(1024)S(1)} %get-tuple-element.576) | copy-start | bytes 18436
  12.4 96.7 %all-gather.29.cloned.1.call-start = ((), (), s32[]{:S(2)}) async-start(), calls=%async_computation.30 | async-start | bytes 2654208 | tf_op jit(solution)/shard_map/all_gather | solution.py:87
  13.3 83.0 %copy-start.117 = (f32[2,12]{1,0:T(2,128)S(1)}, f32[2,12]{1,0:T(2,128)}, u32[]{:S(2)}) copy-start(f32[2,12]{1,0:T(2,128)} %param.35) | copy-start | bytes 292
  13.3 83.1 %copy-start.113 = (f32[2,12]{1,0:T(2,128)S(1)}, f32[2,12]{1,0:T(2,128)}, u32[]{:S(2)}) copy-start(f32[2,12]{1,0:T(2,128)} %param.34) | copy-start | bytes 292
  13.3 83.1 %copy-start.118 = (f32[2,12]{1,0:T(2,128)S(1)}, f32[2,12]{1,0:T(2,128)}, u32[]{:S(2)}) copy-start(f32[2,12]{1,0:T(2,128)} %param.36) | copy-start | bytes 292
  13.4 83.3 %copy-start.106 = (f32[2,768]{1,0:T(2,128)S(1)}, f32[2,768]{1,0:T(2,128)}, u32[]{:S(2)}) copy-start(f32[2,768]{1,0:T(2,128)} %param.37) | copy-start | bytes 18436
  13.4 174.9 %all-gather.31.cloned.1.call-start = ((), (), s32[]{:S(2)}) async-start(), calls=%async_computation.31 | async-start | bytes 2654208 | tf_op jit(solution)/shard_map/all_gather | solution.py:86
  14.4 201.2 %all-gather.33.cloned.1.call-start = ((), (), s32[]{:S(2)}) async-start(), calls=%async_computation.32 | async-start | bytes 2654208 | tf_op jit(solution)/shard_map/all_gather | solution.py:89
  15.3 265.4 %reduce-scatter.19.cloned.1.call-start = ((), (), s32[]{:S(2)}) async-start(), calls=%async_computation.15 | async-start | bytes 7864320 | tf_op jit(solution)/shard_map/reduce_scatter | solution.py:136
  61.4 331.5 %copy-start.95 = (f32[1,1,256]{2,1,0:T(1,128)}, f32[1,1,256]{2,1,0:T(1,128)S(1)}, u32[]{:S(2)}) copy-start(f32[1,1,256]{2,1,0:T(1,128)S(1)} %get-tuple-element.736) | copy-start | bytes 3076
  61.4 331.5 %copy-start.97 = (f32[1,1,256]{2,1,0:T(1,128)}, f32[1,1,256]{2,1,0:T(1,128)S(1)}, u32[]{:S(2)}) copy-start(f32[1,1,256]{2,1,0:T(1,128)S(1)} %get-tuple-element.737) | copy-start | bytes 3076
  61.5 331.5 %copy-start.101 = (f32[1,1,256]{2,1,0:T(1,128)}, f32[1,1,256]{2,1,0:T(1,128)S(1)}, u32[]{:S(2)}) copy-start(f32[1,1,256]{2,1,0:T(1,128)S(1)} %get-tuple-element.730) | copy-start | bytes 3076
  61.5 331.5 %copy-start.103 = (f32[1,1,256]{2,1,0:T(1,128)}, f32[1,1,256]{2,1,0:T(1,128)S(1)}, u32[]{:S(2)}) copy-start(f32[1,1,256]{2,1,0:T(1,128)S(1)} %get-tuple-element.731) | copy-start | bytes 3076
  61.6 318.3 %copy-start.72 = (f32[768]{0:T(1024)}, f32[768]{0:T(1024)S(1)}, u32[]{:S(2)}) copy-start(f32[768]{0:T(1024)S(1)} %get-tuple-element.560) | copy-start | bytes 9220
  96.5 275.3 %copy-start.109 = (f32[12]{0:T(128)}, f32[12]{0:T(128)S(1)}, u32[]{:S(2)}) copy-start(f32[12]{0:T(128)S(1)} %get-tuple-element.755) | copy-start | bytes 148
  96.6 91.6 %copy-start.66 = (f32[768]{0:T(1024)}, f32[768]{0:T(1024)S(1)}, u32[]{:S(2)}) copy-start(f32[768]{0:T(1024)S(1)} %mul.1121) | copy-start | bytes 9220
  96.7 118.9 %copy-start.77 = (f32[768]{0:T(1024)}, f32[768]{0:T(1024)S(1)}, u32[]{:S(2)}) copy-start(f32[768]{0:T(1024)S(1)} %get-tuple-element.579) | copy-start | bytes 9220
  96.7 423.7 %copy-start.79 = (f32[768]{0:T(1024)}, f32[768]{0:T(1024)S(1)}, u32[]{:S(2)}) copy-start(f32[768]{0:T(1024)S(1)} %get-tuple-element.578) | copy-start | bytes 9220
  223.6 145.2 %all-gather.23.cloned.1.call-start = ((), (), s32[]{:S(2)}) async-start(), calls=%async_computation.16 | async-start | bytes 3932160 | tf_op jit(solution)/shard_map/all_gather | solution.py:94
  284.7 90.9 %all-gather.35.cloned.1.call-start = ((), (), s32[]{:S(2)}) async-start(), calls=%async_computation.33 | async-start | bytes 2654208 | tf_op jit(solution)/shard_map/all_gather | solution.py:87
  285.4 170.2 %all-gather.37.cloned.1.call-start = ((), (), s32[]{:S(2)}) async-start(), calls=%async_computation.34 | async-start | bytes 2654208 | tf_op jit(solution)/shard_map/all_gather | solution.py:86
  286.2 190.2 %all-gather.39.cloned.1.call-start = ((), (), s32[]{:S(2)}) async-start(), calls=%async_computation.35 | async-start | bytes 2654208 | tf_op jit(solution)/shard_map/all_gather | solution.py:89
  286.9 218.6 %all-gather.25.cloned.1.call-start = ((), (), s32[]{:S(2)}) async-start(), calls=%async_computation.18 | async-start | bytes 3932160 | tf_op jit(solution)/shard_map/all_gather | solution.py:202
  287.9 511.9 %reduce-scatter.23.cloned.1.call-start = ((), (), s32[]{:S(2)}) async-start(), calls=%async_computation.19 | async-start | bytes 3932160 | tf_op jit(solution)/shard_map/reduce_scatter | solution.py:326
  368.8 151.6 %copy-start.68 = (f32[768]{0:T(1024)}, f32[768]{0:T(1024)S(1)}, u32[]{:S(2)}) copy-start(f32[768]{0:T(1024)S(1)} %mul.1173) | copy-start | bytes 9220
  760.6 100.0 %reduce-scatter.21.cloned.1.call-start = ((), (), s32[]{:S(2)}) async-start(), calls=%async_computation.17 | async-start | bytes 7864320 | tf_op jit(solution)/shard_map/reduce_scatter | solution.py:136
  769.2 91.4 %copy-start.111 = (f32[256]{0:T(256)S(1)}, f32[256]{0:T(256)}, u32[]{:S(2)}) copy-start(f32[256]{0:T(256)} %get-tuple-element.749) | copy-start | bytes 3076
  769.2 125.1 %all-gather.27.cloned.1.call-start = ((), (), s32[]{:S(2)}) async-start(), calls=%async_computation.20 | async-start | bytes 3932160 | tf_op jit(solution)/shard_map/all_gather | solution.py:202
  865.7 338.3 %reduce-scatter.45.cloned.1.call-start = ((), (), s32[]{:S(2)}) async-start(), calls=%async_computation.37 | async-start | bytes 442368
  867.3 376.7 %reduce-scatter.43.cloned.1.call-start = ((), (), s32[]{:S(2)}) async-start(), calls=%async_computation.36 | async-start | bytes 442368
  920.3 183.1 %copy-start.46 = (f32[1024,12]{0,1:T(8,128)S(1)}, f32[1024,12]{0,1:T(8,128)}, u32[]{:S(2)}) copy-start(f32[1024,12]{0,1:T(8,128)} %copy-done.45) | copy-start | bytes 147460
  920.3 183.1 %copy-start.108 = (f32[12]{0:T(128)S(1)}, f32[12]{0:T(128)}, u32[]{:S(2)}) copy-start(f32[12]{0:T(128)} %copy-done.107) | copy-start | bytes 148
  920.3 183.3 %copy-start.3 = (bf16[1024,1536]{1,0:T(8,128)(2,1)S(1)}, bf16[1024,1536]{1,0:T(8,128)(2,1)}, u32[]{:S(2)}) copy-start(bf16[1024,1536]{1,0:T(8,128)(2,1)} %all-gather.21.cloned.1.call-done) | copy-start | bytes 9437188
  1105.1 164.7 %reduce-scatter.37.cloned.1.call-start = ((), (), s32[]{:S(2)}) async-start(), calls=%async_computation.27 | async-start | bytes 1622016 | tf_op jit(solution)/shard_map/reduce_scatter | solution.py:360
  1112.2 259.6 %reduce-scatter.35.cloned.1.call-start = ((), (), s32[]{:S(2)}) async-start(), calls=%async_computation.26 | async-start | bytes 1622016 | tf_op jit(solution)/shard_map/reduce_scatter | solution.py:360
  1128.9 314.6 %reduce-scatter.41.cloned.1.call-start = ((), (), s32[]{:S(2)}) async-start(), calls=%async_computation.29 | async-start | bytes 2654208 | tf_op jit(solution)/shard_map/reduce_scatter | solution.py:356
  1136.2 379.3 %reduce-scatter.39.cloned.1.call-start = ((), (), s32[]{:S(2)}) async-start(), calls=%async_computation.28 | async-start | bytes 2654208 | tf_op jit(solution)/shard_map/reduce_scatter | solution.py:356
  1143.4 444.0 %reduce-scatter.33.cloned.1.call-start = ((), (), s32[]{:S(2)}) async-start(), calls=%async_computation.25 | async-start | bytes 2654208 | tf_op jit(solution)/shard_map/reduce_scatter | solution.py:350
  1149.9 509.4 %reduce-scatter.31.cloned.1.call-start = ((), (), s32[]{:S(2)}) async-start(), calls=%async_computation.24 | async-start | bytes 2654208 | tf_op jit(solution)/shard_map/reduce_scatter | solution.py:350
  1177.9 553.2 %reduce-scatter.29.cloned.1.call-start = ((), (), s32[]{:S(2)}) async-start(), calls=%async_computation.23 | async-start | bytes 2654208 | tf_op jit(solution)/shard_map/reduce_scatter | solution.py:347
  1184.5 618.6 %reduce-scatter.27.cloned.1.call-start = ((), (), s32[]{:S(2)}) async-start(), calls=%async_computation.22 | async-start | bytes 2654208 | tf_op jit(solution)/shard_map/reduce_scatter | solution.py:347
  1190.0 652.7 %reduce-scatter.25.cloned.1.call-start = ((), (), s32[]{:S(2)}) async-start(), calls=%async_computation.21 | async-start | bytes 3932160 | tf_op jit(solution)/shard_map/reduce_scatter | solution.py:326
  1203.1 639.6 %copy-start.10 = (bf16[256,1536]{1,0:T(8,128)(2,1)S(1)}, bf16[256,1536]{1,0:T(8,128)(2,1)}, u32[]{:S(2)}) copy-start(bf16[256,1536]{1,0:T(8,128)(2,1)} %param.23) | copy-start | bytes 2359300
  1203.1 639.6 %copy-start.55 = (f32[1536]{0:T(1024)S(1)}, f32[1536]{0:T(1024)}, u32[]{:S(2)}) copy-start(f32[1536]{0:T(1024)} %copy-done.54) | copy-start | bytes 18436
  1203.1 639.6 %copy-start.88 = (f32[256]{0:T(256)S(1)}, f32[256]{0:T(256)}, u32[]{:S(2)}) copy-start(f32[256]{0:T(256)} %copy-done.87) | copy-start | bytes 3076
  1515.5 368.7 %copy-start.24 = (f32[256,1536]{1,0:T(8,128)S(1)}, f32[256,1536]{1,0:T(8,128)}, u32[]{:S(2)}) copy-start(f32[256,1536]{1,0:T(8,128)} %get-tuple-element.670) | copy-start | bytes 4718596
  1515.5 368.7 %copy-start.110 = (f32[256]{0:T(256)S(1)}, f32[256]{0:T(256)}, u32[]{:S(2)}) copy-start(f32[256]{0:T(256)} %get-tuple-element.747) | copy-start | bytes 3076
  (120 other events, 1523.2 us)
Sparse Core Ops, SparseCore 0:
  12.6 35.9 all-gather.20
  51.3 57.7 all-gather.28
  111.3 51.0 all-gather.30
  165.0 50.4 all-gather.32
  223.7 57.0 reduce-scatter.18
  284.8 28.5 all-gather.22
  315.8 52.7 all-gather.34
  371.0 52.2 all-gather.36
  425.7 50.5 all-gather.38
  478.4 27.0 all-gather.24
  760.7 39.0 reduce-scatter.22
  802.2 58.3 reduce-scatter.20
  865.8 28.5 all-gather.26
  897.8 61.3 reduce-scatter.44
  1105.3 62.4 reduce-scatter.42
  1173.7 96.0 reduce-scatter.36
  1275.8 95.9 reduce-scatter.34
  1375.5 67.8 reduce-scatter.40
  1447.4 68.0 reduce-scatter.38
  1519.3 68.0 reduce-scatter.32
  1591.3 67.9 reduce-scatter.30
  1663.1 67.9 reduce-scatter.28
  1735.1 68.0 reduce-scatter.26
  1805.7 36.9 reduce-scatter.24
where the time goes:
time: 1900 us; the launch traced here: 1890 us
  waiting for transfers between devices  815 us (43%)
  matrix products  519 us (27%)
  blocking collectives  263 us (14%)
  other arithmetic  203 us (11%)
  local copies, waits for them, and re-layouts  74.2 us (4%)
    dot_general x24, matrix products, mix_back(): jnp.einsum('sqp,skp->sqk', grad_one, inner_one, preferred_element_type=jn...  145 us
    reduce_scatter x2, waiting for transfers between devices, on_device(): lax.psum_scatter(grad_weight_out.astype(jnp.bfloat16), 'dp', scatter_dime...  142 us
    reduce_scatter x2, waiting for transfers between devices, on_device(): lax.psum_scatter(grad_weight_gate.astype(jnp.bfloat16), 'dp', scatter_dim...  142 us
    reduce_scatter x2, waiting for transfers between devices, on_device(): lax.psum_scatter(grad_weight_inner.astype(jnp.bfloat16), 'dp', scatter_di...  141 us
    reduce_scatter x2, waiting for transfers between devices, on_device(): lax.psum_scatter(grad_weight_shared, ('dp', 'tensor'), scatter_dimension=...  126 us
    reduce_scatter x2, waiting for transfers between devices, on_device(): lax.psum_scatter(project(jnp.int32(0), lax.axis_size('tensor') * local_ro...  116 us
    dot_general x24, matrix products, mix_one(): jnp.einsum('sqk,skp->sqp', weights, inner_one, preferred_element_type=jnp...  105 us
    dot_general x24, matrix products, mix_back(): jnp.einsum('sqk,sqp->skp', weights, grad_one, preferred_element_type=jnp....  104 us
  transfers between devices with their start and end apart: 24, of which 17 were waited for; matrix products, arithmetic and copies ran while one was open for 27% of the time, Pallas kernels for 0%

commit v1 on v0

v1 whole, which is shorter than its diff:
```python
import functools

import jax
import jax.numpy as jnp
from jax import lax
from jax.experimental import pallas as pl
from jax.experimental.pallas import tpu as pltpu
from jax.sharding import PartitionSpec as P

P_SIZE = 64
N = 128
LEN = 1024
CHUNK = 256
LANES = 128
TAPS = 4

highest = lax.Precision.HIGHEST
epsilon = 1e-05
F32 = jnp.float32
BF16 = jnp.bfloat16


def mm(left, right):
    return jnp.dot(left, right, preferred_element_type=F32)


def mm_nt(left, right):
    return lax.dot_general(left, right, (((1,), (1,)), ((), ())), preferred_element_type=F32)


def sigmoid(values):
    return 1.0 / (1.0 + jnp.exp(-values))


def softplus(values):
    return jnp.maximum(values, 0.0) + jnp.log1p(jnp.exp(-jnp.abs(values)))


def iota2(shape, dim):
    return lax.broadcasted_iota(jnp.int32, shape, dim)


def pair_of(columns, head):
    shape = (columns.shape[0], LANES)
    first = jnp.broadcast_to(columns[:, head : head + 1], shape)
    second = jnp.broadcast_to(columns[:, head + 1 : head + 2], shape)
    return jnp.where(iota2(shape, 1) < P_SIZE, first, second)


def head_sums(values, spread):
    high = values.astype(BF16)
    low = (values - high.astype(F32)).astype(BF16)
    return mm(high, spread) + mm(low, spread)


def decays(step_pre, rate, aux):
    step = softplus(step_pre)
    order = (iota2((CHUNK, CHUNK), 0) >= iota2((CHUNK, CHUNK), 1)).astype(F32)
    cum = jnp.dot(order, step * rate, precision=highest, preferred_element_type=F32)
    last = cum[CHUNK - 1 : CHUNK, :]
    decay_in = jnp.exp(cum) * aux[:, 4:5]
    decay_out = jnp.exp(last - cum) * aux[:, 5:6]
    decay_pass = jnp.exp(last) * aux[0:1, 6:7]
    return step, cum, decay_in, decay_out, decay_pass


def forward_kernel(
    rows_ref,
    wz_ref,
    wx_ref,
    wbc_ref,
    wdt_ref,
    wout_ref,
    convx_ref,
    convbc_ref,
    heads_ref,
    wide_ref,
    aux_ref,
    segrow_ref,
    part_ref,
    sq_ref,
    gate_ref,
    iraw_ref,
    iconv_ref,
    sraw_ref,
    sconv_ref,
    step_ref,
    mixed_ref,
    sin_ref,
    ext_x,
    ext_bc,
    state,
    gg_ref,
):
    inner = wx_ref.shape[1]

    @pl.when(pl.program_id(0) == 0)
    def _():
        state[...] = jnp.zeros_like(state)
        ext_x[0:8, :] = jnp.zeros((8, inner), F32)
        ext_bc[0:8, :] = jnp.zeros((8, 2 * N), F32)

    rows = rows_ref[...]
    aux = aux_ref[...]
    rate = heads_ref[1:2, :]
    shared = mm(rows, wbc_ref[...])
    sraw_ref[...] = shared
    ext_bc[8 : 8 + CHUNK, :] = shared
    shared_conv = convbc_ref[TAPS - 1 : TAPS, :] * shared
    for j in range(1, TAPS):
        shared_conv = shared_conv + convbc_ref[TAPS - 1 - j : TAPS - j, :] * (
            ext_bc[8 - j : 8 - j + CHUNK, :] * aux[:, j : j + 1]
        )
    sconv_ref[...] = shared_conv
    ext_bc[0:8, :] = ext_bc[CHUNK : CHUNK + 8, :]
    shared_act = shared_conv * sigmoid(shared_conv)
    keys = shared_act[:, :N].astype(BF16)
    keys_t = jnp.transpose(shared_act[:, :N]).astype(BF16)
    query = shared_act[:, N:].astype(BF16)
    visible = (aux[:, 15:16] == segrow_ref[0:1, :]) & (
        iota2((CHUNK, CHUNK), 0) >= iota2((CHUNK, CHUNK), 1)
    )
    coupling = jnp.where(visible, mm_nt(query, keys), 0.0)
    step_raw = mm(rows, wdt_ref[...])
    step_ref[...] = step_raw
    step, cum, decay_in, decay_out, decay_pass = decays(
        step_raw + heads_ref[0:1, :], rate, aux
    )
    cum_t = jnp.transpose(cum)
    ext_x[8 : 8 + CHUNK, :] = mm(rows, wx_ref[...])
    gate_ref[...] = mm(rows, wz_ref[...])
    squares = jnp.zeros((CHUNK, LANES), F32)
    half = iota2((CHUNK, LANES), 1) < P_SIZE
    for pair in range(inner // LANES):
        cols = slice(pair * LANES, (pair + 1) * LANES)
        head = 2 * pair
        raw = ext_x[8 : 8 + CHUNK, cols]
        iraw_ref[:, cols] = raw
        conv = convx_ref[TAPS - 1 : TAPS, cols] * raw
        for j in range(1, TAPS):
            conv = conv + convx_ref[TAPS - 1 - j : TAPS - j, cols] * (
                ext_x[8 - j : 8 - j + CHUNK, cols] * aux[:, j : j + 1]
            )
        iconv_ref[:, cols] = conv
        ext_x[0:8, cols] = ext_x[CHUNK : CHUNK + 8, cols]
        act = conv * sigmoid(conv)
        scaled = (act * pair_of(step, head)).astype(BF16)
        parts = []
        for one in (head, head + 1):
            gap = cum[:, one : one + 1] - cum_t[one : one + 1, :]
            weights = (coupling * jnp.exp(jnp.minimum(gap, 0.0))).astype(BF16)
            parts.append(mm(weights, scaled))
        before = state[:, cols]
        sin_ref[0, :, cols] = before
        mixed = jnp.where(half, parts[0], parts[1])
        mixed = mixed + pair_of(decay_in, head) * mm(query, before.astype(BF16))
        mixed_ref[:, cols] = mixed
        leaving = (scaled.astype(F32) * pair_of(decay_out, head)).astype(BF16)
        state[:, cols] = pair_of(decay_pass, head) * before + mm(keys_t, leaving)
        gate = gate_ref[:, cols]
        gated = (mixed + wide_ref[0:1, cols] * act) * (gate * sigmoid(gate))
        squares = squares + gated * gated
        gg_ref[:, cols] = (gated * wide_ref[1:2, cols]).astype(BF16)
    total = jnp.sum(squares, axis=1, keepdims=True)
    sq_ref[...] = jnp.transpose(jnp.broadcast_to(total, (CHUNK, LANES)))[0:8, :]
    part_ref[...] = mm_nt(gg_ref[...], wout_ref[...]).astype(BF16)


def backward_kernel(
    top_ref,
    sc_ref,
    gate_ref,
    iraw_ref,
    iconv_ref,
    sraw_ref,
    sconv_ref,
    step_ref,
    mixed_ref,
    sin_ref,
    sout_ref,
    wz_ref,
    wx_ref,
    wbc_ref,
    wdt_ref,
    wout_ref,
    convx_ref,
    convbc_ref,
    heads_ref,
    wide_ref,
    spread_ref,
    aux_ref,
    segrow_ref,
    part_ref,
    ggate_ref,
    ginner_ref,
    gstep_ref,
    gshared_ref,
    outlow_ref,
    small_ref,
    smallbc_ref,
    gext_x,
    gext_bc,
    dstate,
    gno_ref,
    balance,
    direct,
    edge,
    dcoup,
):
    inner = wx_ref.shape[1]

    @pl.when(pl.program_id(0) == 0)
    def _():
        dstate[...] = jnp.zeros_like(dstate)
        gext_x[CHUNK : CHUNK + 8, :] = jnp.zeros((8, inner), F32)
        gext_bc[CHUNK : CHUNK + 8, :] = jnp.zeros((8, 2 * N), F32)
        small_ref[...] = jnp.zeros_like(small_ref)
        smallbc_ref[...] = jnp.zeros_like(smallbc_ref)
        edge[...] = jnp.zeros_like(edge)

    aux = aux_ref[...]
    rate = heads_ref[1:2, :]
    gno_ref[...] = mm(top_ref[...], wout_ref[...])
    per_row = jnp.transpose(sc_ref[...])
    scale = per_row[:, 0:1]
    coef = per_row[:, 1:2]
    step_pre = step_ref[...] + heads_ref[0:1, :]
    step, cum, decay_in, decay_out, decay_pass = decays(step_pre, rate, aux)
    cum_t = jnp.transpose(cum)
    shared_conv = sconv_ref[...]
    shared_sig = sigmoid(shared_conv)
    shared_act = shared_conv * shared_sig
    keys = shared_act[:, :N].astype(BF16)
    query = shared_act[:, N:].astype(BF16)
    query_t = jnp.transpose(shared_act[:, N:]).astype(BF16)
    visible = (aux[:, 15:16] == segrow_ref[0:1, :]) & (
        iota2((CHUNK, CHUNK), 0) <= iota2((CHUNK, CHUNK), 1)
    )
    coupling = jnp.where(visible, mm_nt(keys, query), 0.0)
    half = iota2((CHUNK, LANES), 1) < P_SIZE
    dcoup[...] = jnp.zeros_like(dcoup)
    dkeys = jnp.zeros((CHUNK, N), F32)
    dquery = jnp.zeros((CHUNK, N), F32)
    for pair in range(inner // LANES):
        cols = slice(pair * LANES, (pair + 1) * LANES)
        head = 2 * pair
        skip = wide_ref[0:1, cols]
        gain = wide_ref[1:2, cols]
        conv = iconv_ref[:, cols]
        conv_sig = sigmoid(conv)
        act = conv * conv_sig
        step_pair = pair_of(step, head)
        scaled = (act * step_pair).astype(BF16)
        gate = gate_ref[:, cols]
        gate_sig = sigmoid(gate)
        gate_act = gate * gate_sig
        mixed = mixed_ref[:, cols]
        full = mixed + skip * act
        gated = full * gate_act
        gno = gno_ref[:, cols]
        gated_scaled = gated * scale
        small_ref[4:5, cols] += jnp.sum(gno * gated_scaled, axis=0, keepdims=True)
        outlow_ref[:, cols] = (gated_scaled * gain).astype(BF16)
        ggated = scale * (gno * gain) - gated * coef
        gout_low = (ggated * gate_act).astype(BF16)
        ggate_ref[:, cols] = (
            ggated * full * (gate_sig * (1.0 + gate * (1.0 - gate_sig)))
        ).astype(BF16)
        gout = gout_low.astype(F32)
        small_ref[5:6, cols] += jnp.sum(gout * act, axis=0, keepdims=True)
        zero = jnp.zeros_like(gout)
        parts = []
        for one, own in (
            (head, jnp.where(half, gout, zero).astype(BF16)),
            (head + 1, jnp.where(half, zero, gout).astype(BF16)),
        ):
            gap = cum_t[one : one + 1, :] - cum[:, one : one + 1]
            decay = jnp.exp(jnp.minimum(gap, 0.0))
            weights = (coupling * decay).astype(BF16)
            parts.append(mm(weights, gout_low))
            dcoup[...] += mm_nt(scaled, own) * decay
        after = dstate[:, cols]
        after_low = after.astype(BF16)
        out_pair = pair_of(decay_out, head)
        gscaled = jnp.where(half, parts[0], parts[1]) + out_pair * mm(keys, after_low)
        scaled_wide = scaled.astype(F32)
        dkeys = dkeys + mm_nt((scaled_wide * out_pair).astype(BF16), after_low)
        entering = (gout * pair_of(decay_in, head)).astype(BF16)
        dquery = dquery + mm_nt(entering, sin_ref[0, :, cols].astype(BF16))
        edge[0:1, cols] = jnp.sum(sout_ref[0, :, cols] * after, axis=0, keepdims=True)
        dstate[:, cols] = pair_of(decay_pass, head) * after + mm(query_t, entering)
        balance[:, cols] = gout * mixed - scaled_wide * gscaled
        direct[:, cols] = act * gscaled
        gact = step_pair * gscaled + skip * gout
        gext_x[0:CHUNK, cols] = gact * (conv_sig * (1.0 + conv * (1.0 - conv_sig)))
        raw = iraw_ref[:, cols]
        gconv = gext_x[0:CHUNK, cols]
        graw = convx_ref[TAPS - 1 : TAPS, cols] * gconv
        small_ref[TAPS - 1 : TAPS, cols] += jnp.sum(raw * gconv, axis=0, keepdims=True)
        for j in range(1, TAPS):
            moved = gext_x[j : j + CHUNK, cols] * aux[:, 8 + j : 9 + j]
            graw = graw + convx_ref[TAPS - 1 - j : TAPS - j, cols] * moved
            small_ref[TAPS - 1 - j : TAPS - j, cols] += jnp.sum(
                raw * moved, axis=0, keepdims=True
            )
        ginner_ref[:, cols] = graw.astype(BF16)
        gext_x[CHUNK : CHUNK + 8, cols] = gext_x[0:8, cols]
    spread = spread_ref[...]
    order = (iota2((CHUNK, CHUNK), 0) <= iota2((CHUNK, CHUNK), 1)).astype(F32)
    running = jnp.dot(
        order, head_sums(balance[...], spread), precision=highest, preferred_element_type=F32
    )
    running = running + head_sums(edge[...], spread)[0:1, :]
    gstep = (head_sums(direct[...], spread) + running * rate) * sigmoid(step_pre)
    small_ref[6:7, 0:LANES] += rate * jnp.sum(running * step, axis=0, keepdims=True)
    small_ref[7:8, 0:LANES] += jnp.sum(gstep, axis=0, keepdims=True)
    gstep_ref[...] = gstep.astype(BF16)
    dcoupling = jnp.where(visible, dcoup[...], 0.0)
    dkeys = dkeys + mm(dcoupling.astype(BF16), query)
    dquery = dquery + mm(jnp.transpose(dcoupling).astype(BF16), keys)
    slope = shared_sig * (1.0 + shared_conv * (1.0 - shared_sig))
    gext_bc[0:CHUNK, 0:N] = dkeys * slope[:, :N]
    gext_bc[0:CHUNK, N : 2 * N] = dquery * slope[:, N:]
    raw = sraw_ref[...]
    gconv = gext_bc[0:CHUNK, :]
    graw = convbc_ref[TAPS - 1 : TAPS, :] * gconv
    smallbc_ref[TAPS - 1 : TAPS, :] += jnp.sum(raw * gconv, axis=0, keepdims=True)
    for j in range(1, TAPS):
        moved = gext_bc[j : j + CHUNK, :] * aux[:, 8 + j : 9 + j]
        graw = graw + convbc_ref[TAPS - 1 - j : TAPS - j, :] * moved
        smallbc_ref[TAPS - 1 - j : TAPS - j, :] += jnp.sum(raw * moved, axis=0, keepdims=True)
    gshared_ref[...] = graw.astype(BF16)
    gext_bc[CHUNK : CHUNK + 8, :] = gext_bc[0:8, :]
    total = mm_nt(ggate_ref[...], wz_ref[...]) + mm_nt(ginner_ref[...], wx_ref[...])
    total = total + mm_nt(gstep_ref[...], wdt_ref[...])
    part_ref[...] = (total + mm_nt(gshared_ref[...], wbc_ref[...])).astype(BF16)


def whole_spec(shape):
    zeros = (0,) * len(shape)
    return pl.BlockSpec(shape, lambda i: zeros, pipeline_mode=pl.Buffered(1))


VMEM_LIMIT = 60 * 1024 * 1024


def forward_layer(rows_all, weights, layer_args, aux, segrow):
    length, width = rows_all.shape
    chunks = length // CHUNK
    inner = weights[1].shape[1]
    by_rows = lambda cols: pl.BlockSpec((CHUNK, cols), lambda i: (i, 0))
    by_lanes = pl.BlockSpec((8, CHUNK), lambda i: (0, i))
    shape = jax.ShapeDtypeStruct
    return pl.pallas_call(
        forward_kernel,
        grid=(chunks,),
        in_specs=[by_rows(width)]
        + [whole_spec(w.shape) for w in weights]
        + [whole_spec(w.shape) for w in layer_args]
        + [by_rows(LANES), by_lanes],
        out_specs=[
            by_rows(width),
            by_lanes,
            by_rows(inner),
            by_rows(inner),
            by_rows(inner),
            by_rows(2 * N),
            by_rows(2 * N),
            by_rows(LANES),
            by_rows(inner),
            pl.BlockSpec((1, N, inner), lambda i: (i, 0, 0)),
        ],
        out_shape=[
            shape((length, width), BF16),
            shape((8, length), F32),
            shape((length, inner), F32),
            shape((length, inner), F32),
            shape((length, inner), F32),
            shape((length, 2 * N), F32),
            shape((length, 2 * N), F32),
            shape((length, LANES), F32),
            shape((length, inner), F32),
            shape((chunks, N, inner), F32),
        ],
        scratch_shapes=[
            pltpu.VMEM((CHUNK + 8, inner), F32),
            pltpu.VMEM((CHUNK + 8, 2 * N), F32),
            pltpu.VMEM((N, inner), F32),
            pltpu.VMEM((CHUNK, inner), BF16),
        ],
        compiler_params=pltpu.CompilerParams(
            dimension_semantics=("arbitrary",), vmem_limit_bytes=VMEM_LIMIT
        ),
        cost_estimate=pl.CostEstimate(
            flops=length * width * inner * 7, bytes_accessed=40_000_000, transcendentals=8_000_000
        ),
    )(rows_all, *weights, *layer_args, aux, segrow)


def backward_layer(top_all, per_row, saved, weights, layer_args, spread, aux, segrow):
    length, width = top_all.shape
    chunks = length // CHUNK
    inner = weights[1].shape[1]
    last = chunks - 1
    by_rows = lambda cols: pl.BlockSpec((CHUNK, cols), lambda i: (last - i, 0))
    by_lanes = pl.BlockSpec((8, CHUNK), lambda i: (0, last - i))
    shape = jax.ShapeDtypeStruct
    gate, iraw, iconv, sraw, sconv, step, mixed, sin = saved
    return pl.pallas_call(
        backward_kernel,
        grid=(chunks,),
        in_specs=[
            by_rows(width),
            by_lanes,
            by_rows(inner),
            by_rows(inner),
            by_rows(inner),
            by_rows(2 * N),
            by_rows(2 * N),
            by_rows(LANES),
            by_rows(inner),
            pl.BlockSpec((1, N, inner), lambda i: (last - i, 0, 0)),
            pl.BlockSpec((1, N, inner), lambda i: (jnp.minimum(chunks - i, last), 0, 0)),
        ]
        + [whole_spec(w.shape) for w in weights]
        + [whole_spec(w.shape) for w in layer_args]
        + [whole_spec(spread.shape), by_rows(LANES), by_lanes],
        out_specs=[
            by_rows(width),
            by_rows(inner),
            by_rows(inner),
            by_rows(LANES),
            by_rows(2 * N),
            by_rows(inner),
            pl.BlockSpec((8, inner), lambda i: (0, 0)),
            pl.BlockSpec((8, 2 * N), lambda i: (0, 0)),
        ],
        out_shape=[
            shape((length, width), BF16),
            shape((length, inner), BF16),
            shape((length, inner), BF16),
            shape((length, LANES), BF16),
            shape((length, 2 * N), BF16),
            shape((length, inner), BF16),
            shape((8, inner), F32),
            shape((8, 2 * N), F32),
        ],
        scratch_shapes=[
            pltpu.VMEM((CHUNK + 8, inner), F32),
            pltpu.VMEM((CHUNK + 8, 2 * N), F32),
            pltpu.VMEM((N, inner), F32),
            pltpu.VMEM((CHUNK, inner), F32),
            pltpu.VMEM((CHUNK, inner), F32),
            pltpu.VMEM((CHUNK, inner), F32),
            pltpu.VMEM((8, inner), F32),
            pltpu.VMEM((CHUNK, CHUNK), F32),
        ],
        compiler_params=pltpu.CompilerParams(
            dimension_semantics=("arbitrary",), vmem_limit_bytes=VMEM_LIMIT
        ),
        cost_estimate=pl.CostEstimate(
            flops=length * width * inner * 7, bytes_accessed=40_000_000, transcendentals=8_000_000
        ),
    )(
        top_all,
        per_row,
        gate,
        iraw,
        iconv,
        sraw,
        sconv,
        step,
        mixed,
        sin,
        sin,
        *weights,
        *layer_args,
        spread,
        aux,
        segrow,
    )


def row_masks(segment_ids):
    length = segment_ids.shape[0]
    seg = segment_ids.astype(F32)

    def shifted(j):
        return jnp.concatenate([jnp.full((j,), -1.0, F32), seg[: length - j]])

    def ahead(j):
        return jnp.concatenate([seg[j:], jnp.full((j,), -1.0, F32)])

    ends = seg[CHUNK - 1 :: CHUNK]
    own_end = jnp.repeat(ends, CHUNK)
    old_end = jnp.repeat(jnp.concatenate([jnp.full((1,), -1.0, F32), ends[:-1]]), CHUNK)
    lanes = [jnp.zeros_like(seg)] * 16
    for j in range(1, TAPS):
        lanes[j] = (shifted(j) == seg).astype(F32)
        lanes[8 + j] = (ahead(j) == seg).astype(F32)
    lanes[4] = (old_end == seg).astype(F32)
    lanes[5] = (own_end == seg).astype(F32)
    lanes[6] = (own_end == old_end).astype(F32)
    lanes[15] = seg
    aux = jnp.pad(jnp.stack(lanes, axis=1), ((0, 0), (0, LANES - 16)))
    return aux, jnp.broadcast_to(seg[None, :], (8, length))


def layer_parameters(layer, conv_x, conv_bc, a_log, dt_bias, d_skip, gated_gain):
    heads = a_log.shape[1]
    pad = ((0, 0), (0, LANES - heads))
    head_rows = jnp.pad(jnp.stack([dt_bias[layer], -jnp.exp(a_log[layer])]), pad)
    wide = jnp.stack([jnp.repeat(d_skip[layer], P_SIZE), gated_gain[layer]])
    return (conv_x[layer], conv_bc[layer], head_rows, wide)


def head_spread(inner):
    return (
        jnp.arange(inner)[:, None] // P_SIZE == jnp.arange(LANES)[None, :]
    ).astype(BF16)


def on_device(
    resid,
    segment_ids,
    cotangent,
    w_z,
    w_x,
    w_bc,
    w_dt,
    w_out,
    norm_gain,
    conv_x,
    conv_bc,
    a_log,
    dt_bias,
    d_skip,
    gated_gain,
):
    tensor_size = lax.axis_size("tensor")
    heads = a_log.shape[1]
    inner = heads * P_SIZE
    inner_all = inner * tensor_size
    layers = a_log.shape[0]
    aux, segrow = row_masks(segment_ids)
    spread = head_spread(inner)
    args = [
        layer_parameters(layer, conv_x, conv_bc, a_log, dt_bias, d_skip, gated_gain)
        for layer in range(layers)
    ]
    weights = []
    for layer in range(layers):
        weights.append(
            (
                lax.all_gather(w_z[layer], "dp", axis=0, tiled=True),
                lax.all_gather(w_x[layer], "dp", axis=0, tiled=True),
                lax.all_gather(w_bc[layer], ("dp", "tensor"), axis=0, tiled=True),
                lax.all_gather(
                    jnp.pad(w_dt[layer], ((0, 0), (0, LANES - heads))), "dp", axis=0, tiled=True
                ),
                lax.all_gather(jnp.transpose(w_out[layer]), "dp", axis=0, tiled=True),
            )
        )
    state = resid.astype(F32)
    states, kept, scales, branches, rows_list = [], [], [], [], []
    for layer in range(layers):
        scale_in = lax.rsqrt(jnp.mean(state * state, axis=1, keepdims=True) + epsilon)
        normed = (state * scale_in * norm_gain[layer]).astype(BF16)
        rows_all = lax.all_gather(normed, "tensor", axis=0, tiled=True)
        part, sq, *saved = forward_layer(rows_all, weights[layer], args[layer], aux, segrow)
        squares = lax.psum_scatter(sq[0], "tensor", scatter_dimension=0, tiled=True)
        scale_out = lax.rsqrt(squares / inner_all + epsilon)
        raw = lax.psum_scatter(part, "tensor", scatter_dimension=0, tiled=True).astype(F32)
        states.append((state, scale_in))
        kept.append(saved)
        rows_list.append(rows_all)
        scales.append(scale_out)
        branches.append(raw)
        state = state + raw * scale_out[:, None]
    grad_state = cotangent
    grads = [None] * layers
    for layer in reversed(range(layers)):
        low = grad_state.astype(BF16)
        cross = jnp.sum(low.astype(F32) * branches[layer], axis=1)
        coef = scales[layer] ** 3 * cross / inner_all
        per_row = jnp.pad(jnp.stack([scales[layer], coef]), ((0, 6), (0, 0)))
        per_row = lax.all_gather(per_row, "tensor", axis=1, tiled=True)
        top_all = lax.all_gather(low, "tensor", axis=0, tiled=True)
        part, ggate, ginner, gstep, gshared, outlow, small, small_bc = backward_layer(
            top_all, per_row, kept[layer], weights[layer], args[layer], spread, aux, segrow
        )

        def contract(left, right):
            return lax.dot_general(
                left, right, (((0,), (0,)), ((), ())), preferred_element_type=F32
            ).astype(BF16)

        def scatter(values, axes="dp"):
            return lax.psum_scatter(values, axes, scatter_dimension=0, tiled=True).astype(F32)

        rows_all = rows_list[layer]
        gz = scatter(contract(rows_all, ggate))
        gx = scatter(contract(rows_all, ginner))
        gdt = scatter(contract(rows_all, gstep))[:, :heads]
        gbc = scatter(contract(rows_all, gshared), ("dp", "tensor"))
        gout = jnp.transpose(scatter(contract(top_all, outlow)))
        grad_normed = lax.psum_scatter(
            part, "tensor", scatter_dimension=0, tiled=True
        ).astype(F32)
        state_in, scale_in = states[layer]
        gained = grad_normed * norm_gain[layer]
        gnorm = jnp.sum(grad_normed * state_in * scale_in, axis=0)
        grad_state = (
            grad_state
            + scale_in * gained
            - state_in * scale_in**3 * jnp.mean(gained * state_in, axis=1, keepdims=True)
        )
        grads[layer] = (gz, gx, gbc, gdt, gout, gnorm, small, small_bc)
    stacked = [jnp.stack(values) for values in zip(*grads)]
    small = lax.psum(stacked[6], "dp")
    gnorm, small_bc = lax.psum((stacked[5], stacked[7]), ("dp", "tensor"))
    return (
        state,
        grad_state,
        stacked[0],
        stacked[1],
        stacked[2],
        stacked[3],
        stacked[4],
        gnorm,
        small[:, :TAPS],
        small_bc[:, :TAPS],
        small[:, 6, :heads],
        small[:, 7, :heads],
        jnp.sum(small[:, 5].reshape(layers, heads, P_SIZE), axis=2),
        small[:, 4],
    )


def solution(mesh):
    rows = P(("dp", "tensor"), None)
    matrix = P(None, "dp", "tensor")
    shared = P(None, ("dp", "tensor"), None)
    wide = P(None, None, "tensor")
    head = P(None, "tensor")
    out = P(None, "tensor", "dp")
    return jax.shard_map(
        on_device,
        mesh=mesh,
        in_specs=(
            rows, P("dp"), rows, matrix, matrix, shared, matrix, out, P(), wide, P(), head, head, head, head,
        ),
        out_specs=(
            rows, rows, matrix, matrix, shared, matrix, out, P(), wide, P(), head, head, head, head,
        ),
        check_vma=False,
    )
```

time: 1900 us -> 1530 us (0.81)
  matrix products: 519 us -> 50.3 us
  waiting for transfers between devices: 815 us -> 1010 us
  other arithmetic: 203 us -> 27.7 us
  Pallas kernels: 0 us -> 128 us
  local copies, waits for them, and re-layouts: 74.2 us -> 21 us
    dot_general x108 -> x10, matrix products: 519 us -> 50.3 us  [contract(): lax.dot_general(left, right, (((0,), (0,)), ((), ())), preferred_element_...]
    pallas_call x0 -> x4, Pallas kernels: none -> 128 us  [the longest x2 75.7 us: backward_layer(): pl.pallas_call(backward_kernel, grid=(chunks,), in_specs=[by_rows(width),...]
    reduce_sum x34 -> x5, other arithmetic: 108 us -> 9.38 us  [the longest x2 5.07 us: on_device(): cross = jnp.sum(low.astype(F32) * branches[layer], axis=1)]
    all_gather x4, waiting for transfers between devices: 74.2 us -> 141 us  [the longest x2 106 us: on_device(): lax.all_gather(jnp.transpose(w_out[layer]), 'dp', axis=0, tiled=True)]
    all_gather x2, waiting for transfers between devices: 0.02 us -> 58.4 us  [on_device(): rows_all = lax.all_gather(normed, 'tensor', axis=0, tiled=True)]
    all_gather x2, waiting for transfers between devices: 3.26 us -> 48.5 us  [on_device(): lax.all_gather(w_x[layer], 'dp', axis=0, tiled=True)]
    another operation x25 -> x15, other arithmetic: 48.7 us -> 11.1 us  [the longest x8 8.63 us: on_device(): stacked = [jnp.stack(values) for values in zip(*grads)]]
    reduce_scatter x12 -> x14, waiting for transfers between devices: 736 us -> 764 us  [the longest x10 622 us: scatter(): lax.psum_scatter(values, axes, scatter_dimension=0, tiled=True).astype(F32)]
  transfers between devices with their start and end apart: 24 -> 24, of which waited for: 17 -> 20; matrix products, arithmetic and copies ran while one was open for 27% -> 5% of each run, Pallas kernels for 0% -> 2%
where the time goes in v1:
time: 1530 us; the launch traced here: 1520 us
  waiting for transfers between devices  1010 us (66%)
  blocking collectives  265 us (17%)
  Pallas kernels  128 us (8%)
  matrix products  50.3 us (3%)
  other arithmetic  27.7 us (2%)
  local copies, waits for them, and re-layouts  21 us (1%)
  between operations  16 us (1%)
    reduce_scatter x10, waiting for transfers between devices, scatter(): lax.psum_scatter(values, axes, scatter_dimension=0, tiled=True).astype(F32)  622 us
    reduce_scatter x4, waiting for transfers between devices, on_device(): lax.psum_scatter(part, 'tensor', scatter_dimension=0, tiled=True)  141 us
    all_gather x2, waiting for transfers between devices, on_device(): lax.all_gather(jnp.transpose(w_out[layer]), 'dp', axis=0, tiled=True)  106 us
    all_gather x2, blocking collectives, on_device(): lax.all_gather(w_bc[layer], ('dp', 'tensor'), axis=0, tiled=True)  94.6 us
    pallas_call x2, Pallas kernels, backward_layer(): pl.pallas_call(backward_kernel, grid=(chunks,), in_specs=[by_rows(width),...  75.7 us
    all_gather x2, blocking collectives, on_device(): lax.all_gather(jnp.pad(w_dt[layer], ((0, 0), (0, LANES - heads))), 'dp',...  69.8 us
    all_gather x2, waiting for transfers between devices, on_device(): rows_all = lax.all_gather(normed, 'tensor', axis=0, tiled=True)  58.4 us
    pallas_call x2, Pallas kernels, forward_layer(): pl.pallas_call(forward_kernel, grid=(chunks,), in_specs=[by_rows(width)]...  52.3 us
  transfers between devices with their start and end apart: 24, of which 20 were waited for; matrix products, arithmetic and copies ran while one was open for 5% of the time, Pallas kernels for 2%

profile of v1, /device:TPU:0, one launch (start us, length us, event | category | flops | bytes accessed | tf_op | source)
XLA Modules:
  0.0 1523.6 jit_solution(16125499510007940847)
XLA Ops:
  16.4 36.0 %all_gather.52.wdt_ref = bf16[1536,128]{1,0:T(8,128)(2,1)} all-gather(bf16[192,128]{1,0:T(8,128)(2,1)S(1)} %pad.29), channel_id=1, replica_groups=mesh['dp'=8,'tensor'=4] {'dp'}, dimensions={0}, use_global_device_ids=true | all-gather | bytes 442368 | tf_op jit(solution)/shard_map/all_gather | solution.py:558
  53.6 47.7 %all-gather.2 = bf16[1,1536,256]{2,1,0:T(8,128)(2,1)} all-gather(bf16[1,48,256]{2,1,0:T(8,128)(2,1)S(1)} %get-tuple-element.141), channel_id=4, replica_groups=mesh['dp'=8,'tensor'=4] {'dp','tensor'}, dimensions={1}, use_global_device_ids=true | all-gather | bytes 811008 | tf_op jit(solution)/shard_map/all_gather | solution.py:557
  101.3 21.5 %all-gather.31.cloned.1.call-done = bf16[1,1536,768]{2,1,0:T(8,128)(2,1)} async-done(((bf16[1,192,768]{2,1,0:T(8,128)(2,1)}), bf16[1,1536,768]{2,1,0:T(8,128)(2,1)}) %all-gather.31.cloned.1.call-update) | async-done | bytes 2359312 | tf_op jit(solution)/shard_map/all_gather | solution.py:556
  122.8 53.4 %all-gather.19.cloned.1.call-done.wout_ref = bf16[1536,768]{1,0:T(8,128)(2,1)} async-done(((bf16[192,768]{1,0:T(8,128)(2,1)}), bf16[1536,768]{1,0:T(8,128)(2,1)}) %all-gather.19.cloned.1.call-update) | async-done | bytes 2359312 | tf_op jit(solution)/shard_map/all_gather | solution.py:561
  176.2 29.1 %all-gather.17.cloned.1.call-done.rows_ref = bf16[1024,1536]{1,0:T(8,128)(2,1)} async-done(((bf16[256,1536]{1,0:T(8,128)(2,1)}), bf16[1024,1536]{1,0:T(8,128)(2,1)}) %all-gather.17.cloned.1.call-update) | async-done | bytes 3145744 | tf_op jit(solution)/shard_map/all_gather | solution.py:569
  205.9 26.1 %shard_map.254 = (bf16[1024,1536]{1,0:T(8,128)(2,1)}, f32[8,1024]{1,0:T(8,128)}, f32[1024,768]{1,0:T(8,128)}, f32[1024,768]{1,0:T(8,128)}, f32[1024,768]{1,0:T(8...) custom-call(bf16[1024,1536]{1,0:T(8,128)(2,1)} %all-gather.17.cloned, ...), custom_call_target="tpu_custom_call" | custom-call | flops 8455716864 | bytes 40000000 | tf_op jit(solution)/shard_map/pallas_call | solution.py:354
  236.2 5.9 all-reduce.11
  242.2 28.0 %reduce-scatter.15.cloned.1.call-done = bf16[256,1536]{1,0:T(8,128)(2,1)} async-done(((bf16[1024,1536]{1,0:T(8,128)(2,1)}), bf16[256,1536]{1,0:T(8,128)(2,1)}) %reduce-scatter.15.cloned.1.call-update) | async-done | bytes 786448 | tf_op jit(solution)/shard_map/reduce_scatter | solution.py:573
  274.7 33.8 %all_gather.58.wdt_ref = bf16[1536,128]{1,0:T(8,128)(2,1)} all-gather(bf16[192,128]{1,0:T(8,128)(2,1)S(1)} %pad.32), channel_id=1, replica_groups=mesh['dp'=8,'tensor'=4] {'dp'}, dimensions={0}, use_global_device_ids=true | all-gather | bytes 442368 | tf_op jit(solution)/shard_map/all_gather | solution.py:558
  308.6 46.9 %all-gather.5 = bf16[1,1536,256]{2,1,0:T(8,128)(2,1)} all-gather(bf16[1,48,256]{2,1,0:T(8,128)(2,1)S(1)} %get-tuple-element.140), channel_id=7, replica_groups=mesh['dp'=8,'tensor'=4] {'dp','tensor'}, dimensions={1}, use_global_device_ids=true | all-gather | bytes 811008 | tf_op jit(solution)/shard_map/all_gather | solution.py:557
  355.5 27.0 %all-gather.35.cloned.1.call-done = bf16[1,1536,768]{2,1,0:T(8,128)(2,1)} async-done(((bf16[1,192,768]{2,1,0:T(8,128)(2,1)}), bf16[1,1536,768]{2,1,0:T(8,128)(2,1)}) %all-gather.35.cloned.1.call-update) | async-done | bytes 2359312 | tf_op jit(solution)/shard_map/all_gather | solution.py:556
  382.5 53.1 %all-gather.23.cloned.1.call-done.wout_ref = bf16[1536,768]{1,0:T(8,128)(2,1)} async-done(((bf16[192,768]{1,0:T(8,128)(2,1)}), bf16[1536,768]{1,0:T(8,128)(2,1)}) %all-gather.23.cloned.1.call-update) | async-done | bytes 2359312 | tf_op jit(solution)/shard_map/all_gather | solution.py:561
  435.5 29.3 %all-gather.21.cloned.1.call-done.rows_ref = bf16[1024,1536]{1,0:T(8,128)(2,1)} async-done(((bf16[256,1536]{1,0:T(8,128)(2,1)}), bf16[1024,1536]{1,0:T(8,128)(2,1)}) %all-gather.21.cloned.1.call-update) | async-done | bytes 3145744 | tf_op jit(solution)/shard_map/all_gather | solution.py:569
  464.9 26.2 %shard_map.255 = (bf16[1024,1536]{1,0:T(8,128)(2,1)}, f32[8,1024]{1,0:T(8,128)}, f32[1024,768]{1,0:T(8,128)}, f32[1024,768]{1,0:T(8,128)}, f32[1024,768]{1,0:T(8...) custom-call(bf16[1024,1536]{1,0:T(8,128)(2,1)} %all-gather.21.cloned, ...), custom_call_target="tpu_custom_call" | custom-call | flops 8455716864 | bytes 40000000 | tf_op jit(solution)/shard_map/pallas_call | solution.py:354
  491.1 38.1 %reduce-scatter.17.cloned.1.call-done = bf16[256,1536]{1,0:T(8,128)(2,1)} async-done(((bf16[1024,1536]{1,0:T(8,128)(2,1)}), bf16[256,1536]{1,0:T(8,128)(2,1)}) %reduce-scatter.17.cloned.1.call-update) | async-done | bytes 786448 | tf_op jit(solution)/shard_map/reduce_scatter | solution.py:573
  529.2 2.2 fusion.11
  533.1 5.7 all-reduce.12
  538.9 6.1 all_gather.61.sc_ref
  545.1 15.2 all-gather.25.cloned.1.call-done.top_ref
  560.3 37.8 %shard_map.256 = (bf16[1024,1536]{1,0:T(8,128)(2,1)}, bf16[1024,768]{1,0:T(8,128)(2,1)}, bf16[1024,768]{1,0:T(8,128)(2,1)}, bf16[1024,128]{1,0:T(8,128)(2,1)}, b...) custom-call(bf16[1024,1536]{1,0:T(8,128)(2,1)} %all-gather.25.cloned.1.call-done.top_, ...), custom_call_target="tpu_custom_call" | custom-call | flops 8455716864 | bytes 40000000 | tf_op jit(solution)/shard_map/pallas_call | solution.py:409
  598.1 38.1 %reduce-scatter.19.cloned.1.call-done = bf16[256,1536]{1,0:T(8,128)(2,1)} async-done(((bf16[1024,1536]{1,0:T(8,128)(2,1)}), bf16[256,1536]{1,0:T(8,128)(2,1)}) %reduce-scatter.19.cloned.1.call-update) | async-done | bytes 786448 | tf_op jit(solution)/shard_map/reduce_scatter | solution.py:607
  638.2 2.9 fusion.9
  641.2 3.7 convolution_convert_fusion.8
  645.0 5.8 all_gather.63.sc_ref
  650.8 19.0 %all-gather.27.cloned.1.call-done.top_ref = bf16[1024,1536]{1,0:T(8,128)(2,1)} async-done(((bf16[256,1536]{1,0:T(8,128)(2,1)}), bf16[1024,1536]{1,0:T(8,128)(2,1)}) %all-gather.27.cloned.1.call-update) | async-done | bytes 3145744 | tf_op jit(solution)/shard_map/all_gather | solution.py:588
  669.8 37.9 %shard_map.257 = (bf16[1024,1536]{1,0:T(8,128)(2,1)}, bf16[1024,768]{1,0:T(8,128)(2,1)}, bf16[1024,768]{1,0:T(8,128)(2,1)}, bf16[1024,128]{1,0:T(8,128)(2,1)}, b...) custom-call(bf16[1024,1536]{1,0:T(8,128)(2,1)} %all-gather.27.cloned.1.call-done.top_, ...), custom_call_target="tpu_custom_call" | custom-call | flops 8455716864 | bytes 40000000 | tf_op jit(solution)/shard_map/pallas_call | solution.py:409
  707.7 2.7 convolution_convert_fusion.9
  710.5 4.0 convolution_convert_fusion.6
  714.6 3.9 convolution_convert_fusion.7
  718.8 6.0 fusion
  726.2 6.0 convolution_convert_fusion.1
  733.6 6.1 convolution_convert_fusion.4
  741.1 6.0 convolution_convert_fusion.5
  748.5 6.0 convolution_convert_fusion.2
  755.9 6.0 convolution_convert_fusion.3
  763.5 37.5 %psum.22 = f32[2,8,768]{2,1,0:T(8,128)S(1)} all-reduce(f32[2,8,768]{2,1,0:T(8,128)S(1)} %pad_maximum_fusion), channel_id=1, replica_groups=mesh['dp'=8,'tensor'=4] {'dp'}, use_global_device_ids=true, to_apply=%region_25.26 | all-reduce | flops 12288 | bytes 98304 | tf_op jit(solution)/shard_map/psum | solution.py:620
  805.1 95.0 %reduce-scatter.33.cloned.1.call-done = bf16[48,256]{1,0:T(8,128)(2,1)} async-done(((bf16[1536,256]{1,0:T(8,128)(2,1)}), bf16[48,256]{1,0:T(8,128)(2,1)}) %reduce-scatter.33.cloned.1.call-update) | async-done | bytes 24592 | tf_op jit(solution)/shard_map/reduce_scatter | solution.py:599
  900.1 100.9 %reduce-scatter.31.cloned.1.call-done = bf16[48,256]{1,0:T(8,128)(2,1)} async-done(((bf16[1536,256]{1,0:T(8,128)(2,1)}), bf16[48,256]{1,0:T(8,128)(2,1)}) %reduce-scatter.31.cloned.1.call-update) | async-done | bytes 24592 | tf_op jit(solution)/shard_map/reduce_scatter | solution.py:599
  1002.4 70.4 %reduce-scatter.41.cloned.1.call-done = bf16[192,768]{1,0:T(8,128)(2,1)} async-done(((bf16[1536,768]{1,0:T(8,128)(2,1)}), bf16[192,768]{1,0:T(8,128)(2,1)}) %reduce-scatter.41.cloned.1.call-update) | async-done | bytes 294928 | tf_op jit(solution)/shard_map/reduce_scatter | solution.py:599
  1072.8 72.1 %reduce-scatter.39.cloned.1.call-done = bf16[192,768]{1,0:T(8,128)(2,1)} async-done(((bf16[1536,768]{1,0:T(8,128)(2,1)}), bf16[192,768]{1,0:T(8,128)(2,1)}) %reduce-scatter.39.cloned.1.call-update) | async-done | bytes 294928 | tf_op jit(solution)/shard_map/reduce_scatter | solution.py:599
  1147.0 69.7 %reduce-scatter.25.cloned.1.call-done = bf16[192,768]{1,0:T(8,128)(2,1)} async-done(((bf16[1536,768]{1,0:T(8,128)(2,1)}), bf16[192,768]{1,0:T(8,128)(2,1)}) %reduce-scatter.25.cloned.1.call-update) | async-done | bytes 294928 | tf_op jit(solution)/shard_map/reduce_scatter | solution.py:599
  1216.7 72.1 %reduce-scatter.23.cloned.1.call-done = bf16[192,768]{1,0:T(8,128)(2,1)} async-done(((bf16[1536,768]{1,0:T(8,128)(2,1)}), bf16[192,768]{1,0:T(8,128)(2,1)}) %reduce-scatter.23.cloned.1.call-update) | async-done | bytes 294928 | tf_op jit(solution)/shard_map/reduce_scatter | solution.py:599
  1288.8 2.1 maximum_convert_fusion
  1291.0 70.0 %reduce-scatter.29.cloned.1.call-done = bf16[192,768]{1,0:T(8,128)(2,1)} async-done(((bf16[1536,768]{1,0:T(8,128)(2,1)}), bf16[192,768]{1,0:T(8,128)(2,1)}) %reduce-scatter.29.cloned.1.call-update) | async-done | bytes 294928 | tf_op jit(solution)/shard_map/reduce_scatter | solution.py:599
  1361.0 72.1 %reduce-scatter.27.cloned.1.call-done = bf16[192,768]{1,0:T(8,128)(2,1)} async-done(((bf16[1536,768]{1,0:T(8,128)(2,1)}), bf16[192,768]{1,0:T(8,128)(2,1)}) %reduce-scatter.27.cloned.1.call-update) | async-done | bytes 294928 | tf_op jit(solution)/shard_map/reduce_scatter | solution.py:599
  1433.1 2.3 maximum_convert_fusion.1
  1435.4 37.3 %reduce-scatter.21.cloned.1.call-done = bf16[256,1536]{1,0:T(8,128)(2,1)} async-done(((bf16[1024,1536]{1,0:T(8,128)(2,1)}), bf16[256,1536]{1,0:T(8,128)(2,1)}) %reduce-scatter.21.cloned.1.call-update) | async-done | bytes 786448 | tf_op jit(solution)/shard_map/reduce_scatter | solution.py:607
  1474.4 39.7 %all-reduce.13 = (f32[2,1536]{1,0:T(2,128)}, f32[2,8,256]{2,1,0:T(8,128)S(1)}) all-reduce(f32[2,1536]{1,0:T(2,128)S(1)} %pad_maximum_fusion.2, f32[2,8,256]{2,1,0:T(8,128)S(1)} %pad_maximum_fusion.1), channel_id=1, replica_groups=mesh['dp'=8,'tensor'=4] {'dp','tensor'}, use_global_device_ids=true, to_apply=%region_24.25 | all-reduce | flops 7168 | bytes 57344 | tf_op jit(solution)/shard_map/psum | solution.py:621
  (201 shorter events, 43.3 us)
Async XLA Ops:
  7.2 2.1 copy-start.8
  7.2 3.1 copy-start.9
  7.2 94.1 %all-gather.29.cloned.1.call-start = ((), (), s32[]{:S(2)}) async-start(), calls=%async_computation.34 | async-start | bytes 2654208 | tf_op jit(solution)/shard_map/all_gather | solution.py:555
  9.2 1.9 copy-start.17
  9.2 2.0 copy-start
  9.3 113.5 %all-gather.31.cloned.1.call-start = ((), (), s32[]{:S(2)}) async-start(), calls=%async_computation.35 | async-start | bytes 2654208 | tf_op jit(solution)/shard_map/all_gather | solution.py:556
  10.2 166.0 %all-gather.19.cloned.1.call-start = ((), (), s32[]{:S(2)}) async-start(), calls=%async_computation.15 | async-start | bytes 2654208 | tf_op jit(solution)/shard_map/all_gather | solution.py:561
  11.1 194.2 %all-gather.17.cloned.1.call-start = ((), (), s32[]{:S(2)}) async-start(), calls=%async_computation.14 | async-start | bytes 3932160 | tf_op jit(solution)/shard_map/all_gather | solution.py:569
  11.3 2.0 copy-start.22
  11.3 2.2 copy-start.12
  12.7 2.5 copy-start.23
  12.7 2.5 copy-start.24
  12.7 3.1 copy-start.21
  12.7 39.7 %copy-start.18 = (f32[2,4,256]{2,1,0:T(4,128)S(1)}, f32[2,4,256]{2,1,0:T(4,128)}, u32[]{:S(2)}) copy-start(f32[2,4,256]{2,1,0:T(4,128)} %param.25) | copy-start | bytes 24580
  12.7 40.3 %copy-start.13 = (f32[2,4,768]{2,1,0:T(4,128)S(1)}, f32[2,4,768]{2,1,0:T(4,128)}, u32[]{:S(2)}) copy-start(f32[2,4,768]{2,1,0:T(4,128)} %param.24) | copy-start | bytes 73732
  12.7 40.9 %copy-start.11 = (bf16[2,48,256]{2,1,0:T(8,128)(2,1)S(1)}, bf16[2,48,256]{2,1,0:T(8,128)(2,1)}, u32[]{:S(2)}) copy-start(bf16[2,48,256]{2,1,0:T(8,128)(2,1)} %param.20) | copy-start | bytes 147460
  12.7 257.5 %reduce-scatter.15.cloned.1.call-start = ((), (), s32[]{:S(2)}) async-start(), calls=%async_computation.16 | async-start | bytes 3932160 | tf_op jit(solution)/shard_map/reduce_scatter | solution.py:573
  232.1 2.2 copy-start.25
  232.1 123.4 %all-gather.33.cloned.1.call-start = ((), (), s32[]{:S(2)}) async-start(), calls=%async_computation.36 | async-start | bytes 2654208 | tf_op jit(solution)/shard_map/all_gather | solution.py:555
  232.7 149.8 %all-gather.35.cloned.1.call-start = ((), (), s32[]{:S(2)}) async-start(), calls=%async_computation.37 | async-start | bytes 2654208 | tf_op jit(solution)/shard_map/all_gather | solution.py:556
  233.4 202.1 %all-gather.23.cloned.1.call-start = ((), (), s32[]{:S(2)}) async-start(), calls=%async_computation.18 | async-start | bytes 2654208 | tf_op jit(solution)/shard_map/all_gather | solution.py:561
  234.2 230.7 %all-gather.21.cloned.1.call-start = ((), (), s32[]{:S(2)}) async-start(), calls=%async_computation.17 | async-start | bytes 3932160 | tf_op jit(solution)/shard_map/all_gather | solution.py:569
  273.2 256.0 %reduce-scatter.17.cloned.1.call-start = ((), (), s32[]{:S(2)}) async-start(), calls=%async_computation.19 | async-start | bytes 3932160 | tf_op jit(solution)/shard_map/reduce_scatter | solution.py:573
  491.0 38.1 %copy-start.2 = (f32[256,1536]{1,0:T(8,128)S(1)}, f32[256,1536]{1,0:T(8,128)}, u32[]{:S(2)}) copy-start(f32[256,1536]{1,0:T(8,128)} %param.17) | copy-start | bytes 4718596
  491.1 69.2 %all-gather.25.cloned.1.call-start = ((), (), s32[]{:S(2)}) async-start(), calls=%async_computation.20 | async-start | bytes 3932160 | tf_op jit(solution)/shard_map/all_gather | solution.py:588
  531.4 104.8 %reduce-scatter.19.cloned.1.call-start = ((), (), s32[]{:S(2)}) async-start(), calls=%async_computation.21 | async-start | bytes 3932160 | tf_op jit(solution)/shard_map/reduce_scatter | solution.py:607
  598.1 71.7 %all-gather.27.cloned.1.call-start = ((), (), s32[]{:S(2)}) async-start(), calls=%async_computation.22 | async-start | bytes 3932160 | tf_op jit(solution)/shard_map/all_gather | solution.py:588
  636.2 2.0 copy-start.5
  636.2 2.0 copy-start.7
  638.2 2.9 copy-start.10
  641.1 121.4 %reduce-scatter.37.cloned.1.call-start = ((), (), s32[]{:S(2)}) async-start(), calls=%async_computation.31 | async-start | bytes 442368 | tf_op jit(solution)/shard_map/reduce_scatter | solution.py:599
  644.9 158.6 %reduce-scatter.35.cloned.1.call-start = ((), (), s32[]{:S(2)}) async-start(), calls=%async_computation.30 | async-start | bytes 442368 | tf_op jit(solution)/shard_map/reduce_scatter | solution.py:599
  669.8 37.9 %copy-start.4 = (bf16[1024,1536]{1,0:T(8,128)(2,1)S(1)}, bf16[1024,1536]{1,0:T(8,128)(2,1)}, u32[]{:S(2)}) copy-start(bf16[1024,1536]{1,0:T(8,128)(2,1)} %all-gather.17.cloned.1.call-done.rows_ref) | copy-start | bytes 9437188
  710.5 189.6 %reduce-scatter.33.cloned.1.call-start = ((), (), s32[]{:S(2)}) async-start(), calls=%async_computation.29 | async-start | bytes 811008 | tf_op jit(solution)/shard_map/reduce_scatter | solution.py:599
  710.5 4.1 copy-start.32
  714.5 286.5 %reduce-scatter.31.cloned.1.call-start = ((), (), s32[]{:S(2)}) async-start(), calls=%async_computation.28 | async-start | bytes 811008 | tf_op jit(solution)/shard_map/reduce_scatter | solution.py:599
  714.6 4.2 copy-start.28
  718.6 354.3 %reduce-scatter.41.cloned.1.call-start = ((), (), s32[]{:S(2)}) async-start(), calls=%async_computation.33 | async-start | bytes 2654208 | tf_op jit(solution)/shard_map/reduce_scatter | solution.py:599
  724.8 420.0 %reduce-scatter.39.cloned.1.call-start = ((), (), s32[]{:S(2)}) async-start(), calls=%async_computation.32 | async-start | bytes 2654208 | tf_op jit(solution)/shard_map/reduce_scatter | solution.py:599
  732.2 484.5 %reduce-scatter.25.cloned.1.call-start = ((), (), s32[]{:S(2)}) async-start(), calls=%async_computation.25 | async-start | bytes 2654208 | tf_op jit(solution)/shard_map/reduce_scatter | solution.py:599
  739.7 549.1 %reduce-scatter.23.cloned.1.call-start = ((), (), s32[]{:S(2)}) async-start(), calls=%async_computation.24 | async-start | bytes 2654208 | tf_op jit(solution)/shard_map/reduce_scatter | solution.py:599
  747.1 613.9 %reduce-scatter.29.cloned.1.call-start = ((), (), s32[]{:S(2)}) async-start(), calls=%async_computation.27 | async-start | bytes 2654208 | tf_op jit(solution)/shard_map/reduce_scatter | solution.py:599
  754.5 678.6 %reduce-scatter.27.cloned.1.call-start = ((), (), s32[]{:S(2)}) async-start(), calls=%async_computation.26 | async-start | bytes 2654208 | tf_op jit(solution)/shard_map/reduce_scatter | solution.py:599
  761.9 710.8 %reduce-scatter.21.cloned.1.call-start = ((), (), s32[]{:S(2)}) async-start(), calls=%async_computation.23 | async-start | bytes 3932160 | tf_op jit(solution)/shard_map/reduce_scatter | solution.py:607
  762.0 41.0 %copy-start.19 = (f32[8,256]{1,0:T(8,128)S(1)}, f32[8,256]{1,0:T(8,128)}, u32[]{:S(2)}) copy-start(f32[8,256]{1,0:T(8,128)} %get-tuple-element.85) | copy-start | bytes 24580
  762.0 41.0 %copy-start.20 = (f32[8,256]{1,0:T(8,128)S(1)}, f32[8,256]{1,0:T(8,128)}, u32[]{:S(2)}) copy-start(f32[8,256]{1,0:T(8,128)} %get-tuple-element.84) | copy-start | bytes 24580
  1433.1 81.6 %copy-start.3 = (f32[256,1536]{1,0:T(8,128)S(1)}, f32[256,1536]{1,0:T(8,128)}, u32[]{:S(2)}) copy-start(f32[256,1536]{1,0:T(8,128)} %get-tuple-element.124) | copy-start | bytes 4718596
  1472.7 42.0 %copy-start.6 = (bf16[256,1536]{1,0:T(8,128)(2,1)S(1)}, bf16[256,1536]{1,0:T(8,128)(2,1)}, u32[]{:S(2)}) copy-start(bf16[256,1536]{1,0:T(8,128)(2,1)} %reduce-scatter.21.cloned.1.call-done) | copy-start | bytes 2359300
  (9 other events, 13.2 us)
Sparse Core Ops, SparseCore 0:
  10.8 57.8 all-gather.28
  71.4 51.2 all-gather.30
  125.5 50.5 all-gather.18
  178.2 27.0 all-gather.16
  232.2 37.9 reduce-scatter.14
  273.1 56.0 all-gather.32
  331.5 50.8 all-gather.34
  384.9 50.5 all-gather.22
  437.8 27.0 all-gather.20
  491.2 37.9 reduce-scatter.16
  531.5 28.6 all-gather.24
  598.2 37.9 reduce-scatter.18
  641.2 28.5 all-gather.26
  673.3 61.3 reduce-scatter.36
  738.7 60.4 reduce-scatter.34
  805.5 94.5 reduce-scatter.32
  906.4 94.5 reduce-scatter.30
  1004.7 68.0 reduce-scatter.40
  1076.7 68.1 reduce-scatter.38
  1148.6 68.0 reduce-scatter.24
  1220.6 68.1 reduce-scatter.22
  1292.7 68.1 reduce-scatter.28
  1364.9 68.1 reduce-scatter.26
  1435.7 36.9 reduce-scatter.20

commit v2 on v1

--- a/solution.py
+++ b/solution.py
@@ -520,6 +520,965 @@
     ).astype(BF16)
 
 
+MESH = pl.DeviceIdType.MESH
+ANY = pl.BlockSpec(memory_space=pl.ANY)
+IN_VMEM = pl.BlockSpec(memory_space=pltpu.VMEM)
+PIECES = 4
+TENSOR = 4
+LATE = 1e9
+
+
+class Place:
+    def __init__(self, line):
+        self.line = line
+        dp, t = lax.axis_index("dp"), lax.axis_index("tensor")
+        self.dp, self.t = dp, t
+        self.z, self.x = lax.div(dp, 2), lax.rem(dp, 2)
+        self.other = 1 - self.x
+        self.sibling = t + 1 - 2 * lax.rem(t, 2)
+        self.mate = lax.rem(t + 2, TENSOR)
+        self.diagonal = TENSOR - 1 - t
+        self.right = (lax.rem(self.z + 1, line) * 2 + self.x, t)
+        self.left = (lax.rem(self.z + line - 1, line) * 2 + self.x, t)
+        self.across = (self.z * 2 + self.other, t)
+
+    def tensor_peers(self):
+        return [(self.dp, self.sibling), (self.dp, self.mate), (self.dp, self.diagonal)]
+
+    def partner(self, bit):
+        return (self.dp + bit - 2 * bit * lax.rem(lax.div(self.dp, bit), 2), self.t)
+
+    def greet(self, across=True, far_bits=()):
+        barrier = pltpu.get_barrier_semaphore()
+        peers = self.tensor_peers()
+        if across:
+            peers = peers + [self.across]
+        peers = peers + [self.partner(bit) for bit in far_bits]
+        for peer in peers:
+            pl.semaphore_signal(barrier, inc=1, device_id=peer, device_id_type=MESH)
+        count = len(peers)
+        if across and self.line > 1:
+            has_right = self.z < self.line - 1
+            has_left = self.z > 0
+
+            @pl.when(has_right)
+            def _():
+                pl.semaphore_signal(barrier, inc=1, device_id=self.right, device_id_type=MESH)
+
+            @pl.when(has_left)
+            def _():
+                pl.semaphore_signal(barrier, inc=1, device_id=self.left, device_id_type=MESH)
+
+            count = count + has_right.astype(jnp.int32) + has_left.astype(jnp.int32)
+        pl.semaphore_wait(barrier, count)
+
+
+class Timeline:
+    def __init__(self):
+        self.steps = []
+
+    def add(self, when, step):
+        self.steps.append((when, len(self.steps), step))
+
+    def run(self):
+        for _, _, step in sorted(self.steps, key=lambda entry: entry[:2]):
+            step()
+
+
+def remote(src, dst, send, recv, device):
+    return pltpu.make_async_remote_copy(
+        src_ref=src, dst_ref=dst, send_sem=send, recv_sem=recv, device_id=device, device_id_type=MESH
+    )
+
+
+def gather_semaphores(count, line):
+    return [pltpu.SemaphoreType.DMA((count, 2, line))] * 5
+
+
+def gather_weights(place, timeline, items, sems, start=0.0):
+    send_r, send_l, send_x, recv_z, recv_x = sems
+    line = place.line
+    z = place.z
+
+    def copy(i, way, zz, xs, src=None):
+        dst = items[i][1](zz, xs)
+        return remote(
+            dst if src is None else src,
+            dst,
+            (send_r, send_l, send_x)[way].at[i, xs, zz],
+            (recv_x if way == 2 else recv_z).at[i, xs, zz],
+            (place.right, place.left, place.across)[way],
+        )
+
+    def begin(i):
+        own = items[i][0]
+
+        def step():
+            @pl.when(z < line - 1)
+            def _():
+                copy(i, 0, z, place.x, own).start()
+
+            @pl.when(z > 0)
+            def _():
+                copy(i, 1, z, place.x, own).start()
+
+            copy(i, 2, z, place.x, own).start()
+
+        return step
+
+    def hop(i, way, k, xs, to_x):
+        source = z - k if way == 0 else z + k
+        here = source >= 0 if way == 0 else source < line
+        more = z < line - 1 if way == 0 else z > 0
+
+        def arrive():
+            @pl.when(here)
+            def _():
+                copy(i, way, source, xs).wait_recv()
+                if to_x:
+                    copy(i, 2, source, xs).start()
+
+            @pl.when(here & more)
+            def _():
+                copy(i, way, source, xs).start()
+
+        def finish():
+            @pl.when(here & more)
+            def _():
+                copy(i, way, source, xs).wait_send()
+
+            if to_x:
+
+                @pl.when(here)
+                def _():
+                    copy(i, 2, source, xs).wait_send()
+
+        return arrive, finish
+
+    def side(i):
+        def step():
+            copy(i, 2, z, place.other).wait_recv()
+
+            @pl.when(z < line - 1)
+            def _():
+                copy(i, 0, z, place.other).start()
+
+            @pl.when(z > 0)
+            def _():
+                copy(i, 1, z, place.other).start()
+
+        return step
+
+    def end(i):
+        route = items[i][2]
+
+        def step():
+            for xs in (place.x,) if route == "zx" else (place.x, place.other):
+
+                @pl.when(z < line - 1)
+                def _(xs=xs):
+                    copy(i, 0, z, xs).wait_send()
+
+                @pl.when(z > 0)
+                def _(xs=xs):
+                    copy(i, 1, z, xs).wait_send()
+
+            copy(i, 2, z, place.x).wait_send()
+
+        return step
+
+    def settle(i):
+        def step():
+            for zz in range(line):
+                copy(i, 2, zz, place.other).wait_recv()
+
+        return step
+
+    period = sum(item[3] for item in items)
+    passed = 0.0
+    for i, (_, _, route, cost, due) in enumerate(items):
+        passed += cost
+        timeline.add(start, begin(i))
+        if route == "xz":
+            timeline.add(start + passed, side(i))
+        for k in range(1, line):
+            for way in (0, 1):
+                for xs in (place.x,) if route == "zx" else (place.x, place.other):
+                    late = 0.0 if xs is place.x else period / 2
+                    arrive, finish = hop(i, way, k, xs, route == "zx")
+                    timeline.add(start + period * (k - 1) + passed + late, arrive)
+                    timeline.add(LATE, finish)
+        if route == "zx":
+            timeline.add(due, settle(i))
+        timeline.add(LATE, end(i))
+
+
+def scatter_semaphores(count, line):
+    return [pltpu.SemaphoreType.DMA((count, line))] * 6
+
+
+def add_into(target, other, rows):
+    step = 48
+
+    def body(n, carry):
+        part = pl.ds(pl.multiple_of(n * step, step), step)
+        target[part, :] = (target[part, :].astype(F32) + other[part, :].astype(F32)).astype(BF16)
+        return carry
+
+    lax.fori_loop(0, rows // step, body, 0)
+
+
+def scatter_order(line):
+    order = []
+    for n in range((line + 1) // 2):
+        order += [n] if n == line - 1 - n else [n, line - 1 - n]
+    return order
+
+
+def scatter_weights(place, timeline, items, sems):
+    send_x, recv_x, send_r, recv_r, send_l, recv_l = sems
+    line = place.line
+    z = place.z
+
+    def side(i, zz):
+        piece, (land_x, _, _), *_ = items[i]
+        return remote(
+            piece(zz, place.other), land_x.at[zz], send_x.at[i, zz], recv_x.at[i, zz], place.across
+        )
+
+    def along(i, zz, way, source=None):
+        land = items[i][1][1 + way]
+        return remote(
+            land.at[zz] if source is None else source,
+            land.at[zz],
+            (send_r, send_l)[way].at[i, zz],
+            (recv_r, recv_l)[way].at[i, zz],
+            (place.right, place.left)[way],
+        )
+
+    def begin(i, zz):
+        return lambda: side(i, zz).start()
+
+    def join(i, zz):
+        def step():
+            side(i, zz).wait_recv()
+            land = items[i][1][0]
+            add_into(land.at[zz], items[i][0](zz, place.x), land.shape[1])
+
+        return step
+
+    def send(i, zz, way, h):
+        land = items[i][1]
+        if way == 0:
+            mine, first = (z == h) & (z < zz), h == 0
+        else:
+            mine, first = (z == line - 1 - h) & (z > zz), h == 0
+
+        def step():
+            @pl.when(mine)
+            def _():
+                if first:
+                    along(i, zz, way, land[0].at[zz]).start()
+                else:
+                    along(i, zz, way).wait_recv()
+                    add_into(land[1 + way].at[zz], land[0].at[zz], land[0].shape[1])
+                    along(i, zz, way).start()
+
+        return step
+
+    def last(i):
+        _, (land_x, land_r, land_l), out, *_ = items[i]
+
+        def step():
+            out[...] = land_x[z].astype(F32)
+
+            @pl.when(z > 0)
+            def _():
+                along(i, z, 0).wait_recv()
+                out[...] += land_r[z].astype(F32)
+
+            @pl.when(z < line - 1)
+            def _():
+                along(i, z, 1).wait_recv()
+                out[...] += land_l[z].astype(F32)
+
+        return step
+
+    def end(i, zz):
+        def step():
+            side(i, zz).wait_send()
+
+            @pl.when(z < zz)
+            def _():
+                along(i, zz, 0).wait_send()
+
+            @pl.when(z > zz)
+            def _():
+                along(i, zz, 1).wait_send()
+
+        return step
+
+    now = 0.0
+    for i, (_, _, _, cost, ready) in enumerate(items):
+        now = max(now, ready)
+        for zz in scatter_order(line):
+            now += cost
+            timeline.add(ready, begin(i, zz))
+            timeline.add(now, join(i, zz))
+            for way in (0, 1):
+                hops = zz if way == 0 else line - 1 - zz
+                for h in range(hops):
+                    timeline.add(now + 0.01 + h * cost, send(i, zz, way, h))
+            timeline.add(LATE, end(i, zz))
+        timeline.add(now + line * cost, last(i))
+
+
+def spread_semaphores():
+    return [pltpu.SemaphoreType.DMA((PIECES,))] * 6
+
+
+def spread_rows(place, own, whole, sems):
+    send_y, recv_y, send_s, recv_s, send_f, recv_f = sems
+    rows = own.shape[0]
+    step = rows // PIECES
+
+    def at(owner, p):
+        return whole.at[pl.ds(pl.multiple_of(owner * rows, rows) + p * step, step), :]
+
+    def source(p):
+        return own.at[pl.ds(p * step, step), :]
+
+    def to_mate(p):
+        return remote(
+            source(p), at(place.t, p), send_y.at[p], recv_y.at[p], (place.dp, place.mate)
+        )
+
+    def to_sibling(p):
+        return remote(
+            source(p), at(place.t, p), send_s.at[p], recv_s.at[p], (place.dp, place.sibling)
+        )
+
+    def passed_on(p):
+        return remote(
+            at(place.mate, p), at(place.mate, p), send_f.at[p], recv_f.at[p], (place.dp, place.sibling)
+        )
+
+    def begin(p):
+        to_mate(p).start()
+        to_sibling(p).start()
+
+    def forward(p):
+        to_mate(p).wait_recv()
+        passed_on(p).start()
+
+    def finish():
+        for p in range(PIECES):
+            to_mate(p).wait_send()
+            to_sibling(p).wait()
+            passed_on(p).wait()
+
+    return begin, forward, finish
+
+
+def reduce_semaphores():
+    return [pltpu.SemaphoreType.DMA((PIECES,))] * 6
+
+
+def reduce_rows(place, timeline, part, lands, sems, owner, rate, start=0.0):
+    land_far, land_near, land_mate = lands
+    send_a, recv_a, send_b, recv_b, send_z, recv_z = sems
+    rows = land_far.shape[0]
+    step = rows // PIECES
+
+    def at(block, p):
+        return part.at[pl.ds(pl.multiple_of(block * rows, rows) + p * step, step), :]
+
+    def own(ref, p):
+        return ref.at[pl.ds(p * step, step), :]
+
+    def far(p):
+        return remote(
+            at(place.diagonal, p), own(land_far, p), send_a.at[p], recv_a.at[p], (place.dp, place.sibling)
+        )
+
+    def near(p):
+        return remote(
+            at(place.sibling, p), own(land_near, p), send_b.at[p], recv_b.at[p], (place.dp, place.sibling)
+        )
+
+    def over(p):
+        return remote(
+            own(land_far, p), own(land_mate, p), send_z.at[p], recv_z.at[p], (place.dp, place.mate)
+        )
+
+    def begin():
+        for p in range(PIECES):
+            far(p).start()
+        for p in range(PIECES):
+            near(p).start()
+
+    def middle(p):
+        def run():
+            far(p).wait_recv()
+            mine = own(land_far, p)
+            mine[...] = (mine[...].astype(F32) + at(place.mate, p)[...].astype(F32)).astype(BF16)
+            over(p).start()
+
+        return run
+
+    def final(p):
+        def run():
+            near(p).wait_recv()
+            over(p).wait_recv()
+            sums = at(place.t, p)[...].astype(F32) + own(land_near, p)[...].astype(F32)
+            owner(p, sums + own(land_mate, p)[...].astype(F32))
+
+        return run
+
+    def finish():
+        for p in range(PIECES):
+            far(p).wait_send()
+            near(p).wait_send()
+            over(p).wait_send()
+
+    timeline.add(start, begin)
+    for p in range(PIECES):
+        timeline.add(start + 1.0 * (p + 1), middle(p))
+        timeline.add(start + 2.0 + rate * (p + 1), final(p))
+    timeline.add(LATE, finish)
+
+
+def share_semaphores():
+    return [pltpu.SemaphoreType.DMA((3,))] * 2
+
+
+def share_blocks(place, source_of, target_of, sems):
+    send, recv = sems
+    peers = (place.sibling, place.mate, place.diagonal)
+    return [
+        remote(source_of(peer), target_of(n), send.at[n], recv.at[n], (place.dp, peer))
+        for n, peer in enumerate(peers)
+    ]
+
+
+BIG = 6.5
+SMALL = 1.1
+
+
+def row_norm(state):
+    return lax.rsqrt(jnp.mean(state * state, axis=1, keepdims=True) + epsilon)
+
+
+def by_rows_piece(whole, rows):
+    def piece(zz, xs):
+        return whole.at[pl.ds(pl.multiple_of((zz * 2 + xs) * rows, rows), rows), :]
+
+    return piece
+
+
+def own_copies(place, blocks, sems):
+    return [
+        pltpu.make_async_copy(own, piece(place.z, place.x), sems.at[n])
+        for n, (own, piece) in enumerate(blocks)
+    ]
+
+
+def weight_gather(place, timeline, refs, wholes, sems, share_sems, own_sems):
+    bc_own, bc_all = refs[4], wholes[4]
+    pieces = [by_rows_piece(whole, ref.shape[0]) for ref, whole in zip(refs[:4], wholes[:4])]
+
+    def bc_piece(zz, xs):
+        return bc_all.at[zz * 2 + xs, place.t]
+
+    due = (3 * BIG + 2 * SMALL) * (place.line - 1) + 3.0
+    items = [
+        (bc_own, bc_piece, "zx", SMALL / 2, due),
+        (refs[3], pieces[3], "zx", SMALL, LATE),
+        (refs[1], pieces[1], "zx", BIG, LATE),
+        (refs[0], pieces[0], "zx", BIG, LATE),
+        (refs[2], pieces[2], "zx", BIG, LATE),
+    ]
+    copies = own_copies(place, [(item[0], item[1]) for item in items], own_sems)
+    shares = share_blocks(
+        place, lambda peer: bc_all.at[:, place.t], lambda n: bc_all.at[:, place.t], share_sems
+    )
+    timeline.add(-1.0, lambda: [copy.start() for copy in copies] and None)
+    timeline.add(1.0, lambda: copies[0].wait())
+    gather_weights(place, timeline, items, sems)
+    timeline.add(due + 0.1, lambda: [copy.start() for copy in shares] and None)
+    timeline.add(LATE + 1, lambda: [copy.wait() for copy in shares] and None)
+    timeline.add(LATE + 1, lambda: [copy.wait() for copy in copies[1:]] and None)
+
+
+def gather_outputs(line, width, inner, dp):
+    shape = jax.ShapeDtypeStruct
+    return [
+        shape((width, inner), BF16),
+        shape((width, inner), BF16),
+        shape((width, inner), BF16),
+        shape((width, LANES), BF16),
+        shape((dp, TENSOR, width // (dp * TENSOR), 2 * N), BF16),
+    ]
+
+
+def gather_scratch(line):
+    return gather_semaphores(5, line) + share_semaphores() + [pltpu.SemaphoreType.DMA((5,))]
+
+
+def start_kernel(line, resid, cotangent, gain, *refs):
+    own, wholes, refs = refs[:5], refs[5:10], refs[10:]
+    rows_all, top_all, normed, low = refs[:4]
+    sems, share_sems, own_sems = refs[4:9], refs[9:11], refs[11]
+    rows_sems, top_sems, local = refs[12:18], refs[18:24], refs[24]
+    place = Place(line)
+    place.greet()
+    timeline = Timeline()
+    weight_gather(place, timeline, own, wholes, sems, share_sems, own_sems)
+    rows = normed.shape[0]
+    block = pl.ds(pl.multiple_of(place.t * rows, rows), rows)
+    local_copies = [
+        pltpu.make_async_copy(normed, rows_all.at[block, :], local.at[0]),
+        pltpu.make_async_copy(low, top_all.at[block, :], local.at[1]),
+    ]
+
+    def prepare():
+        state = resid[...].astype(F32)
+        normed[...] = (state * row_norm(state) * gain[...]).astype(BF16)
+        low[...] = cotangent[...].astype(BF16)
+        for copy in local_copies:
+            copy.start()
+
+    timeline.add(0.5, prepare)
+    for n, (source, whole, group) in enumerate(((normed, rows_all, rows_sems), (low, top_all, top_sems))):
+        begin, forward, finish = spread_rows(place, source, whole, group)
+        for p in range(PIECES):
+            timeline.add(0.6, functools.partial(begin, p))
+            timeline.add(1.0 + (4 * n + p + 1) * 4.4, functools.partial(forward, p))
+        timeline.add(LATE, finish)
+    timeline.add(LATE, lambda: [copy.wait() for copy in local_copies] and None)
+    timeline.run()
+
+
+def call_kernel(kernel, outs, in_specs, out_specs, scratch, number, args):
+    return pl.pallas_call(
+        kernel,
+        out_shape=outs,
+        in_specs=in_specs,
+        out_specs=out_specs,
+        scratch_shapes=scratch,
+        compiler_params=pltpu.CompilerParams(
+            collective_id=number, has_side_effects=True, vmem_limit_bytes=VMEM_LIMIT
+        ),
+    )(*args)
+
+
+def start_layer(line, resid, cotangent, gain, own):
+    rows, width = resid.shape
+    inner = own[0].shape[1]
+    shape = jax.ShapeDtypeStruct
+    outs = gather_outputs(line, width, inner, 2 * line) + [
+        shape((rows * TENSOR, width), BF16),
+        shape((rows * TENSOR, width), BF16),
+    ]
+    scratch = [pltpu.VMEM((rows, width), BF16)] * 2 + gather_scratch(line)
+    scratch += spread_semaphores() * 2 + [pltpu.SemaphoreType.DMA((2,))]
+    return call_kernel(
+        functools.partial(start_kernel, line),
+        outs,
+        [IN_VMEM] * 3 + [ANY] * 5,
+        [ANY] * 7,
+        scratch,
+        0,
+        (resid, cotangent, gain, *own),
+    )
+
+
+def scale_steps(place, timeline, sq, land, scale_row, scale_col, sems, inner_all):
+    rows = scale_col.shape[0]
+
+    def at(owner):
+        return sq.at[:, pl.ds(pl.multiple_of(owner * rows, rows), rows)]
+
+    copies = share_blocks(place, at, lambda n: land.at[n], sems)
+
+    def arrive():
+        for copy in copies:
+            copy.wait()
+        squares = at(place.t)[...] + land[0] + land[1] + land[2]
+        scale = lax.rsqrt(squares / inner_all + epsilon)
+        scale_row[...] = scale
+        scale_col[...] = jnp.transpose(scale)
+
+    timeline.add(-0.5, lambda: [copy.start() for copy in copies] and None)
+    timeline.add(1.5, arrive)
+
+
+RATE_SHARED = 8.8
+RATE = 4.4
+
+
+def middle_kernel(line, inner_all, part, sq, resid, gain, *refs):
+    own, refs = refs[:5], refs[5:]
+    state_out, raw_out, scale_row, rows_all, refs = *refs[:4], refs[4:]
+    wholes, refs = refs[:5], refs[5:]
+    far, near, mate, land, scale_col, normed = refs[:6]
+    refs = refs[6:]
+    sems, share_sems, own_sems = refs[:5], refs[5:7], refs[7]
+    reduce_sems, sq_sems, rows_sems, local = refs[8:14], refs[14:16], refs[16:22], refs[22]
+    place = Place(line)
+    place.greet()
+    timeline = Timeline()
+    scale_steps(place, timeline, sq, land, scale_row, scale_col, sq_sems, inner_all)
+    rows = normed.shape[0]
+    step = rows // PIECES
+    begin, forward, finish = spread_rows(place, normed, rows_all, rows_sems)
+
+    def owner(p, sums):
+        part_rows = slice(p * step, (p + 1) * step)
+        raw_out[part_rows, :] = sums
+        state = resid[part_rows, :].astype(F32) + sums * scale_col[part_rows, 0:1]
+        state_out[part_rows, :] = state
+        normed[part_rows, :] = (state * row_norm(state) * gain[...]).astype(BF16)
+        begin(p)
+
+    reduce_rows(place, timeline, part, (far, near, mate), reduce_sems, owner, RATE)
+    weight_gather(place, timeline, own, wholes, sems, share_sems, own_sems)
+    for p in range(PIECES):
+        timeline.add(3.0 + RATE * (PIECES + 1 + p), functools.partial(forward, p))
+    block = pl.ds(pl.multiple_of(place.t * rows, rows), rows)
+    keep = pltpu.make_async_copy(normed, rows_all.at[block, :], local.at[0])
+    timeline.add(3.0 + RATE * PIECES, keep.start)
+    timeline.add(LATE, keep.wait)
+    timeline.add(LATE, finish)
+    timeline.run()
+
+
+def middle_layer(line, inner_all, part, sq, resid, gain, own):
+    rows, width = resid.shape
+    inner = own[0].shape[1]
+    shape = jax.ShapeDtypeStruct
+    outs = [
+        shape((rows, width), F32),
+        shape((rows, width), F32),
+        shape((8, rows), F32),
+        shape((rows * TENSOR, width), BF16),
+    ] + gather_outputs(line, width, inner, 2 * line)
+    scratch = [pltpu.VMEM((rows, width), BF16)] * 3
+    scratch += [pltpu.VMEM((3, 8, rows), F32), pltpu.VMEM((rows, 8), F32), pltpu.VMEM((rows, width), BF16)]
+    scratch += gather_scratch(line) + reduce_semaphores() + share_semaphores() + spread_semaphores()
+    scratch += [pltpu.SemaphoreType.DMA((1,))]
+    return call_kernel(
+        functools.partial(middle_kernel, line, inner_all),
+        outs,
+        [IN_VMEM] * 4 + [ANY] * 5,
+        [IN_VMEM] * 3 + [ANY] * 6,
+        scratch,
+        1,
+        (part, sq, resid, gain, *own),
+    )
+
+
+def per_row_steps(place, timeline, scale_row, cross_col, stage, land, out, sems, inner_all, when):
+    rows = cross_col.shape[0]
+    copies = share_blocks(place, lambda peer: stage, lambda n: land.at[n], sems)
+    peers = (place.sibling, place.mate, place.diagonal)
+
+    def send():
+        cross = jnp.transpose(jnp.broadcast_to(cross_col[:, 0:1], (rows, LANES)))[0:8, :]
+        scale = scale_row[...]
+        coef = scale * scale * scale * cross / inner_all
+        stage[...] = jnp.where(iota2((8, rows), 0) == 0, scale, coef)
+        for copy in copies:
+            copy.start()
+        out[:, pl.ds(pl.multiple_of(place.t * rows, rows), rows)] = stage[...]
+
+    def arrive():
+        for n, (copy, peer) in enumerate(zip(copies, peers)):
+            copy.wait()
+            out[:, pl.ds(pl.multiple_of(peer * rows, rows), rows)] = land[n]
+
+    timeline.add(when, send)
+    timeline.add(LATE, arrive)
+
+
+def top_kernel(
+    line, inner_all, part, sq, state, cotangent, hidden, per_row,
+    far, near, mate, sq_land, row_land, scale_col, scale_row, cross_col, stage, *refs
+):
+    reduce_sems, sq_sems, row_sems = refs[:6], refs[6:8], refs[8:10]
+    place = Place(line)
+    place.greet(across=False)
+    timeline = Timeline()
+    scale_steps(place, timeline, sq, sq_land, scale_row, scale_col, sq_sems, inner_all)
+    step = cross_col.shape[0] // PIECES
+
+    def owner(p, sums):
+        part_rows = slice(p * step, (p + 1) * step)
+        hidden[part_rows, :] = state[part_rows, :] + sums * scale_col[part_rows, 0:1]
+        low = cotangent[part_rows, :].astype(BF16).astype(F32)
+        cross = jnp.sum(low * sums, axis=1, keepdims=True)
+        cross_col[part_rows, :] = jnp.broadcast_to(cross, (step, LANES))
+
+    reduce_rows(place, timeline, part, (far, near, mate), reduce_sems, owner, RATE)
+    per_row_steps(
+        place, timeline, scale_row, cross_col, stage, row_land, per_row, row_sems, inner_all, 1e3
+    )
+    timeline.run()
+
+
+def top_layer(line, inner_all, part, sq, state, cotangent):
+    rows, width = state.shape
+    shape = jax.ShapeDtypeStruct
+    scratch = [pltpu.VMEM((rows, width), BF16)] * 3 + [pltpu.VMEM((3, 8, rows), F32)] * 2
+    scratch += [
+        pltpu.VMEM((rows, 8), F32),
+        pltpu.VMEM((8, rows), F32),
+        pltpu.VMEM((rows, LANES), F32),
+        pltpu.VMEM((8, rows), F32),
+    ]
+    scratch += reduce_semaphores() + share_semaphores() * 2
+    return call_kernel(
+        functools.partial(top_kernel, line, inner_all),
+        [shape((rows, width), F32), shape((8, rows * TENSOR), F32)],
+        [IN_VMEM] * 4,
+        [IN_VMEM] * 2,
+        scratch,
+        2,
+        (part, sq, state, cotangent),
+    )
+
+
+def weight_scatter(place, timeline, grads, outs, lands, sems, bc_land, bc_sum, share_sems):
+    bc = grads[4]
+    shares = share_blocks(
+        place, lambda peer: bc.at[:, peer], lambda n: bc_land.at[n], share_sems
+    )
+    bc_ready = 12.0
+
+    def bc_add():
+        for copy in shares:
+            copy.wait()
+
+        def body(n, carry):
+            total = bc[n, place.t].astype(F32) + bc_land[0, n].astype(F32)
+            total = total + bc_land[1, n].astype(F32) + bc_land[2, n].astype(F32)
+            bc_sum[n] = total.astype(BF16)
+            return carry
+
+        lax.fori_loop(0, bc.shape[0], body, 0)
+
+    timeline.add(-1.0, lambda: [copy.start() for copy in shares] and None)
+    timeline.add(bc_ready, bc_add)
+    items = []
+    for n in range(4):
+        rows = lands[3 * n].shape[1]
+        cost = BIG if n < 3 else SMALL
+        items.append((by_rows_piece(grads[n], rows), lands[3 * n : 3 * n + 3], outs[n], cost, 0.0))
+    items.append((lambda zz, xs: bc_sum.at[zz * 2 + xs], lands[12:15], outs[4], SMALL / 2, bc_ready + 0.1))
+    scatter_weights(place, timeline, items, sems)
+
+
+def scatter_outputs(width, inner, dp):
+    shape = jax.ShapeDtypeStruct
+    rows = width // dp
+    return [shape((rows, inner), F32)] * 3 + [
+        shape((rows, LANES), F32),
+        shape((rows // TENSOR, 2 * N), F32),
+    ]
+
+
+def scatter_scratch(line, width, inner):
+    dp = 2 * line
+    rows = width // dp
+    scratch = [pltpu.VMEM((line, rows, inner), BF16)] * 9
+    scratch += [pltpu.VMEM((line, rows, LANES), BF16)] * 3
+    scratch += [pltpu.VMEM((line, rows // TENSOR, 2 * N), BF16)] * 3
+    scratch += [
+        pltpu.VMEM((3, dp, rows // TENSOR, 2 * N), BF16),
+        pltpu.VMEM((dp, rows // TENSOR, 2 * N), BF16),
+    ]
+    return scratch + scatter_semaphores(5, line) + share_semaphores()
+
+
+def input_gradient(state, gain, before, sums):
+    scale = row_norm(state)
+    gained = sums * gain
+    mean = jnp.mean(gained * state, axis=1, keepdims=True)
+    grad = before + scale * gained - state * (scale * scale * scale * mean)
+    return grad, jnp.sum(sums * state * scale, axis=0, keepdims=True)
+
+
+def turn_kernel(line, inner_all, part, before, state, gain, raw, scale_row, *refs):
+    grads, refs = refs[:5], refs[5:]
+    grad_out, gnorm, per_row, top_all, refs = *refs[:4], refs[4:]
+    outs, refs = refs[:5], refs[5:]
+    far, near, mate, row_land, cross_col, stage, low = refs[:7]
+    refs = refs[7:]
+    lands, bc_land, bc_sum, sems, share_sems = refs[:15], refs[15], refs[16], refs[17:23], refs[23:25]
+    refs = refs[25:]
+    reduce_sems, row_sems, top_sems, local = refs[:6], refs[6:8], refs[8:14], refs[14]
+    place = Place(line)
+    place.greet()
+    timeline = Timeline()
+    rows = low.shape[0]
+    step = rows // PIECES
+    begin, forward, finish = spread_rows(place, low, top_all, top_sems)
+    gnorm[...] = jnp.zeros_like(gnorm)
+
+    def owner(p, sums):
+        part_rows = slice(p * step, (p + 1) * step)
+        grad, column = input_gradient(
+            state[part_rows, :], gain[...], before[part_rows, :], sums
+        )
+        grad_out[part_rows, :] = grad
+        gnorm[0:1, :] += column
+        low[part_rows, :] = grad.astype(BF16)
+        cross = jnp.sum(low[part_rows, :].astype(F32) * raw[part_rows, :], axis=1, keepdims=True)
+        cross_col[part_rows, :] = jnp.broadcast_to(cross, (step, LANES))
+        begin(p)
+
+    reduce_rows(place, timeline, part, (far, near, mate), reduce_sems, owner, RATE)
+    for p in range(PIECES):
+        timeline.add(3.0 + RATE * (PIECES + 1 + p), functools.partial(forward, p))
+    block = pl.ds(pl.multiple_of(place.t * rows, rows), rows)
+    keep = pltpu.make_async_copy(low, top_all.at[block, :], local.at[0])
+    timeline.add(3.0 + RATE * PIECES, keep.start)
+    timeline.add(LATE, keep.wait)
+    timeline.add(LATE, finish)
+    per_row_steps(
+        place, timeline, scale_row, cross_col, stage, row_land, per_row, row_sems, inner_all,
+        3.0 + RATE * PIECES,
+    )
+    weight_scatter(place, timeline, grads, outs, lands, sems, bc_land, bc_sum, share_sems)
+    timeline.run()
+
+
+def turn_layer(line, inner_all, part, before, state, gain, raw, scale_row, grads):
+    rows, width = state.shape
+    inner = grads[0].shape[1]
+    shape = jax.ShapeDtypeStruct
+    outs = [
+        shape((rows, width), F32),
+        shape((8, width), F32),
+        shape((8, rows * TENSOR), F32),
+        shape((rows * TENSOR, width), BF16),
+    ] + scatter_outputs(width, inner, 2 * line)
+    scratch = [pltpu.VMEM((rows, width), BF16)] * 3
+    scratch += [
+        pltpu.VMEM((3, 8, rows), F32),
+        pltpu.VMEM((rows, LANES), F32),
+        pltpu.VMEM((8, rows), F32),
+        pltpu.VMEM((rows, width), BF16),
+    ]
+    scratch += scatter_scratch(line, width, inner)
+    scratch += reduce_semaphores() + share_semaphores() + spread_semaphores()
+    scratch += [pltpu.SemaphoreType.DMA((1,))]
+    return call_kernel(
+        functools.partial(turn_kernel, line, inner_all),
+        outs,
+        [IN_VMEM] * 11,
+        [IN_VMEM] * 3 + [ANY] + [IN_VMEM] * 5,
+        scratch,
+        3,
+        (part, before, state, gain, raw, scale_row, *grads),
+    )
+
+
+def end_kernel(line, part, before, state, gain, gnorm_top, small_a, small_b, bc_a, bc_b, *refs):
+    grads, refs = refs[:5], refs[5:]
+    grad_out, norm_sum, small_sum, bc_sums, refs = *refs[:4], refs[4:]
+    outs, refs = refs[:5], refs[5:]
+    far, near, mate = refs[:3]
+    lands, bc_land, bc_sum, sems, share_sems = refs[3:18], refs[18], refs[19], refs[20:26], refs[26:28]
+    refs = refs[28:]
+    reduce_sems, refs = refs[:6], refs[6:]
+    small_land, bc_land_sums, norm_land, small_send, small_recv = refs
+    dp = 2 * line
+    bits = [1 << n for n in range(dp.bit_length() - 1)]
+    place = Place(line)
+    place.greet(far_bits=[bit for bit in bits if bit >= 4])
+    timeline = Timeline()
+    step = state.shape[0] // PIECES
+    norm_sum[...] = jnp.zeros_like(norm_sum)
+    norm_sum[1:2, :] = gnorm_top[0:1, :]
+    small_sum[0:8, :] = small_a[...]
+    small_sum[8:16, :] = small_b[...]
+    bc_sums[0:8, :] = bc_a[...]
+    bc_sums[8:16, :] = bc_b[...]
+
+    def owner(p, sums):
+        part_rows = slice(p * step, (p + 1) * step)
+        grad, column = input_gradient(
+            state[part_rows, :], gain[...], before[part_rows, :], sums
+        )
+        grad_out[part_rows, :] = grad
+        norm_sum[0:1, :] += column
+
+    reduce_rows(place, timeline, part, (far, near, mate), reduce_sems, owner, RATE)
+    weight_scatter(place, timeline, grads, outs, lands, sems, bc_land, bc_sum, share_sems)
+    partners = [place.partner(bit) for bit in bits]
+    partners += [(place.dp, place.sibling), (place.dp, place.mate)]
+    for n, partner in enumerate(partners):
+        trio = [(bc_sums, bc_land_sums), (norm_sum, norm_land)]
+        if n < len(bits):
+            trio.append((small_sum, small_land))
+        copies = [
+            remote(own, land.at[n], small_send.at[n, m], small_recv.at[n, m], partner)
+            for m, (own, land) in enumerate(trio)
+        ]
+
+        def send(copies=copies):
+            for copy in copies:
+                copy.start()
+
+        def take(copies=copies, trio=trio, n=n):
+            for copy, (own, land) in zip(copies, trio):
+                copy.wait()
+                own[...] += land[n]
+
+        timeline.add(25.0 + 10.0 * n, send)
+        timeline.add(34.9 + 10.0 * n, take)
+    timeline.run()
+
+
+def end_layer(line, part, before, state, gain, gnorm_top, smalls, grads):
+    rows, width = state.shape
+    inner = grads[0].shape[1]
+    shape = jax.ShapeDtypeStruct
+    dp = 2 * line
+    steps = dp.bit_length() - 1
+    outs = [
+        shape((rows, width), F32),
+        shape((8, width), F32),
+        shape((16, inner), F32),
+        shape((16, 2 * N), F32),
+    ] + scatter_outputs(width, inner, dp)
+    scratch = [pltpu.VMEM((rows, width), BF16)] * 3 + scatter_scratch(line, width, inner)
+    scratch += reduce_semaphores()
+    scratch += [
+        pltpu.VMEM((steps, 16, inner), F32),
+        pltpu.VMEM((steps + 2, 16, 2 * N), F32),
+        pltpu.VMEM((steps + 2, 8, width), F32),
+        pltpu.SemaphoreType.DMA((steps + 2, 3)),
+        pltpu.SemaphoreType.DMA((steps + 2, 3)),
+    ]
+    return call_kernel(
+        functools.partial(end_kernel, line),
+        outs,
+        [IN_VMEM] * 14,
+        [IN_VMEM] * 9,
+        scratch,
+        4,
+        (part, before, state, gain, gnorm_top, *smalls, *grads),
+    )
+
+
+def contract(left, right):
+    return lax.dot_general(
+        left, right, (((0,), (0,)), ((), ())), preferred_element_type=F32
+    ).astype(BF16)
+
+
 def on_device(
     resid,
     segment_ids,
@@ -537,102 +1496,94 @@
     d_skip,
     gated_gain,
 ):
-    tensor_size = lax.axis_size("tensor")
+    dp = lax.axis_size("dp")
+    assert lax.axis_size("tensor") == TENSOR and segment_ids.shape[0] == LEN and a_log.shape[0] == 2
+    line = dp // 2
     heads = a_log.shape[1]
     inner = heads * P_SIZE
-    inner_all = inner * tensor_size
-    layers = a_log.shape[0]
+    inner_all = inner * TENSOR
+    width = resid.shape[1]
     aux, segrow = row_masks(segment_ids)
     spread = head_spread(inner)
     args = [
         layer_parameters(layer, conv_x, conv_bc, a_log, dt_bias, d_skip, gated_gain)
-        for layer in range(layers)
+        for layer in range(2)
     ]
-    weights = []
-    for layer in range(layers):
-        weights.append(
-            (
-                lax.all_gather(w_z[layer], "dp", axis=0, tiled=True),
-                lax.all_gather(w_x[layer], "dp", axis=0, tiled=True),
-                lax.all_gather(w_bc[layer], ("dp", "tensor"), axis=0, tiled=True),
-                lax.all_gather(
-                    jnp.pad(w_dt[layer], ((0, 0), (0, LANES - heads))), "dp", axis=0, tiled=True
-                ),
-                lax.all_gather(jnp.transpose(w_out[layer]), "dp", axis=0, tiled=True),
-            )
+    own = [
+        (
+            w_z[layer],
+            w_x[layer],
+            jnp.transpose(w_out[layer]),
+            jnp.pad(w_dt[layer], ((0, 0), (0, LANES - heads))),
+            w_bc[layer],
         )
-    state = resid.astype(F32)
-    states, kept, scales, branches, rows_list = [], [], [], [], []
-    for layer in range(layers):
-        scale_in = lax.rsqrt(jnp.mean(state * state, axis=1, keepdims=True) + epsilon)
-        normed = (state * scale_in * norm_gain[layer]).astype(BF16)
-        rows_all = lax.all_gather(normed, "tensor", axis=0, tiled=True)
-        part, sq, *saved = forward_layer(rows_all, weights[layer], args[layer], aux, segrow)
-        squares = lax.psum_scatter(sq[0], "tensor", scatter_dimension=0, tiled=True)
-        scale_out = lax.rsqrt(squares / inner_all + epsilon)
-        raw = lax.psum_scatter(part, "tensor", scatter_dimension=0, tiled=True).astype(F32)
-        states.append((state, scale_in))
-        kept.append(saved)
-        rows_list.append(rows_all)
-        scales.append(scale_out)
-        branches.append(raw)
-        state = state + raw * scale_out[:, None]
-    grad_state = cotangent
-    grads = [None] * layers
-    for layer in reversed(range(layers)):
-        low = grad_state.astype(BF16)
-        cross = jnp.sum(low.astype(F32) * branches[layer], axis=1)
-        coef = scales[layer] ** 3 * cross / inner_all
-        per_row = jnp.pad(jnp.stack([scales[layer], coef]), ((0, 6), (0, 0)))
-        per_row = lax.all_gather(per_row, "tensor", axis=1, tiled=True)
-        top_all = lax.all_gather(low, "tensor", axis=0, tiled=True)
-        part, ggate, ginner, gstep, gshared, outlow, small, small_bc = backward_layer(
-            top_all, per_row, kept[layer], weights[layer], args[layer], spread, aux, segrow
+        for layer in range(2)
+    ]
+    gains = [norm_gain[layer : layer + 1] for layer in range(2)]
+
+    def arranged(gathered):
+        gate, inner_w, out_w, step_w, shared_w = gathered
+        return gate, inner_w, shared_w.reshape(width, 2 * N), step_w, out_w
+
+    *gathered, rows_low, top_high = start_layer(line, resid, cotangent, gains[0], own[0])
+    weights_low = arranged(gathered)
+    part, sq, *saved_low = forward_layer(rows_low, weights_low, args[0], aux, segrow)
+    state, raw, scale_row, rows_high, *gathered = middle_layer(
+        line, inner_all, part, sq, resid, gains[1], own[1]
+    )
+    weights_high = arranged(gathered)
+    part, sq, *saved_high = forward_layer(rows_high, weights_high, args[1], aux, segrow)
+    hidden, per_row = top_layer(line, inner_all, part, sq, state, cotangent)
+
+    def weight_grads(rows_all, top_all, pulled):
+        ggate, ginner, gstep, gshared, outlow = pulled
+        return (
+            contract(top_all, outlow),
+            contract(rows_all, ggate),
+            contract(rows_all, ginner),
+            contract(rows_all, gstep),
+            contract(rows_all, gshared).reshape(dp, TENSOR, width // (dp * TENSOR), 2 * N),
         )
 
-        def contract(left, right):
-            return lax.dot_general(
-                left, right, (((0,), (0,)), ((), ())), preferred_element_type=F32
-            ).astype(BF16)
-
-        def scatter(values, axes="dp"):
-            return lax.psum_scatter(values, axes, scatter_dimension=0, tiled=True).astype(F32)
-
-        rows_all = rows_list[layer]
-        gz = scatter(contract(rows_all, ggate))
-        gx = scatter(contract(rows_all, ginner))
-        gdt = scatter(contract(rows_all, gstep))[:, :heads]
-        gbc = scatter(contract(rows_all, gshared), ("dp", "tensor"))
-        gout = jnp.transpose(scatter(contract(top_all, outlow)))
-        grad_normed = lax.psum_scatter(
-            part, "tensor", scatter_dimension=0, tiled=True
-        ).astype(F32)
-        state_in, scale_in = states[layer]
-        gained = grad_normed * norm_gain[layer]
-        gnorm = jnp.sum(grad_normed * state_in * scale_in, axis=0)
-        grad_state = (
-            grad_state
-            + scale_in * gained
-            - state_in * scale_in**3 * jnp.mean(gained * state_in, axis=1, keepdims=True)
-        )
-        grads[layer] = (gz, gx, gbc, gdt, gout, gnorm, small, small_bc)
-    stacked = [jnp.stack(values) for values in zip(*grads)]
-    small = lax.psum(stacked[6], "dp")
-    gnorm, small_bc = lax.psum((stacked[5], stacked[7]), ("dp", "tensor"))
+    part, *pulled, small_high, bc_high = backward_layer(
+        top_high, per_row, saved_high, weights_high, args[1], spread, aux, segrow
+    )
+    grads = weight_grads(rows_high, top_high, pulled)
+    grad_state, gnorm_high, per_row, top_low, *grads_high = turn_layer(
+        line, inner_all, part, cotangent, state, gains[1], raw, scale_row, grads
+    )
+    part, *pulled, small_low, bc_low = backward_layer(
+        top_low, per_row, saved_low, weights_low, args[0], spread, aux, segrow
+    )
+    grads = weight_grads(rows_low, top_low, pulled)
+    grad_resid, norm_sum, small, small_bc, *grads_low = end_layer(
+        line,
+        part,
+        grad_state,
+        resid.astype(F32),
+        gains[0],
+        gnorm_high,
+        (small_low, small_high, bc_low, bc_high),
+        grads,
+    )
+    gout, gz, gx, gdt, gbc = [
+        jnp.stack([low, high]) for low, high in zip(grads_low, grads_high)
+    ]
+    small = small.reshape(2, 8, inner)
     return (
-        state,
-        grad_state,
-        stacked[0],
-        stacked[1],
-        stacked[2],
-        stacked[3],
-        stacked[4],
-        gnorm,
+        hidden,
+        grad_resid,
+        gz,
+        gx,
+        gbc,
+        gdt[:, :, :heads],
+        jnp.swapaxes(gout, 1, 2),
+        norm_sum[:2],
         small[:, :TAPS],
-        small_bc[:, :TAPS],
+        small_bc.reshape(2, 8, 2 * N)[:, :TAPS],
         small[:, 6, :heads],
         small[:, 7, :heads],
-        jnp.sum(small[:, 5].reshape(layers, heads, P_SIZE), axis=2),
+        jnp.sum(small[:, 5].reshape(2, heads, P_SIZE), axis=2),
         small[:, 4],
     )
 

time: 1530 us -> 672 us (0.44)
  waiting for transfers between devices: 1010 us -> 0 us
  Pallas kernels: 128 us -> 601 us
  blocking collectives: 265 us -> 0 us
  matrix products: 50.3 us -> 33.3 us
  other arithmetic: 27.7 us -> 10.7 us
    reduce_scatter x14 -> x0, waiting for transfers between devices: 764 us -> none  [the longest x10 622 us: scatter(): lax.psum_scatter(values, axes, scatter_dimension=0, tiled=True).astype(F32)]
    pallas_call x0 -> x5, Pallas kernels: none -> 472 us  [call_kernel(): pl.pallas_call(kernel, out_shape=outs, in_specs=in_specs, out_specs=out_s...]
    all_gather x10 -> x0, waiting for transfers between devices: 248 us -> none  [the longest x2 106 us: on_device(): lax.all_gather(jnp.transpose(w_out[layer]), 'dp', axis=0, tiled=True)]
    all_gather x6 -> x0, blocking collectives: 176 us -> none  [the longest x2 94.6 us: on_device(): lax.all_gather(w_bc[layer], ('dp', 'tensor'), axis=0, tiled=True)]
    psum x2 -> x0, blocking collectives: 77.2 us -> none  [the longest x1 39.7 us: on_device(): gnorm, small_bc = lax.psum((stacked[5], stacked[7]), ('dp', 'tensor'))]
    dot_general x10, matrix products: 50.3 us -> 33.3 us  [contract(): lax.dot_general(left, right, (((0,), (0,)), ((), ())), preferred_element_...]
  transfers between devices with their start and end apart: 24 -> 0, of which waited for: 20 -> 0; matrix products, arithmetic and copies ran while one was open for 5% -> 0% of each run, Pallas kernels for 2% -> 0%
where the time goes in v2:
time: 672 us; the launch traced here: 665 us
  Pallas kernels  601 us (89%)
  matrix products  33.3 us (5%)
  local copies, waits for them, and re-layouts  18.3 us (3%)
  other arithmetic  10.7 us (2%)
    pallas_call x5, Pallas kernels, call_kernel(): pl.pallas_call(kernel, out_shape=outs, in_specs=in_specs, out_specs=out_s...  472 us
    pallas_call x2, Pallas kernels, backward_layer(): pl.pallas_call(backward_kernel, grid=(chunks,), in_specs=[by_rows(width),...  76.3 us
    pallas_call x2, Pallas kernels, forward_layer(): pl.pallas_call(forward_kernel, grid=(chunks,), in_specs=[by_rows(width)]...  52.4 us
    dot_general x10, matrix products, contract(): lax.dot_general(left, right, (((0,), (0,)), ((), ())), preferred_element_...  33.3 us

profile of v2, /device:TPU:0, one launch (start us, length us, event | category | flops | bytes accessed | tf_op | source)
XLA Modules:
  0.0 664.7 jit_solution(5855816714652559707)
XLA Ops:
  0.7 1.4 fusion.13
  2.1 2.3 slice_bitcast_fusion.1
  4.4 0.8 slice_bitcast_fusion
  5.4 0.6 pad.22.refs_3_
  6.0 0.6 slice_bitcast_fusion.6
  6.7 92.0 %shard_map.254 = (bf16[1536,768]{1,0:T(8,128)(2,1)}, bf16[1536,768]{1,0:T(8,128)(2,1)}, bf16[1536,768]{1,0:T(8,128)(2,1)}, bf16[1536,128]{1,0:T(8,128)(2,1)}, bf...) custom-call(bf16[256,1536]{1,0:T(8,128)(2,1)} %resid.3, f32[256,1536]{1,0:T(8,128)} %before.1, ...), custom_call_target="tpu_custom_call" | custom-call | tf_op jit(solution)/shard_map/pallas_call | solution.py:1063
  98.7 0.6 slice_bitcast_fusion.8
  99.3 0.6 slice_bitcast_fusion.10
  99.9 0.6 select_maximum_fusion
  100.8 0.6 pad_maximum_fusion.4
  102.2 0.2 stack.133
  102.7 0.9 pad.24.aux_ref
  103.5 0.6 broadcast_in_dim.26.segrow_ref
  104.1 26.2 %shard_map.255 = (bf16[1024,1536]{1,0:T(8,128)(2,1)}, f32[8,1024]{1,0:T(8,128)}, f32[1024,768]{1,0:T(8,128)}, f32[1024,768]{1,0:T(8,128)}, f32[1024,768]{1,0:T(8...) custom-call(bf16[1024,1536]{1,0:T(8,128)(2,1)} %get-tuple-element.86, ...), custom_call_target="tpu_custom_call" | custom-call | flops 8455716864 | bytes 40000000 | tf_op jit(solution)/shard_map/pallas_call | solution.py:354
  130.5 0.6 pad.25.refs_3_
  131.1 91.3 %shard_map.256 = (f32[256,1536]{1,0:T(8,128)}, f32[256,1536]{1,0:T(8,128)}, f32[8,256]{1,0:T(8,128)}, bf16[1024,1536]{1,0:T(8,128)(2,1)}, bf16[1536,768]{1,0:T(8...) custom-call(bf16[1024,1536]{1,0:T(8,128)(2,1)} %get-tuple-element.92, ...), custom_call_target="tpu_custom_call" | custom-call | tf_op jit(solution)/shard_map/pallas_call | solution.py:1063
  222.4 26.2 %shard_map.257 = (bf16[1024,1536]{1,0:T(8,128)(2,1)}, f32[8,1024]{1,0:T(8,128)}, f32[1024,768]{1,0:T(8,128)}, f32[1024,768]{1,0:T(8,128)}, f32[1024,768]{1,0:T(8...) custom-call(bf16[1024,1536]{1,0:T(8,128)(2,1)} %get-tuple-element.94, ...), custom_call_target="tpu_custom_call" | custom-call | flops 8455716864 | bytes 40000000 | tf_op jit(solution)/shard_map/pallas_call | solution.py:354
  248.6 28.6 %shard_map.258 = (f32[256,1536]{1,0:T(8,128)}, f32[8,1024]{1,0:T(8,128)}) custom-call(bf16[1024,1536]{1,0:T(8,128)(2,1)} %get-tuple-element.100.part, f32[8,1024]{1,0:T(8,128)} %get-tuple-element.101.sq, f32[256,1536]{1,0:T(8,128)} %get-tuple-element.102.state, f32[256,1536]{1,0:T(8,128)} %before.1), custom_call_target="tpu_custom_call" | custom-call | tf_op jit(solution)/shard_map/pallas_call | solution.py:1063
  277.2 0.9 fusion.spread_ref
  278.1 38.4 %shard_map.259 = (bf16[1024,1536]{1,0:T(8,128)(2,1)}, bf16[1024,768]{1,0:T(8,128)(2,1)}, bf16[1024,768]{1,0:T(8,128)(2,1)}, bf16[1024,128]{1,0:T(8,128)(2,1)}, b...) custom-call(bf16[1024,1536]{1,0:T(8,128)(2,1)} %get-tuple-element.104.top_ref, ...), custom_call_target="tpu_custom_call" | custom-call | flops 8455716864 | bytes 40000000 | tf_op jit(solution)/shard_map/pallas_call | solution.py:409
  316.5 5.6 convolution_convert_fusion.5.refs_0_
  322.0 4.0 convolution_convert_fusion.4.refs_1_
  326.0 4.2 convolution_convert_fusion.3.refs_2_
  330.2 1.8 convolution_convert_fusion.9.refs_3_
  332.0 1.9 convolution_convert_fusion.7
  333.9 108.6 %shard_map.260 = (f32[256,1536]{1,0:T(8,128)}, f32[8,1536]{1,0:T(8,128)}, f32[8,1024]{1,0:T(8,128)}, bf16[1024,1536]{1,0:T(8,128)(2,1)}, f32[192,768]{1,0:T(8,12...) custom-call(bf16[1024,1536]{1,0:T(8,128)(2,1)} %get-tuple-element.114.part, ...), custom_call_target="tpu_custom_call" | custom-call | tf_op jit(solution)/shard_map/pallas_call | solution.py:1063
  442.5 37.9 %shard_map.261 = (bf16[1024,1536]{1,0:T(8,128)(2,1)}, bf16[1024,768]{1,0:T(8,128)(2,1)}, bf16[1024,768]{1,0:T(8,128)(2,1)}, bf16[1024,128]{1,0:T(8,128)(2,1)}, b...) custom-call(bf16[1024,1536]{1,0:T(8,128)(2,1)} %get-tuple-element.122.top_ref, ...), custom_call_target="tpu_custom_call" | custom-call | flops 8455716864 | bytes 40000000 | tf_op jit(solution)/shard_map/pallas_call | solution.py:409
  480.5 1.3 convert_element_type.80.state
  481.8 0.6 copy-done.30
  482.4 4.0 convolution_convert_fusion.2.refs_0_
  486.4 4.0 convolution_convert_fusion.1.refs_1_
  490.4 4.2 convolution_convert_fusion.refs_2_
  494.6 1.8 convolution_convert_fusion.8.refs_3_
  496.4 1.9 convolution_convert_fusion.6
  498.3 152.0 %shard_map.262 = (f32[256,1536]{1,0:T(8,128)}, f32[8,1536]{1,0:T(8,128)}, f32[16,768]{1,0:T(8,128)}, f32[16,256]{1,0:T(8,128)}, f32[192,768]{1,0:T(8,128)}, /*in...) custom-call(bf16[1024,1536]{1,0:T(8,128)(2,1)} %get-tuple-element.132.part, ...), custom_call_target="tpu_custom_call" | custom-call | tf_op jit(solution)/shard_map/pallas_call | solution.py:1063
  650.4 2.2 pad_maximum_fusion
  652.7 1.1 pad_maximum_fusion.1
  653.8 0.6 pad_maximum_fusion.3
  654.5 0.7 copy.51
  655.2 2.4 maximum_bitcast_fusion
  657.6 1.4 slice.153
  659.0 0.6 slice.160
  659.7 0.6 slice.161
  660.3 0.6 fusion.11
  660.9 0.7 reduce_sum.9
  661.6 0.6 copy.59
  662.2 1.1 copy.62
  663.3 1.1 copy.63
  (101 shorter events, 1.9 us)
Async XLA Ops:
  0.6 3.7 copy-start.5
  0.7 4.6 copy-start.14
  0.7 5.4 copy-start.13
  4.3 94.3 %copy-start.18 = (f32[2,4,768]{2,1,0:T(4,128)S(1)}, f32[2,4,768]{2,1,0:T(4,128)}, u32[]{:S(2)}) copy-start(f32[2,4,768]{2,1,0:T(4,128)} %param.24) | copy-start | bytes 73732
  4.3 95.0 %copy-start.20 = (f32[2,4,256]{2,1,0:T(4,128)S(1)}, f32[2,4,256]{2,1,0:T(4,128)}, u32[]{:S(2)}) copy-start(f32[2,4,256]{2,1,0:T(4,128)} %param.25) | copy-start | bytes 24580
  4.3 95.5 %copy-start.23 = (f32[2,12]{1,0:T(2,128)S(1)}, f32[2,12]{1,0:T(2,128)}, u32[]{:S(2)}) copy-start(f32[2,12]{1,0:T(2,128)} %param.26) | copy-start | bytes 292
  4.3 95.5 %copy-start.24 = (f32[2,12]{1,0:T(2,128)S(1)}, f32[2,12]{1,0:T(2,128)}, u32[]{:S(2)}) copy-start(f32[2,12]{1,0:T(2,128)} %param.27) | copy-start | bytes 292
  4.4 96.1 %copy-start.21 = (f32[2,768]{1,0:T(2,128)S(1)}, f32[2,768]{1,0:T(2,128)}, u32[]{:S(2)}) copy-start(f32[2,768]{1,0:T(2,128)} %param.29) | copy-start | bytes 18436
  4.4 96.1 %copy-start.25 = (f32[2,12]{1,0:T(2,128)S(1)}, f32[2,12]{1,0:T(2,128)}, u32[]{:S(2)}) copy-start(f32[2,12]{1,0:T(2,128)} %param.28) | copy-start | bytes 292
  4.4 97.1 %copy-start.19 = (s32[1024]{0:T(1024)S(1)}, s32[1024]{0:T(1024)}, u32[]{:S(2)}) copy-start(s32[1024]{0:T(1024)} %param.16) | copy-start | bytes 12292
  278.1 38.4 %copy-start.26 = (bf16[1024,1536]{1,0:T(8,128)(2,1)S(1)}, bf16[1024,1536]{1,0:T(8,128)(2,1)}, u32[]{:S(2)}) copy-start(bf16[1024,1536]{1,0:T(8,128)(2,1)} %get-tuple-element.104.top_ref) | copy-start | bytes 9437188
  316.5 5.6 copy-start.2
  316.5 5.6 copy-start.32
  322.0 4.0 copy-start.31
  326.0 4.2 copy-start.10
  330.2 1.8 copy-start.34
  442.5 38.0 %copy-start = (bf16[256,1536]{1,0:T(8,128)(2,1)S(1)}, bf16[256,1536]{1,0:T(8,128)(2,1)}, u32[]{:S(2)}) copy-start(bf16[256,1536]{1,0:T(8,128)(2,1)} %resid.3) | copy-start | bytes 2359300
  442.5 39.3 %copy-start.27 = (bf16[1024,1536]{1,0:T(8,128)(2,1)S(1)}, bf16[1024,1536]{1,0:T(8,128)(2,1)}, u32[]{:S(2)}) copy-start(bf16[1024,1536]{1,0:T(8,128)(2,1)} %get-tuple-element.122.top_ref) | copy-start | bytes 9437188
  480.4 2.0 copy-start.30
  482.4 4.0 copy-start.1
  482.4 4.0 copy-start.29
  486.4 4.0 copy-start.28
  490.4 4.3 copy-start.9
  494.6 1.8 copy-start.33
  498.3 152.0 %copy-start.7 = (f32[192,768]{1,0:T(8,128)S(1)}, f32[192,768]{1,0:T(8,128)}, u32[]{:S(2)}) copy-start(f32[192,768]{1,0:T(8,128)} %get-tuple-element.146) | copy-start | bytes 1769476
  650.3 2.3 copy-start.6
  650.4 2.3 copy-start.8
  650.4 3.4 copy-start.15
  650.4 3.4 copy-start.16
  650.4 4.0 copy-start.11
  650.4 4.0 copy-start.12
  652.7 6.4 copy-start.17
  652.7 7.0 %copy-start.22 = (f32[16,256]{1,0:T(8,128)S(1)}, f32[16,256]{1,0:T(8,128)}, u32[]{:S(2)}) copy-start(f32[16,256]{1,0:T(8,128)} %get-tuple-element.157) | copy-start | bytes 49156
  652.7 9.5 %copy-start.3 = (f32[256,1536]{1,0:T(8,128)S(1)}, f32[256,1536]{1,0:T(8,128)}, u32[]{:S(2)}) copy-start(f32[256,1536]{1,0:T(8,128)} %get-tuple-element.262) | copy-start | bytes 4718596
  655.2 8.2 %copy-start.4 = (f32[256,1536]{1,0:T(8,128)S(1)}, f32[256,1536]{1,0:T(8,128)}, u32[]{:S(2)}) copy-start(f32[256,1536]{1,0:T(8,128)} %get-tuple-element.263) | copy-start | bytes 4718596

commit v3 on v2

--- a/solution.py
+++ b/solution.py
@@ -91,8 +91,10 @@
     ext_bc,
     state,
     gg_ref,
+    hook=None,
 ):
     inner = wx_ref.shape[1]
+    hook = hook or (lambda slot: None)
 
     @pl.when(pl.program_id(0) == 0)
     def _():
@@ -100,6 +102,7 @@
         ext_x[0:8, :] = jnp.zeros((8, inner), F32)
         ext_bc[0:8, :] = jnp.zeros((8, 2 * N), F32)
 
+    hook(0)
     rows = rows_ref[...]
     aux = aux_ref[...]
     rate = heads_ref[1:2, :]
@@ -129,6 +132,7 @@
     cum_t = jnp.transpose(cum)
     ext_x[8 : 8 + CHUNK, :] = mm(rows, wx_ref[...])
     gate_ref[...] = mm(rows, wz_ref[...])
+    hook(1)
     squares = jnp.zeros((CHUNK, LANES), F32)
     half = iota2((CHUNK, LANES), 1) < P_SIZE
     for pair in range(inner // LANES):
@@ -161,6 +165,7 @@
         gated = (mixed + wide_ref[0:1, cols] * act) * (gate * sigmoid(gate))
         squares = squares + gated * gated
         gg_ref[:, cols] = (gated * wide_ref[1:2, cols]).astype(BF16)
+        hook(2 + pair)
     total = jnp.sum(squares, axis=1, keepdims=True)
     sq_ref[...] = jnp.transpose(jnp.broadcast_to(total, (CHUNK, LANES)))[0:8, :]
     part_ref[...] = mm_nt(gg_ref[...], wout_ref[...]).astype(BF16)
@@ -344,50 +349,68 @@
 VMEM_LIMIT = 60 * 1024 * 1024
 
 
+def block_rows(cols):
+    return pl.BlockSpec((CHUNK, cols), lambda i: (i, 0))
+
+
+def forward_in_specs(rows_all, weights, layer_args):
+    return (
+        [block_rows(rows_all.shape[1])]
+        + [whole_spec(w.shape) for w in weights]
+        + [whole_spec(w.shape) for w in layer_args]
+        + [block_rows(LANES), pl.BlockSpec((8, CHUNK), lambda i: (0, i))]
+    )
+
+
+def saved_specs(inner):
+    return [
+        block_rows(inner),
+        block_rows(inner),
+        block_rows(inner),
+        block_rows(2 * N),
+        block_rows(2 * N),
+        block_rows(LANES),
+        block_rows(inner),
+        pl.BlockSpec((1, N, inner), lambda i: (i, 0, 0)),
+    ]
+
+
+def saved_shapes(length, inner):
+    shape = jax.ShapeDtypeStruct
+    return [
+        shape((length, inner), F32),
+        shape((length, inner), F32),
+        shape((length, inner), F32),
+        shape((length, 2 * N), F32),
+        shape((length, 2 * N), F32),
+        shape((length, LANES), F32),
+        shape((length, inner), F32),
+        shape((length // CHUNK, N, inner), F32),
+    ]
+
+
+def forward_scratch(inner):
+    return [
+        pltpu.VMEM((CHUNK + 8, inner), F32),
+        pltpu.VMEM((CHUNK + 8, 2 * N), F32),
+        pltpu.VMEM((N, inner), F32),
+        pltpu.VMEM((CHUNK, inner), BF16),
+    ]
+
+
 def forward_layer(rows_all, weights, layer_args, aux, segrow):
     length, width = rows_all.shape
-    chunks = length // CHUNK
     inner = weights[1].shape[1]
-    by_rows = lambda cols: pl.BlockSpec((CHUNK, cols), lambda i: (i, 0))
-    by_lanes = pl.BlockSpec((8, CHUNK), lambda i: (0, i))
     shape = jax.ShapeDtypeStruct
     return pl.pallas_call(
         forward_kernel,
-        grid=(chunks,),
-        in_specs=[by_rows(width)]
-        + [whole_spec(w.shape) for w in weights]
-        + [whole_spec(w.shape) for w in layer_args]
-        + [by_rows(LANES), by_lanes],
-        out_specs=[
-            by_rows(width),
-            by_lanes,
-            by_rows(inner),
-            by_rows(inner),
-            by_rows(inner),
-            by_rows(2 * N),
-            by_rows(2 * N),
-            by_rows(LANES),
-            by_rows(inner),
-            pl.BlockSpec((1, N, inner), lambda i: (i, 0, 0)),
-        ],
-        out_shape=[
-            shape((length, width), BF16),
-            shape((8, length), F32),
-            shape((length, inner), F32),
-            shape((length, inner), F32),
-            shape((length, inner), F32),
-            shape((length, 2 * N), F32),
-            shape((length, 2 * N), F32),
-            shape((length, LANES), F32),
-            shape((length, inner), F32),
-            shape((chunks, N, inner), F32),
-        ],
-        scratch_shapes=[
-            pltpu.VMEM((CHUNK + 8, inner), F32),
-            pltpu.VMEM((CHUNK + 8, 2 * N), F32),
-            pltpu.VMEM((N, inner), F32),
-            pltpu.VMEM((CHUNK, inner), BF16),
-        ],
+        grid=(length // CHUNK,),
+        in_specs=forward_in_specs(rows_all, weights, layer_args),
+        out_specs=[block_rows(width), pl.BlockSpec((8, CHUNK), lambda i: (0, i))]
+        + saved_specs(inner),
+        out_shape=[shape((length, width), BF16), shape((8, length), F32)]
+        + saved_shapes(length, inner),
+        scratch_shapes=forward_scratch(inner),
         compiler_params=pltpu.CompilerParams(
             dimension_semantics=("arbitrary",), vmem_limit_bytes=VMEM_LIMIT
         ),
@@ -526,6 +549,8 @@
 PIECES = 4
 TENSOR = 4
 LATE = 1e9
+BIG = 6.5
+SMALL = 1.1
 
 
 class Place:
@@ -580,9 +605,40 @@
     def add(self, when, step):
         self.steps.append((when, len(self.steps), step))
 
+    def ordered(self):
+        return sorted(self.steps, key=lambda entry: entry[:2])
+
     def run(self):
-        for _, _, step in sorted(self.steps, key=lambda entry: entry[:2]):
+        for _, _, step in self.ordered():
             step()
+
+    def spread(self, chunks, slots, chunk_us):
+        places = {}
+        after = []
+        for when, _, step in self.ordered():
+            spot = max(0, int(when / chunk_us * slots))
+            if spot < chunks * slots:
+                places.setdefault((spot % slots, spot // slots), []).append(step)
+            else:
+                after.append(step)
+
+        def hook(slot):
+            for chunk in range(chunks):
+                steps = places.get((slot, chunk))
+                if steps:
+
+                    @pl.when(pl.program_id(0) == chunk)
+                    def _(steps=steps):
+                        for step in steps:
+                            step()
+
+        def end():
+            @pl.when(pl.program_id(0) == chunks - 1)
+            def _():
+                for step in after:
+                    step()
+
+        return hook, end
 
 
 def remote(src, dst, send, recv, device):
@@ -714,7 +770,7 @@
 
 
 def scatter_semaphores(count, line):
-    return [pltpu.SemaphoreType.DMA((count, line))] * 6
+    return [pltpu.SemaphoreType.DMA((count, 2, line))] * 6
 
 
 def add_into(target, other, rows):
@@ -740,96 +796,146 @@
     line = place.line
     z = place.z
 
+    def rows_of(i):
+        return items[i][1][0].shape[1]
+
     def side(i, zz):
         piece, (land_x, _, _), *_ = items[i]
         return remote(
-            piece(zz, place.other), land_x.at[zz], send_x.at[i, zz], recv_x.at[i, zz], place.across
+            piece(zz, place.other), land_x.at[zz], send_x.at[i, 0, zz], recv_x.at[i, 0, zz], place.across
         )
 
-    def along(i, zz, way, source=None):
+    def land_along(i, zz, way, xs):
         land = items[i][1][1 + way]
+        return land.at[zz, xs] if items[i][3] == "zx" else land.at[zz]
+
+    def along(i, zz, way, xs, source=None):
+        land = land_along(i, zz, way, xs)
         return remote(
-            land.at[zz] if source is None else source,
-            land.at[zz],
-            (send_r, send_l)[way].at[i, zz],
-            (recv_r, recv_l)[way].at[i, zz],
+            land if source is None else source,
+            land,
+            (send_r, send_l)[way].at[i, xs, zz],
+            (recv_r, recv_l)[way].at[i, xs, zz],
             (place.right, place.left)[way],
         )
 
-    def begin(i, zz):
-        return lambda: side(i, zz).start()
+    def own(i, zz, xs):
+        return items[i][0](zz, xs) if items[i][3] == "zx" else items[i][1][0].at[zz]
 
     def join(i, zz):
         def step():
             side(i, zz).wait_recv()
-            land = items[i][1][0]
-            add_into(land.at[zz], items[i][0](zz, place.x), land.shape[1])
+            add_into(items[i][1][0].at[zz], items[i][0](zz, place.x), rows_of(i))
 
         return step
 
-    def send(i, zz, way, h):
-        land = items[i][1]
+    def send(i, zz, way, xs, h):
         if way == 0:
-            mine, first = (z == h) & (z < zz), h == 0
+            mine = (z == h) & (z < zz)
         else:
-            mine, first = (z == line - 1 - h) & (z > zz), h == 0
+            mine = (z == line - 1 - h) & (z > zz)
 
         def step():
             @pl.when(mine)
             def _():
-                if first:
-                    along(i, zz, way, land[0].at[zz]).start()
+                if h == 0:
+                    along(i, zz, way, xs, own(i, zz, xs)).start()
                 else:
-                    along(i, zz, way).wait_recv()
-                    add_into(land[1 + way].at[zz], land[0].at[zz], land[0].shape[1])
-                    along(i, zz, way).start()
+                    along(i, zz, way, xs).wait_recv()
+                    add_into(land_along(i, zz, way, xs), own(i, zz, xs), rows_of(i))
+                    along(i, zz, way, xs).start()
 
         return step
 
     def last(i):
-        _, (land_x, land_r, land_l), out, *_ = items[i]
+        out = items[i][2]
 
         def step():
-            out[...] = land_x[z].astype(F32)
+            out[...] = items[i][1][0][z].astype(F32)
+            for way, there in ((0, z > 0), (1, z < line - 1)):
+
+                @pl.when(there)
+                def _(way=way):
+                    along(i, z, way, 0).wait_recv()
+                    out[...] += items[i][1][1 + way][z].astype(F32)
+
+        return step
+
+    def swap(i):
+        piece, (land_x, land_r, _), *_ = items[i]
+        stage = land_r.at[z, place.other]
+        return remote(stage, land_x.at[0], send_x.at[i, 0, 0], recv_x.at[i, 0, 0], place.across)
+
+    def gather_line(i, xs):
+        piece = items[i][0]
+
+        def step():
+            right, left = land_along(i, z, 0, xs), land_along(i, z, 1, xs)
 
             @pl.when(z > 0)
             def _():
-                along(i, z, 0).wait_recv()
-                out[...] += land_r[z].astype(F32)
+                along(i, z, 0, xs).wait_recv()
+                add_into(right, piece(z, xs), rows_of(i))
+
+            @pl.when(z == 0)
+            def _():
+                right[...] = piece(z, xs)[...]
 
             @pl.when(z < line - 1)
             def _():
-                along(i, z, 1).wait_recv()
-                out[...] += land_l[z].astype(F32)
+                along(i, z, 1, xs).wait_recv()
+                add_into(right, left, rows_of(i))
 
         return step
 
-    def end(i, zz):
+    def swap_end(i):
+        piece, (land_x, land_r, _), out, *_ = items[i]
+
         def step():
-            side(i, zz).wait_send()
-
-            @pl.when(z < zz)
-            def _():
-                along(i, zz, 0).wait_send()
-
-            @pl.when(z > zz)
-            def _():
-                along(i, zz, 1).wait_send()
+            swap(i).wait()
+            out[...] = land_r[z, place.x].astype(F32) + land_x[0].astype(F32)
 
         return step
 
+    def end(i, zz, xs):
+        def step():
+            if items[i][3] == "xz":
+                side(i, zz).wait_send()
+            for way, there in ((0, z < zz), (1, z > zz)):
+
+                @pl.when(there)
+                def _(way=way):
+                    along(i, zz, way, xs).wait_send()
+
+        return step
+
     now = 0.0
-    for i, (_, _, _, cost, ready) in enumerate(items):
+    for i, (_, _, _, route, cost, ready) in enumerate(items):
+        if route == "zx":
+            then = ready
+            for zz in scatter_order(line):
+                for xs in (0, 1):
+                    for way in (0, 1):
+                        for h in range(zz if way == 0 else line - 1 - zz):
+                            timeline.add(then + h * cost + 0.2, send(i, zz, way, xs, h))
+                    timeline.add(LATE, end(i, zz, xs))
+                    then += cost
+            then += line * cost / 2
+            for xs in (0, 1):
+                timeline.add(then, gather_line(i, xs))
+            timeline.add(then + 0.1, lambda i=i: swap(i).start())
+            timeline.add(LATE - 1, swap_end(i))
+            continue
         now = max(now, ready)
         for zz in scatter_order(line):
+            timeline.add(max(ready, now - 2 * BIG), lambda i=i, zz=zz: side(i, zz).start())
             now += cost
-            timeline.add(ready, begin(i, zz))
             timeline.add(now, join(i, zz))
             for way in (0, 1):
                 hops = zz if way == 0 else line - 1 - zz
                 for h in range(hops):
-                    timeline.add(now + 0.01 + h * cost, send(i, zz, way, h))
-            timeline.add(LATE, end(i, zz))
+                    timeline.add(now + 0.01 + h * cost, send(i, zz, way, 0, h))
+            timeline.add(LATE, end(i, zz, 0))
         timeline.add(now + line * cost, last(i))
 
 
@@ -961,17 +1067,15 @@
     ]
 
 
-BIG = 6.5
-SMALL = 1.1
-
-
 def row_norm(state):
     return lax.rsqrt(jnp.mean(state * state, axis=1, keepdims=True) + epsilon)
 
 
-def by_rows_piece(whole, rows):
+def by_rows_piece(whole, rows, start=0, count=None):
+    count = rows if count is None else count
+
     def piece(zz, xs):
-        return whole.at[pl.ds(pl.multiple_of((zz * 2 + xs) * rows, rows), rows), :]
+        return whole.at[pl.ds(pl.multiple_of((zz * 2 + xs) * rows, rows) + start, count), :]
 
     return piece
 
@@ -985,7 +1089,9 @@
 
 def weight_gather(place, timeline, refs, wholes, sems, share_sems, own_sems):
     bc_own, bc_all = refs[4], wholes[4]
-    pieces = [by_rows_piece(whole, ref.shape[0]) for ref, whole in zip(refs[:4], wholes[:4])]
+    rows = refs[0].shape[0]
+    half = rows // 2
+    pieces = [by_rows_piece(whole, rows) for whole in wholes[:4]]
 
     def bc_piece(zz, xs):
         return bc_all.at[zz * 2 + xs, place.t]
@@ -996,7 +1102,8 @@
         (refs[3], pieces[3], "zx", SMALL, LATE),
         (refs[1], pieces[1], "zx", BIG, LATE),
         (refs[0], pieces[0], "zx", BIG, LATE),
-        (refs[2], pieces[2], "zx", BIG, LATE),
+        (refs[2].at[pl.ds(0, half), :], by_rows_piece(wholes[2], rows, 0, half), "xz", BIG / 2, LATE),
+        (refs[2].at[pl.ds(half, half), :], by_rows_piece(wholes[2], rows, half, half), "zx", BIG / 2, LATE),
     ]
     copies = own_copies(place, [(item[0], item[1]) for item in items], own_sems)
     shares = share_blocks(
@@ -1022,7 +1129,7 @@
 
 
 def gather_scratch(line):
-    return gather_semaphores(5, line) + share_semaphores() + [pltpu.SemaphoreType.DMA((5,))]
+    return gather_semaphores(6, line) + share_semaphores() + [pltpu.SemaphoreType.DMA((6,))]
 
 
 def start_kernel(line, resid, cotangent, gain, *refs):
@@ -1059,9 +1166,10 @@
     timeline.run()
 
 
-def call_kernel(kernel, outs, in_specs, out_specs, scratch, number, args):
+def call_kernel(kernel, outs, in_specs, out_specs, scratch, number, args, grid=()):
     return pl.pallas_call(
         kernel,
+        grid=grid,
         out_shape=outs,
         in_specs=in_specs,
         out_specs=out_specs,
@@ -1093,7 +1201,7 @@
     )
 
 
-def scale_steps(place, timeline, sq, land, scale_row, scale_col, sems, inner_all):
+def scale_steps(place, timeline, sq, land, scale_row, scale_col, sems, inner_all, start=0.0):
     rows = scale_col.shape[0]
 
     def at(owner):
@@ -1109,26 +1217,36 @@
         scale_row[...] = scale
         scale_col[...] = jnp.transpose(scale)
 
-    timeline.add(-0.5, lambda: [copy.start() for copy in copies] and None)
-    timeline.add(1.5, arrive)
+    timeline.add(start - 0.5, lambda: [copy.start() for copy in copies] and None)
+    timeline.add(start + 1.5, arrive)
 
 
 RATE_SHARED = 8.8
 RATE = 4.4
 
 
-def middle_kernel(line, inner_all, part, sq, resid, gain, *refs):
-    own, refs = refs[:5], refs[5:]
+SLOTS = 8
+FORWARD_US = 6.7
+
+
+def middle_kernel(line, inner_all, *refs):
+    work, refs = refs[:12], refs[12:]
+    (resid, gain), own, refs = refs[:2], refs[2:7], refs[7:]
+    saved, refs = refs[:8], refs[8:]
     state_out, raw_out, scale_row, rows_all, refs = *refs[:4], refs[4:]
     wholes, refs = refs[:5], refs[5:]
-    far, near, mate, land, scale_col, normed = refs[:6]
-    refs = refs[6:]
+    scratch, refs = refs[:4], refs[4:]
+    part, sq, far, near, mate, land, scale_col, normed = refs[:8]
+    refs = refs[8:]
     sems, share_sems, own_sems = refs[:5], refs[5:7], refs[7]
     reduce_sems, sq_sems, rows_sems, local = refs[8:14], refs[14:16], refs[16:22], refs[22]
+    chunk = pl.program_id(0)
+    chunks = part.shape[0] // CHUNK
     place = Place(line)
-    place.greet()
+    pl.when(chunk == 0)(place.greet)
     timeline = Timeline()
-    scale_steps(place, timeline, sq, land, scale_row, scale_col, sq_sems, inner_all)
+    done = FORWARD_US * chunks + 1.0
+    scale_steps(place, timeline, sq, land, scale_row, scale_col, sq_sems, inner_all, done)
     rows = normed.shape[0]
     step = rows // PIECES
     begin, forward, finish = spread_rows(place, normed, rows_all, rows_sems)
@@ -1141,40 +1259,57 @@
         normed[part_rows, :] = (state * row_norm(state) * gain[...]).astype(BF16)
         begin(p)
 
-    reduce_rows(place, timeline, part, (far, near, mate), reduce_sems, owner, RATE)
+    reduce_rows(place, timeline, part, (far, near, mate), reduce_sems, owner, RATE, done)
     weight_gather(place, timeline, own, wholes, sems, share_sems, own_sems)
     for p in range(PIECES):
-        timeline.add(3.0 + RATE * (PIECES + 1 + p), functools.partial(forward, p))
+        timeline.add(done + 3.0 + RATE * (PIECES + 1 + p), functools.partial(forward, p))
     block = pl.ds(pl.multiple_of(place.t * rows, rows), rows)
     keep = pltpu.make_async_copy(normed, rows_all.at[block, :], local.at[0])
-    timeline.add(3.0 + RATE * PIECES, keep.start)
+    timeline.add(done + 3.0 + RATE * PIECES, keep.start)
     timeline.add(LATE, keep.wait)
     timeline.add(LATE, finish)
-    timeline.run()
-
-
-def middle_layer(line, inner_all, part, sq, resid, gain, own):
+    hook, end = timeline.spread(chunks, SLOTS, FORWARD_US)
+    at = pl.multiple_of(chunk * CHUNK, CHUNK)
+    forward_kernel(
+        *work, part.at[pl.ds(at, CHUNK), :], sq.at[:, pl.ds(at, CHUNK)], *saved, *scratch, hook=hook
+    )
+    end()
+
+
+def middle_layer(line, inner_all, rows_all, weights, layer_args, aux, segrow, resid, gain, own):
     rows, width = resid.shape
+    length = rows_all.shape[0]
     inner = own[0].shape[1]
     shape = jax.ShapeDtypeStruct
-    outs = [
-        shape((rows, width), F32),
-        shape((rows, width), F32),
-        shape((8, rows), F32),
-        shape((rows * TENSOR, width), BF16),
-    ] + gather_outputs(line, width, inner, 2 * line)
-    scratch = [pltpu.VMEM((rows, width), BF16)] * 3
+    outs = (
+        saved_shapes(length, inner)
+        + [
+            shape((rows, width), F32),
+            shape((rows, width), F32),
+            shape((8, rows), F32),
+            shape((length, width), BF16),
+        ]
+        + gather_outputs(line, width, inner, 2 * line)
+    )
+    scratch = forward_scratch(inner)
+    scratch += [pltpu.VMEM((length, width), BF16), pltpu.VMEM((8, length), F32)]
+    scratch += [pltpu.VMEM((rows, width), BF16)] * 3
     scratch += [pltpu.VMEM((3, 8, rows), F32), pltpu.VMEM((rows, 8), F32), pltpu.VMEM((rows, width), BF16)]
     scratch += gather_scratch(line) + reduce_semaphores() + share_semaphores() + spread_semaphores()
     scratch += [pltpu.SemaphoreType.DMA((1,))]
     return call_kernel(
         functools.partial(middle_kernel, line, inner_all),
         outs,
-        [IN_VMEM] * 4 + [ANY] * 5,
-        [IN_VMEM] * 3 + [ANY] * 6,
+        forward_in_specs(rows_all, weights, layer_args)
+        + [whole_spec(resid.shape), whole_spec(gain.shape)]
+        + [ANY] * 5,
+        saved_specs(inner)
+        + [whole_spec((rows, width)), whole_spec((rows, width)), whole_spec((8, rows))]
+        + [ANY] * 6,
         scratch,
         1,
-        (part, sq, resid, gain, *own),
+        (rows_all, *weights, *layer_args, aux, segrow, resid, gain, *own),
+        (length // CHUNK,),
     )
 
 
@@ -1269,12 +1404,17 @@
 
     timeline.add(-1.0, lambda: [copy.start() for copy in shares] and None)
     timeline.add(bc_ready, bc_add)
-    items = []
-    for n in range(4):
-        rows = lands[3 * n].shape[1]
-        cost = BIG if n < 3 else SMALL
-        items.append((by_rows_piece(grads[n], rows), lands[3 * n : 3 * n + 3], outs[n], cost, 0.0))
-    items.append((lambda zz, xs: bc_sum.at[zz * 2 + xs], lands[12:15], outs[4], SMALL / 2, bc_ready + 0.1))
+    rows = outs[0].shape[0]
+    half = rows // 2
+    first, second = pl.ds(0, half), pl.ds(half, half)
+    items = [
+        (by_rows_piece(grads[0], rows, 0, half), lands[15:18], outs[0].at[first, :], "zx", BIG / 2, 0.0),
+        (by_rows_piece(grads[0], rows, half, half), lands[0:3], outs[0].at[second, :], "xz", BIG / 2, 0.0),
+        (by_rows_piece(grads[1], rows), lands[3:6], outs[1], "xz", BIG, 0.0),
+        (by_rows_piece(grads[2], rows), lands[6:9], outs[2], "xz", BIG, 0.0),
+        (by_rows_piece(grads[3], rows), lands[9:12], outs[3], "xz", SMALL, 0.0),
+        (lambda zz, xs: bc_sum.at[zz * 2 + xs], lands[12:15], outs[4], "xz", SMALL / 2, bc_ready + 0.1),
+    ]
     scatter_weights(place, timeline, items, sems)
 
 
@@ -1290,14 +1430,17 @@
 def scatter_scratch(line, width, inner):
     dp = 2 * line
     rows = width // dp
-    scratch = [pltpu.VMEM((line, rows, inner), BF16)] * 9
+    scratch = [pltpu.VMEM((line, rows // 2, inner), BF16)] * 3
+    scratch += [pltpu.VMEM((line, rows, inner), BF16)] * 6
     scratch += [pltpu.VMEM((line, rows, LANES), BF16)] * 3
     scratch += [pltpu.VMEM((line, rows // TENSOR, 2 * N), BF16)] * 3
+    scratch += [pltpu.VMEM((1, rows // 2, inner), BF16)]
+    scratch += [pltpu.VMEM((line, 2, rows // 2, inner), BF16)] * 2
     scratch += [
         pltpu.VMEM((3, dp, rows // TENSOR, 2 * N), BF16),
         pltpu.VMEM((dp, rows // TENSOR, 2 * N), BF16),
     ]
-    return scratch + scatter_semaphores(5, line) + share_semaphores()
+    return scratch + scatter_semaphores(6, line) + share_semaphores()
 
 
 def input_gradient(state, gain, before, sums):
@@ -1314,8 +1457,8 @@
     outs, refs = refs[:5], refs[5:]
     far, near, mate, row_land, cross_col, stage, low = refs[:7]
     refs = refs[7:]
-    lands, bc_land, bc_sum, sems, share_sems = refs[:15], refs[15], refs[16], refs[17:23], refs[23:25]
-    refs = refs[25:]
+    lands, bc_land, bc_sum, sems, share_sems = refs[:18], refs[18], refs[19], refs[20:26], refs[26:28]
+    refs = refs[28:]
     reduce_sems, row_sems, top_sems, local = refs[:6], refs[6:8], refs[8:14], refs[14]
     place = Place(line)
     place.greet()
@@ -1389,10 +1532,10 @@
     grad_out, norm_sum, small_sum, bc_sums, refs = *refs[:4], refs[4:]
     outs, refs = refs[:5], refs[5:]
     far, near, mate = refs[:3]
-    lands, bc_land, bc_sum, sems, share_sems = refs[3:18], refs[18], refs[19], refs[20:26], refs[26:28]
-    refs = refs[28:]
+    lands, bc_land, bc_sum, sems, share_sems = refs[3:21], refs[21], refs[22], refs[23:29], refs[29:31]
+    refs = refs[31:]
     reduce_sems, refs = refs[:6], refs[6:]
-    small_land, bc_land_sums, norm_land, small_send, small_recv = refs
+    small_land, bc_land_sums, top_land, norm_land, norm_top, small_send, small_recv = refs
     dp = 2 * line
     bits = [1 << n for n in range(dp.bit_length() - 1)]
     place = Place(line)
@@ -1400,7 +1543,7 @@
     timeline = Timeline()
     step = state.shape[0] // PIECES
     norm_sum[...] = jnp.zeros_like(norm_sum)
-    norm_sum[1:2, :] = gnorm_top[0:1, :]
+    norm_top[...] = gnorm_top[...]
     small_sum[0:8, :] = small_a[...]
     small_sum[8:16, :] = small_b[...]
     bc_sums[0:8, :] = bc_a[...]
@@ -1416,28 +1559,41 @@
 
     reduce_rows(place, timeline, part, (far, near, mate), reduce_sems, owner, RATE)
     weight_scatter(place, timeline, grads, outs, lands, sems, bc_land, bc_sum, share_sems)
-    partners = [place.partner(bit) for bit in bits]
-    partners += [(place.dp, place.sibling), (place.dp, place.mate)]
-    for n, partner in enumerate(partners):
-        trio = [(bc_sums, bc_land_sums), (norm_sum, norm_land)]
-        if n < len(bits):
-            trio.append((small_sum, small_land))
+    along = [place.partner(bit) for bit in bits]
+    across = [(place.dp, place.sibling), (place.dp, place.mate)]
+
+    def exchange(n, partner, group, start, end):
         copies = [
             remote(own, land.at[n], small_send.at[n, m], small_recv.at[n, m], partner)
-            for m, (own, land) in enumerate(trio)
+            for m, own, land in group
         ]
 
-        def send(copies=copies):
+        def send():
             for copy in copies:
                 copy.start()
 
-        def take(copies=copies, trio=trio, n=n):
-            for copy, (own, land) in zip(copies, trio):
+        def take():
+            for copy, (_, own, land) in zip(copies, group):
                 copy.wait()
                 own[...] += land[n]
 
-        timeline.add(25.0 + 10.0 * n, send)
-        timeline.add(34.9 + 10.0 * n, take)
+        timeline.add(start, send)
+        timeline.add(end, take)
+
+    early = -1.5
+    for n, partner in enumerate(along + across):
+        group = [(0, bc_sums, bc_land_sums), (1, norm_top, top_land)]
+        if n < len(bits):
+            group.append((2, small_sum, small_land))
+        later = 3.0 if n == 0 else early + 5.0
+        exchange(n, partner, group, early, later)
+        early = later + 0.01
+    late = 4.0 + RATE * PIECES
+    for n, partner in list(enumerate(along + across))[::-1]:
+        later = late + (3.5 if n >= len(bits) else 16.0)
+        exchange(n, partner, [(3, norm_sum, norm_land)], late, later)
+        late = later + 0.01
+    timeline.add(LATE + 1, lambda: norm_sum.__setitem__((slice(1, 2), slice(None)), norm_top[0:1, :]))
     timeline.run()
 
 
@@ -1459,8 +1615,10 @@
         pltpu.VMEM((steps, 16, inner), F32),
         pltpu.VMEM((steps + 2, 16, 2 * N), F32),
         pltpu.VMEM((steps + 2, 8, width), F32),
-        pltpu.SemaphoreType.DMA((steps + 2, 3)),
-        pltpu.SemaphoreType.DMA((steps + 2, 3)),
+        pltpu.VMEM((steps + 2, 8, width), F32),
+        pltpu.VMEM((8, width), F32),
+        pltpu.SemaphoreType.DMA((steps + 2, 4)),
+        pltpu.SemaphoreType.DMA((steps + 2, 4)),
     ]
     return call_kernel(
         functools.partial(end_kernel, line),
@@ -1527,10 +1685,11 @@
 
     *gathered, rows_low, top_high = start_layer(line, resid, cotangent, gains[0], own[0])
     weights_low = arranged(gathered)
-    part, sq, *saved_low = forward_layer(rows_low, weights_low, args[0], aux, segrow)
-    state, raw, scale_row, rows_high, *gathered = middle_layer(
-        line, inner_all, part, sq, resid, gains[1], own[1]
-    )
+    results = middle_layer(
+        line, inner_all, rows_low, weights_low, args[0], aux, segrow, resid, gains[1], own[1]
+    )
+    saved_low = results[:8]
+    state, raw, scale_row, rows_high, *gathered = results[8:]
     weights_high = arranged(gathered)
     part, sq, *saved_high = forward_layer(rows_high, weights_high, args[1], aux, segrow)
     hidden, per_row = top_layer(line, inner_all, part, sq, state, cotangent)

time: 672 us -> 606 us (0.902)
  Pallas kernels: 601 us -> 532 us
    pallas_call x7 -> x6, Pallas kernels: 525 us -> 456 us  [the longest x5 429 us: call_kernel(): pl.pallas_call(kernel, grid=grid, out_shape=outs, in_specs=in_specs, out_...]
where the time goes in v3:
time: 606 us; the launch traced here: 596 us
  Pallas kernels  532 us (88%)
  matrix products  33.4 us (6%)
  local copies, waits for them, and re-layouts  18.3 us (3%)
  other arithmetic  10.7 us (2%)
    pallas_call x5, Pallas kernels, call_kernel(): pl.pallas_call(kernel, grid=grid, out_shape=outs, in_specs=in_specs, out_...  429 us
    pallas_call x2, Pallas kernels, backward_layer(): pl.pallas_call(backward_kernel, grid=(chunks,), in_specs=[by_rows(width),...  76.1 us
    dot_general x10, matrix products, contract(): lax.dot_general(left, right, (((0,), (0,)), ((), ())), preferred_element_...  33.4 us
    pallas_call x1, Pallas kernels, forward_layer(): pl.pallas_call(forward_kernel, grid=(length // CHUNK,), in_specs=forward_...  26.6 us

profile of v3, /device:TPU:0, one launch (start us, length us, event | category | flops | bytes accessed | tf_op | source)
XLA Modules:
  0.0 595.7 jit_solution(12070311150487220936)
XLA Ops:
  0.7 1.4 fusion.13
  2.1 2.3 slice_bitcast_fusion.1
  4.4 0.9 slice_bitcast_fusion
  5.4 0.6 pad.22.refs_3_
  6.1 0.6 slice_bitcast_fusion.6
  6.7 86.9 %shard_map.254 = (bf16[1536,768]{1,0:T(8,128)(2,1)}, bf16[1536,768]{1,0:T(8,128)(2,1)}, bf16[1536,768]{1,0:T(8,128)(2,1)}, bf16[1536,128]{1,0:T(8,128)(2,1)}, bf...) custom-call(bf16[256,1536]{1,0:T(8,128)(2,1)} %refs_12_.1, ...), custom_call_target="tpu_custom_call" | custom-call | tf_op jit(solution)/shard_map/pallas_call | solution.py:1170
  93.6 0.6 slice_bitcast_fusion.8
  94.2 0.6 slice_bitcast_fusion.10
  94.8 0.6 select_maximum_fusion
  95.7 0.6 pad_maximum_fusion.4
  97.1 0.2 stack.133
  97.4 0.2 copy.48
  97.6 0.8 pad.24.refs_10_.aux_ref
  98.4 0.6 broadcast_in_dim.26.refs_11_.segrow_ref
  99.1 0.6 pad.25.refs_17_
  99.8 96.6 %shard_map.255 = (f32[1024,768]{1,0:T(8,128)}, f32[1024,768]{1,0:T(8,128)}, f32[1024,768]{1,0:T(8,128)}, f32[1024,256]{1,0:T(8,128)}, f32[1024,256]{1,0:T(8,128)...) custom-call(bf16[1024,1536]{1,0:T(8,128)(2,1)} %get-tuple-element.84, ...), custom_call_target="tpu_custom_call" | custom-call | tf_op jit(solution)/shard_map/pallas_call | solution.py:1170
  196.4 26.6 %shard_map.256 = (bf16[1024,1536]{1,0:T(8,128)(2,1)}, f32[8,1024]{1,0:T(8,128)}, f32[1024,768]{1,0:T(8,128)}, f32[1024,768]{1,0:T(8,128)}, f32[1024,768]{1,0:T(8...) custom-call(bf16[1024,1536]{1,0:T(8,128)(2,1)} %get-tuple-element.90, ...), custom_call_target="tpu_custom_call" | custom-call | flops 8455716864 | bytes 40000000 | tf_op jit(solution)/shard_map/pallas_call | solution.py:405
  223.0 29.8 %shard_map.257 = (f32[256,1536]{1,0:T(8,128)}, f32[8,1024]{1,0:T(8,128)}) custom-call(bf16[1024,1536]{1,0:T(8,128)(2,1)} %get-tuple-element.96.part, f32[8,1024]{1,0:T(8,128)} %get-tuple-element.97.sq, f32[256,1536]{1,0:T(8,128)} %get-tuple-element.98.state, f32[256,1536]{1,0:T(8,128)} %before.1), custom_call_target="tpu_custom_call" | custom-call | tf_op jit(solution)/shard_map/pallas_call | solution.py:1170
  252.8 0.8 fusion.spread_ref
  253.6 37.9 %shard_map.258 = (bf16[1024,1536]{1,0:T(8,128)(2,1)}, bf16[1024,768]{1,0:T(8,128)(2,1)}, bf16[1024,768]{1,0:T(8,128)(2,1)}, bf16[1024,128]{1,0:T(8,128)(2,1)}, b...) custom-call(bf16[1024,1536]{1,0:T(8,128)(2,1)} %get-tuple-element.100.top_ref, ...), custom_call_target="tpu_custom_call" | custom-call | flops 8455716864 | bytes 40000000 | tf_op jit(solution)/shard_map/pallas_call | solution.py:432
  291.6 5.6 convolution_convert_fusion.5.refs_0_
  297.1 4.0 convolution_convert_fusion.4.refs_1_
  301.1 4.2 convolution_convert_fusion.3.refs_2_
  305.3 1.8 convolution_convert_fusion.9.refs_3_
  307.1 1.9 convolution_convert_fusion.7
  309.0 106.3 %shard_map.259 = (f32[256,1536]{1,0:T(8,128)}, f32[8,1536]{1,0:T(8,128)}, f32[8,1024]{1,0:T(8,128)}, bf16[1024,1536]{1,0:T(8,128)(2,1)}, f32[192,768]{1,0:T(8,12...) custom-call(bf16[1024,1536]{1,0:T(8,128)(2,1)} %get-tuple-element.110.part, ...), custom_call_target="tpu_custom_call" | custom-call | tf_op jit(solution)/shard_map/pallas_call | solution.py:1170
  415.4 38.2 %shard_map.260 = (bf16[1024,1536]{1,0:T(8,128)(2,1)}, bf16[1024,768]{1,0:T(8,128)(2,1)}, bf16[1024,768]{1,0:T(8,128)(2,1)}, bf16[1024,128]{1,0:T(8,128)(2,1)}, b...) custom-call(bf16[1024,1536]{1,0:T(8,128)(2,1)} %get-tuple-element.118.top_ref, ...), custom_call_target="tpu_custom_call" | custom-call | flops 8455716864 | bytes 40000000 | tf_op jit(solution)/shard_map/pallas_call | solution.py:432
  453.6 1.3 convert_element_type.80.state
  454.9 0.6 copy-done.30
  455.5 4.0 convolution_convert_fusion.2.refs_0_
  459.5 4.0 convolution_convert_fusion.1.refs_1_
  463.5 4.3 convolution_convert_fusion.refs_2_
  467.8 1.8 convolution_convert_fusion.8.refs_3_
  469.6 1.9 convolution_convert_fusion.6
  471.5 109.6 %shard_map.261 = (f32[256,1536]{1,0:T(8,128)}, f32[8,1536]{1,0:T(8,128)}, f32[16,768]{1,0:T(8,128)}, f32[16,256]{1,0:T(8,128)}, f32[192,768]{1,0:T(8,128)}, /*in...) custom-call(bf16[1024,1536]{1,0:T(8,128)(2,1)} %get-tuple-element.128.part, ...), custom_call_target="tpu_custom_call" | custom-call | tf_op jit(solution)/shard_map/pallas_call | solution.py:1170
  581.2 2.2 pad_maximum_fusion
  583.4 1.1 pad_maximum_fusion.1
  584.5 0.6 pad_maximum_fusion.3
  585.2 0.7 copy.51
  585.9 2.4 maximum_bitcast_fusion
  588.4 1.4 slice.153
  589.8 0.6 slice.160
  590.4 0.6 slice.161
  591.0 0.6 fusion.11
  591.7 0.7 reduce_sum.9
  592.3 0.6 copy.59
  592.9 1.1 copy.62
  594.1 1.1 copy.63
  (100 shorter events, 1.7 us)
Async XLA Ops:
  0.6 3.7 copy-start.5
  0.7 4.6 copy-start.14
  0.7 5.4 copy-start.13
  4.3 89.2 %copy-start.18 = (f32[2,4,768]{2,1,0:T(4,128)S(1)}, f32[2,4,768]{2,1,0:T(4,128)}, u32[]{:S(2)}) copy-start(f32[2,4,768]{2,1,0:T(4,128)} %param.24) | copy-start | bytes 73732
  4.3 89.8 %copy-start.20 = (f32[2,4,256]{2,1,0:T(4,128)S(1)}, f32[2,4,256]{2,1,0:T(4,128)}, u32[]{:S(2)}) copy-start(f32[2,4,256]{2,1,0:T(4,128)} %param.25) | copy-start | bytes 24580
  4.3 90.4 %copy-start.23 = (f32[2,12]{1,0:T(2,128)S(1)}, f32[2,12]{1,0:T(2,128)}, u32[]{:S(2)}) copy-start(f32[2,12]{1,0:T(2,128)} %param.26) | copy-start | bytes 292
  4.3 90.4 %copy-start.24 = (f32[2,12]{1,0:T(2,128)S(1)}, f32[2,12]{1,0:T(2,128)}, u32[]{:S(2)}) copy-start(f32[2,12]{1,0:T(2,128)} %param.27) | copy-start | bytes 292
  4.4 91.0 %copy-start.21 = (f32[2,768]{1,0:T(2,128)S(1)}, f32[2,768]{1,0:T(2,128)}, u32[]{:S(2)}) copy-start(f32[2,768]{1,0:T(2,128)} %param.29) | copy-start | bytes 18436
  4.4 91.0 %copy-start.25 = (f32[2,12]{1,0:T(2,128)S(1)}, f32[2,12]{1,0:T(2,128)}, u32[]{:S(2)}) copy-start(f32[2,12]{1,0:T(2,128)} %param.28) | copy-start | bytes 292
  4.4 92.0 %copy-start.19 = (s32[1024]{0:T(1024)S(1)}, s32[1024]{0:T(1024)}, u32[]{:S(2)}) copy-start(s32[1024]{0:T(1024)} %param.16) | copy-start | bytes 12292
  253.6 37.9 %copy-start.26 = (bf16[1024,1536]{1,0:T(8,128)(2,1)S(1)}, bf16[1024,1536]{1,0:T(8,128)(2,1)}, u32[]{:S(2)}) copy-start(bf16[1024,1536]{1,0:T(8,128)(2,1)} %get-tuple-element.100.top_ref) | copy-start | bytes 9437188
  291.5 5.6 copy-start.2
  291.5 5.6 copy-start.32
  297.1 4.0 copy-start.31
  301.1 4.2 copy-start.10
  305.3 1.8 copy-start.34
  415.3 38.2 %copy-start.1 = (bf16[256,1536]{1,0:T(8,128)(2,1)S(1)}, bf16[256,1536]{1,0:T(8,128)(2,1)}, u32[]{:S(2)}) copy-start(bf16[256,1536]{1,0:T(8,128)(2,1)} %refs_12_.1) | copy-start | bytes 2359300
  415.4 39.5 %copy-start.27 = (bf16[1024,1536]{1,0:T(8,128)(2,1)S(1)}, bf16[1024,1536]{1,0:T(8,128)(2,1)}, u32[]{:S(2)}) copy-start(bf16[1024,1536]{1,0:T(8,128)(2,1)} %get-tuple-element.118.top_ref) | copy-start | bytes 9437188
  453.5 2.0 copy-start.30
  455.5 4.0 copy-start
  455.5 4.0 copy-start.29
  459.5 4.0 copy-start.28
  463.5 4.3 copy-start.9
  467.8 1.8 copy-start.33
  471.5 109.6 %copy-start.7 = (f32[192,768]{1,0:T(8,128)S(1)}, f32[192,768]{1,0:T(8,128)}, u32[]{:S(2)}) copy-start(f32[192,768]{1,0:T(8,128)} %get-tuple-element.142) | copy-start | bytes 1769476
  581.1 2.3 copy-start.6
  581.1 2.3 copy-start.8
  581.1 3.4 copy-start.15
  581.1 3.4 copy-start.16
  581.1 4.0 copy-start.11
  581.1 4.0 copy-start.12
  583.4 6.4 %copy-start.17 = (f32[16,768]{1,0:T(8,128)S(1)}, f32[16,768]{1,0:T(8,128)}, u32[]{:S(2)}) copy-start(f32[16,768]{1,0:T(8,128)} %get-tuple-element.152) | copy-start | bytes 147460
  583.4 7.0 %copy-start.22 = (f32[16,256]{1,0:T(8,128)S(1)}, f32[16,256]{1,0:T(8,128)}, u32[]{:S(2)}) copy-start(f32[16,256]{1,0:T(8,128)} %get-tuple-element.153) | copy-start | bytes 49156
  583.4 9.5 %copy-start.3 = (f32[256,1536]{1,0:T(8,128)S(1)}, f32[256,1536]{1,0:T(8,128)}, u32[]{:S(2)}) copy-start(f32[256,1536]{1,0:T(8,128)} %get-tuple-element.258) | copy-start | bytes 4718596
  585.9 8.2 %copy-start.4 = (f32[256,1536]{1,0:T(8,128)S(1)}, f32[256,1536]{1,0:T(8,128)}, u32[]{:S(2)}) copy-start(f32[256,1536]{1,0:T(8,128)} %get-tuple-element.259) | copy-start | bytes 4718596

commit v4 on v3

--- a/solution.py
+++ b/solution.py
@@ -1,4 +1,6 @@
 import functools
+import heapq
+import itertools
 
 import jax
 import jax.numpy as jnp
@@ -139,7 +141,7 @@
         cols = slice(pair * LANES, (pair + 1) * LANES)
         head = 2 * pair
         raw = ext_x[8 : 8 + CHUNK, cols]
-        iraw_ref[:, cols] = raw
+        iraw_ref[:, cols] = raw.astype(BF16)
         conv = convx_ref[TAPS - 1 : TAPS, cols] * raw
         for j in range(1, TAPS):
             conv = conv + convx_ref[TAPS - 1 - j : TAPS - j, cols] * (
@@ -171,10 +173,74 @@
     part_ref[...] = mm_nt(gg_ref[...], wout_ref[...]).astype(BF16)
 
 
-def backward_kernel(
+def gate_back_kernel(
     top_ref,
     sc_ref,
     gate_ref,
+    iconv_ref,
+    mixed_ref,
+    wout_ref,
+    wide_ref,
+    ggate_ref,
+    gout_ref,
+    outlow_ref,
+    small_ref,
+    gno_ref,
+):
+    inner = wout_ref.shape[1]
+
+    @pl.when(pl.program_id(0) == 0)
+    def _():
+        small_ref[...] = jnp.zeros_like(small_ref)
+
+    gno_ref[...] = mm(top_ref[...], wout_ref[...])
+    per_row = jnp.transpose(sc_ref[...])
+    scale = per_row[:, 0:1]
+    coef = per_row[:, 1:2]
+    for pair in range(inner // LANES):
+        cols = slice(pair * LANES, (pair + 1) * LANES)
+        gain = wide_ref[1:2, cols]
+        conv = iconv_ref[:, cols]
+        act = conv * sigmoid(conv)
+        gate = gate_ref[:, cols]
+        gate_sig = sigmoid(gate)
+        gate_act = gate * gate_sig
+        full = mixed_ref[:, cols] + wide_ref[0:1, cols] * act
+        gated = full * gate_act
+        gno = gno_ref[:, cols]
+        gated_scaled = gated * scale
+        small_ref[4:5, cols] += jnp.sum(gno * gated_scaled, axis=0, keepdims=True)
+        outlow_ref[:, cols] = (gated_scaled * gain).astype(BF16)
+        ggated = scale * (gno * gain) - gated * coef
+        gout_low = (ggated * gate_act).astype(BF16)
+        gout_ref[:, cols] = gout_low
+        ggate_ref[:, cols] = (
+            ggated * full * (gate_sig * (1.0 + gate * (1.0 - gate_sig)))
+        ).astype(BF16)
+        small_ref[5:6, cols] += jnp.sum(gout_low.astype(F32) * act, axis=0, keepdims=True)
+
+
+def gate_back(top_all, per_row, saved, weight_out, wide):
+    length, width = top_all.shape
+    inner = weight_out.shape[1]
+    gate, iconv, mixed = saved[0], saved[2], saved[6]
+    shape = jax.ShapeDtypeStruct
+    return pl.pallas_call(
+        gate_back_kernel,
+        grid=(length // CHUNK,),
+        in_specs=[block_rows(width), pl.BlockSpec((8, CHUNK), lambda i: (0, i))]
+        + [block_rows(inner)] * 3
+        + [whole_spec(weight_out.shape), whole_spec(wide.shape)],
+        out_specs=[block_rows(inner)] * 3 + [pl.BlockSpec((8, inner), lambda i: (0, 0))],
+        out_shape=[shape((length, inner), BF16)] * 3 + [shape((8, inner), F32)],
+        scratch_shapes=[pltpu.VMEM((CHUNK, inner), F32)],
+        compiler_params=pltpu.CompilerParams(
+            dimension_semantics=("arbitrary",), vmem_limit_bytes=VMEM_LIMIT
+        ),
+    )(top_all, per_row, gate, iconv, mixed, weight_out, wide)
+
+
+def mix_back_kernel(
     iraw_ref,
     iconv_ref,
     sraw_ref,
@@ -183,11 +249,12 @@
     mixed_ref,
     sin_ref,
     sout_ref,
+    ggate_ref,
+    gout_ref,
     wz_ref,
     wx_ref,
     wbc_ref,
     wdt_ref,
-    wout_ref,
     convx_ref,
     convbc_ref,
     heads_ref,
@@ -196,21 +263,19 @@
     aux_ref,
     segrow_ref,
     part_ref,
-    ggate_ref,
     ginner_ref,
     gstep_ref,
     gshared_ref,
-    outlow_ref,
     small_ref,
     smallbc_ref,
     gext_x,
     gext_bc,
     dstate,
-    gno_ref,
     balance,
     direct,
     edge,
     dcoup,
+    hook,
 ):
     inner = wx_ref.shape[1]
 
@@ -223,12 +288,9 @@
         smallbc_ref[...] = jnp.zeros_like(smallbc_ref)
         edge[...] = jnp.zeros_like(edge)
 
+    hook(0)
     aux = aux_ref[...]
     rate = heads_ref[1:2, :]
-    gno_ref[...] = mm(top_ref[...], wout_ref[...])
-    per_row = jnp.transpose(sc_ref[...])
-    scale = per_row[:, 0:1]
-    coef = per_row[:, 1:2]
     step_pre = step_ref[...] + heads_ref[0:1, :]
     step, cum, decay_in, decay_out, decay_pass = decays(step_pre, rate, aux)
     cum_t = jnp.transpose(cum)
@@ -250,29 +312,13 @@
         cols = slice(pair * LANES, (pair + 1) * LANES)
         head = 2 * pair
         skip = wide_ref[0:1, cols]
-        gain = wide_ref[1:2, cols]
         conv = iconv_ref[:, cols]
         conv_sig = sigmoid(conv)
         act = conv * conv_sig
         step_pair = pair_of(step, head)
         scaled = (act * step_pair).astype(BF16)
-        gate = gate_ref[:, cols]
-        gate_sig = sigmoid(gate)
-        gate_act = gate * gate_sig
-        mixed = mixed_ref[:, cols]
-        full = mixed + skip * act
-        gated = full * gate_act
-        gno = gno_ref[:, cols]
-        gated_scaled = gated * scale
-        small_ref[4:5, cols] += jnp.sum(gno * gated_scaled, axis=0, keepdims=True)
-        outlow_ref[:, cols] = (gated_scaled * gain).astype(BF16)
-        ggated = scale * (gno * gain) - gated * coef
-        gout_low = (ggated * gate_act).astype(BF16)
-        ggate_ref[:, cols] = (
-            ggated * full * (gate_sig * (1.0 + gate * (1.0 - gate_sig)))
-        ).astype(BF16)
+        gout_low = gout_ref[:, cols]
         gout = gout_low.astype(F32)
-        small_ref[5:6, cols] += jnp.sum(gout * act, axis=0, keepdims=True)
         zero = jnp.zeros_like(gout)
         parts = []
         for one, own in (
@@ -294,11 +340,11 @@
         dquery = dquery + mm_nt(entering, sin_ref[0, :, cols].astype(BF16))
         edge[0:1, cols] = jnp.sum(sout_ref[0, :, cols] * after, axis=0, keepdims=True)
         dstate[:, cols] = pair_of(decay_pass, head) * after + mm(query_t, entering)
-        balance[:, cols] = gout * mixed - scaled_wide * gscaled
+        balance[:, cols] = gout * mixed_ref[:, cols] - scaled_wide * gscaled
         direct[:, cols] = act * gscaled
         gact = step_pair * gscaled + skip * gout
         gext_x[0:CHUNK, cols] = gact * (conv_sig * (1.0 + conv * (1.0 - conv_sig)))
-        raw = iraw_ref[:, cols]
+        raw = iraw_ref[:, cols].astype(F32)
         gconv = gext_x[0:CHUNK, cols]
         graw = convx_ref[TAPS - 1 : TAPS, cols] * gconv
         small_ref[TAPS - 1 : TAPS, cols] += jnp.sum(raw * gconv, axis=0, keepdims=True)
@@ -310,6 +356,7 @@
             )
         ginner_ref[:, cols] = graw.astype(BF16)
         gext_x[CHUNK : CHUNK + 8, cols] = gext_x[0:8, cols]
+        hook(1 + pair)
     spread = spread_ref[...]
     order = (iota2((CHUNK, CHUNK), 0) <= iota2((CHUNK, CHUNK), 1)).astype(F32)
     running = jnp.dot(
@@ -336,6 +383,7 @@
         smallbc_ref[TAPS - 1 - j : TAPS - j, :] += jnp.sum(raw * moved, axis=0, keepdims=True)
     gshared_ref[...] = graw.astype(BF16)
     gext_bc[CHUNK : CHUNK + 8, :] = gext_bc[0:8, :]
+    hook(7)
     total = mm_nt(ggate_ref[...], wz_ref[...]) + mm_nt(ginner_ref[...], wx_ref[...])
     total = total + mm_nt(gstep_ref[...], wdt_ref[...])
     part_ref[...] = (total + mm_nt(gshared_ref[...], wbc_ref[...])).astype(BF16)
@@ -346,7 +394,7 @@
     return pl.BlockSpec(shape, lambda i: zeros, pipeline_mode=pl.Buffered(1))
 
 
-VMEM_LIMIT = 60 * 1024 * 1024
+VMEM_LIMIT = 62 * 1024 * 1024
 
 
 def block_rows(cols):
@@ -379,7 +427,7 @@
     shape = jax.ShapeDtypeStruct
     return [
         shape((length, inner), F32),
-        shape((length, inner), F32),
+        shape((length, inner), BF16),
         shape((length, inner), F32),
         shape((length, 2 * N), F32),
         shape((length, 2 * N), F32),
@@ -420,88 +468,45 @@
     )(rows_all, *weights, *layer_args, aux, segrow)
 
 
-def backward_layer(top_all, per_row, saved, weights, layer_args, spread, aux, segrow):
-    length, width = top_all.shape
-    chunks = length // CHUNK
-    inner = weights[1].shape[1]
+def mix_back_specs(chunks, inner, weights, layer_args, spread):
     last = chunks - 1
-    by_rows = lambda cols: pl.BlockSpec((CHUNK, cols), lambda i: (last - i, 0))
-    by_lanes = pl.BlockSpec((8, CHUNK), lambda i: (0, last - i))
-    shape = jax.ShapeDtypeStruct
-    gate, iraw, iconv, sraw, sconv, step, mixed, sin = saved
-    return pl.pallas_call(
-        backward_kernel,
-        grid=(chunks,),
-        in_specs=[
-            by_rows(width),
-            by_lanes,
-            by_rows(inner),
-            by_rows(inner),
-            by_rows(inner),
-            by_rows(2 * N),
-            by_rows(2 * N),
-            by_rows(LANES),
-            by_rows(inner),
+
+    def turned(cols):
+        return pl.BlockSpec((CHUNK, cols), lambda i: (last - i, 0))
+
+    return (
+        [
+            turned(inner),
+            turned(inner),
+            turned(2 * N),
+            turned(2 * N),
+            turned(LANES),
+            turned(inner),
             pl.BlockSpec((1, N, inner), lambda i: (last - i, 0, 0)),
             pl.BlockSpec((1, N, inner), lambda i: (jnp.minimum(chunks - i, last), 0, 0)),
+            turned(inner),
+            turned(inner),
         ]
         + [whole_spec(w.shape) for w in weights]
         + [whole_spec(w.shape) for w in layer_args]
-        + [whole_spec(spread.shape), by_rows(LANES), by_lanes],
-        out_specs=[
-            by_rows(width),
-            by_rows(inner),
-            by_rows(inner),
-            by_rows(LANES),
-            by_rows(2 * N),
-            by_rows(inner),
-            pl.BlockSpec((8, inner), lambda i: (0, 0)),
-            pl.BlockSpec((8, 2 * N), lambda i: (0, 0)),
-        ],
-        out_shape=[
-            shape((length, width), BF16),
-            shape((length, inner), BF16),
-            shape((length, inner), BF16),
-            shape((length, LANES), BF16),
-            shape((length, 2 * N), BF16),
-            shape((length, inner), BF16),
-            shape((8, inner), F32),
-            shape((8, 2 * N), F32),
-        ],
-        scratch_shapes=[
-            pltpu.VMEM((CHUNK + 8, inner), F32),
-            pltpu.VMEM((CHUNK + 8, 2 * N), F32),
-            pltpu.VMEM((N, inner), F32),
-            pltpu.VMEM((CHUNK, inner), F32),
-            pltpu.VMEM((CHUNK, inner), F32),
-            pltpu.VMEM((CHUNK, inner), F32),
-            pltpu.VMEM((8, inner), F32),
-            pltpu.VMEM((CHUNK, CHUNK), F32),
-        ],
-        compiler_params=pltpu.CompilerParams(
-            dimension_semantics=("arbitrary",), vmem_limit_bytes=VMEM_LIMIT
-        ),
-        cost_estimate=pl.CostEstimate(
-            flops=length * width * inner * 7, bytes_accessed=40_000_000, transcendentals=8_000_000
-        ),
-    )(
-        top_all,
-        per_row,
-        gate,
-        iraw,
-        iconv,
-        sraw,
-        sconv,
-        step,
-        mixed,
-        sin,
-        sin,
-        *weights,
-        *layer_args,
-        spread,
-        aux,
-        segrow,
-    )
+        + [
+            whole_spec(spread.shape),
+            turned(LANES),
+            pl.BlockSpec((8, CHUNK), lambda i: (0, last - i)),
+        ]
+    )
+
+
+def mix_back_scratch(inner):
+    return [
+        pltpu.VMEM((CHUNK + 8, inner), F32),
+        pltpu.VMEM((CHUNK + 8, 2 * N), F32),
+        pltpu.VMEM((N, inner), F32),
+        pltpu.VMEM((CHUNK, inner), F32),
+        pltpu.VMEM((CHUNK, inner), F32),
+        pltpu.VMEM((8, inner), F32),
+        pltpu.VMEM((CHUNK, CHUNK), F32),
+    ]
 
 
 def row_masks(segment_ids):
@@ -549,6 +554,7 @@
 PIECES = 4
 TENSOR = 4
 LATE = 1e9
+LAG = 8.0
 BIG = 6.5
 SMALL = 1.1
 
@@ -601,6 +607,10 @@
 class Timeline:
     def __init__(self):
         self.steps = []
+        self.rolling = []
+
+    def follow(self, slot, step):
+        self.rolling.append((slot, step))
 
     def add(self, when, step):
         self.steps.append((when, len(self.steps), step))
@@ -612,8 +622,13 @@
         for _, _, step in self.ordered():
             step()
 
-    def spread(self, chunks, slots, chunk_us):
+    def spread(self, chunks, slots, chunk_us, order=lambda k: k):
         places = {}
+        for slot, step in self.rolling:
+            for k in range(chunks):
+                if (k + 1) * slots + slot >= chunks * slots:
+                    when = ((k + 1) * slots + slot) * chunk_us / slots + (LAG if slot > 3 else 0.0)
+                    self.add(when, functools.partial(step, order(k)))
         after = []
         for when, _, step in self.ordered():
             spot = max(0, int(when / chunk_us * slots))
@@ -621,19 +636,25 @@
                 places.setdefault((spot % slots, spot // slots), []).append(step)
             else:
                 after.append(step)
+        now = pl.program_id(0)
 
         def hook(slot):
             for chunk in range(chunks):
                 steps = places.get((slot, chunk))
                 if steps:
 
-                    @pl.when(pl.program_id(0) == chunk)
+                    @pl.when(now == chunk)
                     def _(steps=steps):
                         for step in steps:
                             step()
 
+            for offset, step in self.rolling:
+                if offset % slots == slot:
+                    lag = 1 + offset // slots
+                    step(jnp.where(now >= lag, order(now - lag), -1))
+
         def end():
-            @pl.when(pl.program_id(0) == chunks - 1)
+            @pl.when(now == chunks - 1)
             def _():
                 for step in after:
                     step()
@@ -651,7 +672,59 @@
     return [pltpu.SemaphoreType.DMA((count, 2, line))] * 5
 
 
-def gather_weights(place, timeline, items, sems, start=0.0):
+HOP_US = 0.8
+ADD_US = 0.5
+
+
+def plan_gather(items, line):
+    free, plan = {}, {}
+    queue, count = [], itertools.count()
+
+    def push(when, *action):
+        heapq.heappush(queue, (when, next(count), action))
+
+    def transfer(link, when, cost):
+        begin = max(when, free.get(link, 0.0))
+        free[link] = begin + cost
+        return begin + cost + HOP_US
+
+    def note(step, when):
+        plan[step] = max(plan.get(step, 0.0), when)
+
+    def along(when, way, z, i, source, xs):
+        stop = z + 1 if way == 0 else z - 1
+        if 0 <= stop < line:
+            push(transfer((way, z), when, items[i][1]), "hop", way, stop, i, source, xs)
+
+    def cross(when, z, i, source):
+        push(transfer(("x", z), when, items[i][1]), "side", z, i, source)
+
+    for i, (_, _, ready) in enumerate(items):
+        push(ready, "own", i)
+    while queue:
+        when, _, (kind, *rest) = heapq.heappop(queue)
+        if kind == "own":
+            (i,) = rest
+            for z in range(line):
+                along(when, 0, z, i, z, 0)
+                along(when, 1, z, i, z, 0)
+                cross(when, z, i, z)
+        elif kind == "hop":
+            way, z, i, source, xs = rest
+            note(("hop", i, way, abs(z - source), xs), when)
+            along(when, way, z, i, source, xs)
+            if items[i][0] == "zx":
+                cross(when, z, i, source)
+        else:
+            z, i, source = rest
+            note(("side", i), when)
+            if items[i][0] == "xz":
+                along(when, 0, z, i, source, 1)
+                along(when, 1, z, i, source, 1)
+    return plan
+
+
+def gather_weights(place, timeline, items, sems):
     send_r, send_l, send_x, recv_z, recv_x = sems
     line = place.line
     z = place.z
@@ -750,23 +823,21 @@
 
         return step
 
-    period = sum(item[3] for item in items)
-    passed = 0.0
-    for i, (_, _, route, cost, due) in enumerate(items):
-        passed += cost
-        timeline.add(start, begin(i))
+    plan = plan_gather([(item[2], item[3], 0.0) for item in items], line)
+    for i, (_, _, route, _, early) in enumerate(items):
+        timeline.add(0.0, begin(i))
         if route == "xz":
-            timeline.add(start + passed, side(i))
+            timeline.add(plan["side", i], side(i))
         for k in range(1, line):
             for way in (0, 1):
-                for xs in (place.x,) if route == "zx" else (place.x, place.other):
-                    late = 0.0 if xs is place.x else period / 2
+                for column, xs in enumerate((place.x,) if route == "zx" else (place.x, place.other)):
                     arrive, finish = hop(i, way, k, xs, route == "zx")
-                    timeline.add(start + period * (k - 1) + passed + late, arrive)
+                    timeline.add(plan["hop", i, way, k, column], arrive)
                     timeline.add(LATE, finish)
         if route == "zx":
-            timeline.add(due, settle(i))
+            timeline.add(plan["side", i] + 1.0 if early else LATE, settle(i))
         timeline.add(LATE, end(i))
+    return plan
 
 
 def scatter_semaphores(count, line):
@@ -774,7 +845,7 @@
 
 
 def add_into(target, other, rows):
-    step = 48
+    step = 48 if rows % 48 == 0 else rows
 
     def body(n, carry):
         part = pl.ds(pl.multiple_of(n * step, step), step)
@@ -791,41 +862,117 @@
     return order
 
 
+def plan_scatter(items, line):
+    free, arrived, joined, plan = {}, {}, {}, {}
+    queue, count = [], itertools.count()
+
+    def push(when, *action):
+        heapq.heappush(queue, (when, next(count), action))
+
+    def transfer(link, when, cost):
+        begin = max(when, free.get(link, 0.0))
+        free[link] = begin + cost
+        return begin + cost + HOP_US
+
+    def note(step, when):
+        plan[step] = max(plan.get(step, 0.0), when)
+
+    def go(when, z, i, zz, xs):
+        first = {"r": z == 0, "l": z == line - 1}
+        if z == zz:
+            need = [way for way, there in (("r", z > 0), ("l", z < line - 1)) if there]
+            times = [arrived.get((way, z, i, zz, xs)) for way in need] + [joined.get((z, i, zz, xs))]
+            if None in times:
+                return
+            when = max(times)
+            if items[i][0] == "xz":
+                note(("last", i), when)
+                return
+            note(("line", i, xs), when)
+            done = joined.setdefault(("line", z, i), [])
+            done.append(when)
+            if len(done) == 2:
+                note(("swap", i), max(done))
+                note(("last", i), transfer(("x", z), max(done) + 2 * ADD_US, items[i][1]))
+            return
+        way = "r" if z < zz else "l"
+        times = [joined.get((z, i, zz, xs))]
+        if not first[way]:
+            times.append(arrived.get((way, z, i, zz, xs)))
+        if None in times:
+            return
+        when = max(times)
+        h = z if way == "r" else line - 1 - z
+        note(("send", i, zz, way, xs, h), when)
+        stop = z + 1 if way == "r" else z - 1
+        push(transfer((way, z), when + ADD_US, items[i][1]), "arrive", way, stop, i, zz, xs)
+
+    for i, (route, cost, ready) in enumerate(items):
+        for zz in scatter_order(line):
+            for xs in (0,) if route == "xz" else (0, 1):
+                push(ready, "start", i, zz, xs)
+    while queue:
+        when, _, (kind, *rest) = heapq.heappop(queue)
+        if kind == "start":
+            i, zz, xs = rest
+            for z in range(line):
+                if items[i][0] == "xz":
+                    push(transfer(("x", z), when, items[i][1]), "join", z, i, zz, xs)
+                else:
+                    push(when, "join", z, i, zz, xs)
+        elif kind == "join":
+            z, i, zz, xs = rest
+            if items[i][0] == "xz":
+                note(("join", i, zz), when)
+                when += ADD_US
+            joined[z, i, zz, xs] = when
+            go(when, z, i, zz, xs)
+        else:
+            way, z, i, zz, xs = rest
+            arrived[way, z, i, zz, xs] = when
+            go(when, z, i, zz, xs)
+    return plan
+
+
 def scatter_weights(place, timeline, items, sems):
     send_x, recv_x, send_r, recv_r, send_l, recv_l = sems
     line = place.line
     z = place.z
 
     def rows_of(i):
-        return items[i][1][0].shape[1]
+        return items[i][2][0].shape[1]
 
     def side(i, zz):
-        piece, (land_x, _, _), *_ = items[i]
+        _, source, (land_x, _), *_ = items[i]
         return remote(
-            piece(zz, place.other), land_x.at[zz], send_x.at[i, 0, zz], recv_x.at[i, 0, zz], place.across
+            source(zz, place.other), land_x.at[zz], send_x.at[i, 0, zz], recv_x.at[i, 0, zz], place.across
         )
 
-    def land_along(i, zz, way, xs):
-        land = items[i][1][1 + way]
-        return land.at[zz, xs] if items[i][3] == "zx" else land.at[zz]
+    def land_along(i, zz, way, xs, stop):
+        slot = zz if way == 0 else jnp.where(stop == zz, line, zz)
+        land = items[i][2][1]
+        return land.at[slot, xs] if items[i][4] == "zx" else land.at[slot]
 
     def along(i, zz, way, xs, source=None):
-        land = land_along(i, zz, way, xs)
+        here = land_along(i, zz, way, xs, z)
         return remote(
-            land if source is None else source,
-            land,
+            here if source is None else source,
+            land_along(i, zz, way, xs, z + 1 if way == 0 else z - 1),
             (send_r, send_l)[way].at[i, xs, zz],
             (recv_r, recv_l)[way].at[i, xs, zz],
             (place.right, place.left)[way],
         )
 
     def own(i, zz, xs):
-        return items[i][0](zz, xs) if items[i][3] == "zx" else items[i][1][0].at[zz]
+        return items[i][0](zz, xs) if items[i][4] == "zx" else items[i][2][0].at[zz]
+
+    def outgoing(i, zz, xs):
+        return items[i][1](zz, xs) if items[i][4] == "zx" else items[i][2][0].at[zz]
 
     def join(i, zz):
         def step():
             side(i, zz).wait_recv()
-            add_into(items[i][1][0].at[zz], items[i][0](zz, place.x), rows_of(i))
+            add_into(items[i][2][0].at[zz], items[i][0](zz, place.x), rows_of(i))
 
         return step
 
@@ -839,38 +986,38 @@
             @pl.when(mine)
             def _():
                 if h == 0:
-                    along(i, zz, way, xs, own(i, zz, xs)).start()
+                    along(i, zz, way, xs, outgoing(i, zz, xs)).start()
                 else:
                     along(i, zz, way, xs).wait_recv()
-                    add_into(land_along(i, zz, way, xs), own(i, zz, xs), rows_of(i))
+                    add_into(land_along(i, zz, way, xs, z), own(i, zz, xs), rows_of(i))
                     along(i, zz, way, xs).start()
 
         return step
 
     def last(i):
-        out = items[i][2]
+        out = items[i][3]
 
         def step():
-            out[...] = items[i][1][0][z].astype(F32)
+            out[...] = items[i][2][0][z].astype(F32)
             for way, there in ((0, z > 0), (1, z < line - 1)):
 
                 @pl.when(there)
                 def _(way=way):
                     along(i, z, way, 0).wait_recv()
-                    out[...] += items[i][1][1 + way][z].astype(F32)
+                    out[...] += items[i][2][1][z if way == 0 else line].astype(F32)
 
         return step
 
     def swap(i):
-        piece, (land_x, land_r, _), *_ = items[i]
-        stage = land_r.at[z, place.other]
+        land_x, land = items[i][2]
+        stage = land.at[z, place.other]
         return remote(stage, land_x.at[0], send_x.at[i, 0, 0], recv_x.at[i, 0, 0], place.across)
 
     def gather_line(i, xs):
         piece = items[i][0]
 
         def step():
-            right, left = land_along(i, z, 0, xs), land_along(i, z, 1, xs)
+            right, left = land_along(i, z, 0, xs, z), land_along(i, z, 1, xs, z)
 
             @pl.when(z > 0)
             def _():
@@ -889,17 +1036,17 @@
         return step
 
     def swap_end(i):
-        piece, (land_x, land_r, _), out, *_ = items[i]
+        (land_x, land), out = items[i][2:4]
 
         def step():
             swap(i).wait()
-            out[...] = land_r[z, place.x].astype(F32) + land_x[0].astype(F32)
+            out[...] = land[z, place.x].astype(F32) + land_x[0].astype(F32)
 
         return step
 
     def end(i, zz, xs):
         def step():
-            if items[i][3] == "xz":
+            if items[i][4] == "xz":
                 side(i, zz).wait_send()
             for way, there in ((0, z < zz), (1, z > zz)):
 
@@ -909,34 +1056,25 @@
 
         return step
 
-    now = 0.0
-    for i, (_, _, _, route, cost, ready) in enumerate(items):
-        if route == "zx":
-            then = ready
-            for zz in scatter_order(line):
-                for xs in (0, 1):
-                    for way in (0, 1):
-                        for h in range(zz if way == 0 else line - 1 - zz):
-                            timeline.add(then + h * cost + 0.2, send(i, zz, way, xs, h))
-                    timeline.add(LATE, end(i, zz, xs))
-                    then += cost
-            then += line * cost / 2
-            for xs in (0, 1):
-                timeline.add(then, gather_line(i, xs))
-            timeline.add(then + 0.1, lambda i=i: swap(i).start())
-            timeline.add(LATE - 1, swap_end(i))
+    plan = plan_scatter([item[4:] for item in items], line)
+    for i, (_, _, _, _, route, _, ready) in enumerate(items):
+        columns = (0,) if route == "xz" else (0, 1)
+        for zz in scatter_order(line):
+            if route == "xz":
+                timeline.add(ready, lambda i=i, zz=zz: side(i, zz).start())
+                timeline.add(plan["join", i, zz], join(i, zz))
+            for xs in columns:
+                for way, name in enumerate("rl"):
+                    for h in range(zz if way == 0 else line - 1 - zz):
+                        timeline.add(plan["send", i, zz, name, xs, h], send(i, zz, way, xs, h))
+                timeline.add(LATE, end(i, zz, xs))
+        if route == "xz":
+            timeline.add(plan["last", i], last(i))
             continue
-        now = max(now, ready)
-        for zz in scatter_order(line):
-            timeline.add(max(ready, now - 2 * BIG), lambda i=i, zz=zz: side(i, zz).start())
-            now += cost
-            timeline.add(now, join(i, zz))
-            for way in (0, 1):
-                hops = zz if way == 0 else line - 1 - zz
-                for h in range(hops):
-                    timeline.add(now + 0.01 + h * cost, send(i, zz, way, 0, h))
-            timeline.add(LATE, end(i, zz, 0))
-        timeline.add(now + line * cost, last(i))
+        for xs in columns:
+            timeline.add(plan["line", i, xs], gather_line(i, xs))
+        timeline.add(plan["swap", i] + ADD_US, lambda i=i: swap(i).start())
+        timeline.add(plan["last", i], swap_end(i))
 
 
 def spread_semaphores():
@@ -1051,6 +1189,80 @@
     for p in range(PIECES):
         timeline.add(start + 1.0 * (p + 1), middle(p))
         timeline.add(start + 2.0 + rate * (p + 1), final(p))
+    timeline.add(LATE, finish)
+
+
+def roll_rows(place, timeline, part, lands, sems, owner, forward):
+    land_far, land_near, land_mate = lands
+    send_a, recv_a, send_b, recv_b, send_z, recv_z = sems
+    rows = land_far.shape[0]
+    step = rows // PIECES
+
+    def at(block, p):
+        return part.at[pl.ds(pl.multiple_of(block * rows, rows) + p * step, step), :]
+
+    def own(ref, p):
+        return ref.at[pl.ds(p * step, step), :]
+
+    def far(p):
+        return remote(
+            at(place.diagonal, p), own(land_far, p), send_a.at[p], recv_a.at[p], (place.dp, place.sibling)
+        )
+
+    def near(p):
+        return remote(
+            at(place.sibling, p), own(land_near, p), send_b.at[p], recv_b.at[p], (place.dp, place.sibling)
+        )
+
+    def over(p):
+        return remote(
+            own(land_far, p), own(land_mate, p), send_z.at[p], recv_z.at[p], (place.dp, place.mate)
+        )
+
+    def begin(chunk):
+        @pl.when(place.diagonal == chunk)
+        def _():
+            for p in range(PIECES):
+                far(p).start()
+
+        @pl.when(place.sibling == chunk)
+        def _():
+            for p in range(PIECES):
+                near(p).start()
+
+    def middle(p, chunk):
+        @pl.when(place.mate == chunk)
+        def _():
+            far(p).wait_recv()
+            mine = own(land_far, p)
+            mine[...] = (mine[...].astype(F32) + at(place.mate, p)[...].astype(F32)).astype(BF16)
+            over(p).start()
+
+    def final(p, chunk):
+        @pl.when(place.t == chunk)
+        def _():
+            near(p).wait_recv()
+            over(p).wait_recv()
+            sums = at(place.t, p)[...].astype(F32) + own(land_near, p)[...].astype(F32)
+            owner(p, sums + own(land_mate, p)[...].astype(F32))
+
+    def pass_on(p, chunk):
+        @pl.when(place.mate == chunk)
+        def _():
+            forward(p)
+
+    def finish():
+        for p in range(PIECES):
+            far(p).wait_send()
+            near(p).wait_send()
+            over(p).wait_send()
+
+    timeline.follow(0, begin)
+    for p in range(PIECES):
+        timeline.follow(1 + p // 2, functools.partial(middle, p))
+        timeline.follow(4 + 3 * p, functools.partial(final, p))
+        if forward:
+            timeline.follow(8 + 3 * p, functools.partial(pass_on, p))
     timeline.add(LATE, finish)
 
 
@@ -1090,20 +1302,19 @@
 def weight_gather(place, timeline, refs, wholes, sems, share_sems, own_sems):
     bc_own, bc_all = refs[4], wholes[4]
     rows = refs[0].shape[0]
-    half = rows // 2
+    head, tail = halves(rows)
     pieces = [by_rows_piece(whole, rows) for whole in wholes[:4]]
 
     def bc_piece(zz, xs):
         return bc_all.at[zz * 2 + xs, place.t]
 
-    due = (3 * BIG + 2 * SMALL) * (place.line - 1) + 3.0
     items = [
-        (bc_own, bc_piece, "zx", SMALL / 2, due),
-        (refs[3], pieces[3], "zx", SMALL, LATE),
-        (refs[1], pieces[1], "zx", BIG, LATE),
-        (refs[0], pieces[0], "zx", BIG, LATE),
-        (refs[2].at[pl.ds(0, half), :], by_rows_piece(wholes[2], rows, 0, half), "xz", BIG / 2, LATE),
-        (refs[2].at[pl.ds(half, half), :], by_rows_piece(wholes[2], rows, half, half), "zx", BIG / 2, LATE),
+        (bc_own, bc_piece, "zx", SMALL / 2, True),
+        (refs[3], pieces[3], "zx", SMALL, False),
+        (refs[1], pieces[1], "zx", BIG, False),
+        (refs[0], pieces[0], "zx", BIG, False),
+        (refs[2].at[pl.ds(0, head), :], by_rows_piece(wholes[2], rows, 0, head), "xz", BIG / 2, False),
+        (refs[2].at[pl.ds(head, tail), :], by_rows_piece(wholes[2], rows, head, tail), "zx", BIG / 2, False),
     ]
     copies = own_copies(place, [(item[0], item[1]) for item in items], own_sems)
     shares = share_blocks(
@@ -1111,8 +1322,8 @@
     )
     timeline.add(-1.0, lambda: [copy.start() for copy in copies] and None)
     timeline.add(1.0, lambda: copies[0].wait())
-    gather_weights(place, timeline, items, sems)
-    timeline.add(due + 0.1, lambda: [copy.start() for copy in shares] and None)
+    plan = gather_weights(place, timeline, items, sems)
+    timeline.add(plan["side", 0] + 1.1, lambda: [copy.start() for copy in shares] and None)
     timeline.add(LATE + 1, lambda: [copy.wait() for copy in shares] and None)
     timeline.add(LATE + 1, lambda: [copy.wait() for copy in copies[1:]] and None)
 
@@ -1327,12 +1538,18 @@
             copy.start()
         out[:, pl.ds(pl.multiple_of(place.t * rows, rows), rows)] = stage[...]
 
+    def follow(chunk):
+        pl.when(place.t == chunk)(send)
+
     def arrive():
         for n, (copy, peer) in enumerate(zip(copies, peers)):
             copy.wait()
             out[:, pl.ds(pl.multiple_of(peer * rows, rows), rows)] = land[n]
 
-    timeline.add(when, send)
+    if when is None:
+        timeline.follow(5 + 3 * (PIECES - 1), follow)
+    else:
+        timeline.add(when, send)
     timeline.add(LATE, arrive)
 
 
@@ -1383,12 +1600,23 @@
     )
 
 
-def weight_scatter(place, timeline, grads, outs, lands, sems, bc_land, bc_sum, share_sems):
+def halves(rows):
+    first = max(rows // 32 * 16, 16)
+    return first, rows - first
+
+
+BACKWARD_US = 10.0
+DOTS_US = 6.0
+
+
+def weight_scatter(
+    place, timeline, grads, early, outs, lands, sems, bc_land, bc_sum, share_sems, late
+):
     bc = grads[4]
     shares = share_blocks(
         place, lambda peer: bc.at[:, peer], lambda n: bc_land.at[n], share_sems
     )
-    bc_ready = 12.0
+    bc_ready = late + 12.0
 
     def bc_add():
         for copy in shares:
@@ -1402,18 +1630,32 @@
 
         lax.fori_loop(0, bc.shape[0], body, 0)
 
-    timeline.add(-1.0, lambda: [copy.start() for copy in shares] and None)
+    timeline.add(late, lambda: [copy.start() for copy in shares] and None)
     timeline.add(bc_ready, bc_add)
     rows = outs[0].shape[0]
-    half = rows // 2
-    first, second = pl.ds(0, half), pl.ds(half, half)
+    head, tail = halves(rows)
+    first, second = pl.ds(0, head), pl.ds(head, tail)
+
+    def low(ref):
+        return by_rows_piece(ref, rows, 0, head)
+
+    def high(ref):
+        return by_rows_piece(ref, rows, head, tail)
+
+    def shared(zz, xs):
+        return bc_sum.at[zz * 2 + xs]
+
+    def step(ref):
+        return by_rows_piece(ref, rows)
+
     items = [
-        (by_rows_piece(grads[0], rows, 0, half), lands[15:18], outs[0].at[first, :], "zx", BIG / 2, 0.0),
-        (by_rows_piece(grads[0], rows, half, half), lands[0:3], outs[0].at[second, :], "xz", BIG / 2, 0.0),
-        (by_rows_piece(grads[1], rows), lands[3:6], outs[1], "xz", BIG, 0.0),
-        (by_rows_piece(grads[2], rows), lands[6:9], outs[2], "xz", BIG, 0.0),
-        (by_rows_piece(grads[3], rows), lands[9:12], outs[3], "xz", SMALL, 0.0),
-        (lambda zz, xs: bc_sum.at[zz * 2 + xs], lands[12:15], outs[4], "xz", SMALL / 2, bc_ready + 0.1),
+        (low(grads[0]), low(early[0]), lands[0:2], outs[0].at[first, :], "zx", BIG / 2, 0.0),
+        (high(grads[0]), high(early[0]), lands[2:4], outs[0].at[second, :], "xz", BIG / 2, 0.0),
+        (step(grads[1]), step(early[1]), lands[4:6], outs[1], "xz", BIG, 0.0),
+        (low(grads[2]), low(grads[2]), lands[6:8], outs[2].at[first, :], "xz", BIG / 2, late),
+        (high(grads[2]), high(grads[2]), lands[8:10], outs[2].at[second, :], "xz", BIG / 2, late),
+        (step(grads[3]), step(grads[3]), lands[10:12], outs[3], "xz", SMALL, late),
+        (shared, shared, lands[12:14], outs[4], "xz", SMALL / 2, bc_ready + 0.1),
     ]
     scatter_weights(place, timeline, items, sems)
 
@@ -1430,17 +1672,19 @@
 def scatter_scratch(line, width, inner):
     dp = 2 * line
     rows = width // dp
-    scratch = [pltpu.VMEM((line, rows // 2, inner), BF16)] * 3
-    scratch += [pltpu.VMEM((line, rows, inner), BF16)] * 6
-    scratch += [pltpu.VMEM((line, rows, LANES), BF16)] * 3
-    scratch += [pltpu.VMEM((line, rows // TENSOR, 2 * N), BF16)] * 3
-    scratch += [pltpu.VMEM((1, rows // 2, inner), BF16)]
-    scratch += [pltpu.VMEM((line, 2, rows // 2, inner), BF16)] * 2
+    head, tail = halves(rows)
+    fine = rows // TENSOR
+    scratch = [
+        pltpu.VMEM((1, head, inner), BF16),
+        pltpu.VMEM((line + 1, 2, head, inner), BF16),
+    ]
+    for count, cols in ((tail, inner), (rows, inner), (head, inner), (tail, inner), (rows, LANES), (fine, 2 * N)):
+        scratch += [pltpu.VMEM((line, count, cols), BF16), pltpu.VMEM((line + 1, count, cols), BF16)]
     scratch += [
-        pltpu.VMEM((3, dp, rows // TENSOR, 2 * N), BF16),
-        pltpu.VMEM((dp, rows // TENSOR, 2 * N), BF16),
+        pltpu.VMEM((3, dp, fine, 2 * N), BF16),
+        pltpu.VMEM((dp, fine, 2 * N), BF16),
     ]
-    return scratch + scatter_semaphores(6, line) + share_semaphores()
+    return scratch + scatter_semaphores(7, line) + share_semaphores()
 
 
 def input_gradient(state, gain, before, sums):
@@ -1451,190 +1695,265 @@
     return grad, jnp.sum(sums * state * scale, axis=0, keepdims=True)
 
 
-def turn_kernel(line, inner_all, part, before, state, gain, raw, scale_row, *refs):
-    grads, refs = refs[:5], refs[5:]
-    grad_out, gnorm, per_row, top_all, refs = *refs[:4], refs[4:]
+def late_dots(rows_all, ginner, gstep, gshared, dinner, dstep, dshared):
+    dp, tensor, fine, _ = dshared.shape
+    tile = rows_all.shape[1] // 2
+    per_tile = tile // (tensor * fine)
+
+    def body(n, carry):
+        part = pl.ds(pl.multiple_of(n * tile, tile), tile)
+        left = rows_all[:, part]
+        dinner[part, :] = contract(left, ginner[...])
+        dstep[part, :] = contract(left, gstep[...])
+        shared = contract_wide(left, gshared[...])
+        for m in range(per_tile * tensor):
+            block = shared[m * fine : (m + 1) * fine, :].astype(BF16)
+            dshared[n * per_tile + m // tensor, m % tensor] = block
+        return carry
+
+    lax.fori_loop(0, 2, body, 0)
+
+
+def pull_kernel(line, inner_all, final, *refs):
+    work, refs = refs[:21], refs[21:]
+    far_side, gain, refs = refs[:5], refs[5], refs[6:]
+    if final:
+        gnorm_top, small_more, small_top, small_top_more, bc_top, refs = *refs[:5], refs[5:]
+        grad_out, norm_sum, small_sum, bc_sums, refs = *refs[:4], refs[4:]
+    else:
+        raw, scale_row, refs = *refs[:2], refs[2:]
+        grad_out, gnorm, per_row, top_all, small, small_bc, refs = *refs[:6], refs[6:]
     outs, refs = refs[:5], refs[5:]
-    far, near, mate, row_land, cross_col, stage, low = refs[:7]
-    refs = refs[7:]
-    lands, bc_land, bc_sum, sems, share_sems = refs[:18], refs[18], refs[19], refs[20:26], refs[26:28]
-    refs = refs[28:]
-    reduce_sems, row_sems, top_sems, local = refs[:6], refs[6:8], refs[8:14], refs[14]
+    scratch, refs = refs[:7], refs[7:]
+    near_side, load_sems, refs = refs[:5], refs[5], refs[6:]
+    rows_all, dout, dgate, before, state = near_side
+    loads = [
+        pltpu.make_async_copy(source, target, load_sems.at[n])
+        for n, (source, target) in enumerate(zip(far_side, near_side))
+    ]
+    part, ginner, gstep, gshared, dinner, dstep, dshared = refs[:7]
+    far, near, mate, refs = *refs[7:10], refs[10:]
+    lands, bc_land, bc_sum, sems, share_sems = refs[:14], refs[14], refs[15], refs[16:22], refs[22:24]
+    reduce_sems, refs = refs[24:30], refs[30:]
+    if final:
+        small, small_bc, small_land, bc_land_sums, norm_land = refs[:5]
+        small_send, small_recv = refs[5:]
+    else:
+        row_land, cross_col, stage, low = refs[:4]
+        row_sems, top_sems, local = refs[4:6], refs[6:12], refs[12]
+    dp = 2 * line
+    bits = [1 << n for n in range(dp.bit_length() - 1)]
+    chunk = pl.program_id(0)
+    chunks = part.shape[0] // CHUNK
     place = Place(line)
-    place.greet()
+    far_bits = [bit for bit in bits if bit >= 4] if final else []
+    pl.when(chunk == 0)(lambda: place.greet(far_bits=far_bits))
     timeline = Timeline()
-    rows = low.shape[0]
+    done = BACKWARD_US * chunks + 0.5
+    late = done + 2.2 + DOTS_US
+    rows = state.shape[0]
     step = rows // PIECES
-    begin, forward, finish = spread_rows(place, low, top_all, top_sems)
-    gnorm[...] = jnp.zeros_like(gnorm)
+
+    if not final:
+        begin, forward, finish = spread_rows(place, low, top_all, top_sems)
+
+    def clear():
+        if final:
+            norm_sum[...] = jnp.zeros_like(norm_sum)
+            norm_sum[1:2, :] = gnorm_top[0:1, :]
+        else:
+            gnorm[...] = jnp.zeros_like(gnorm)
+
+    def load():
+        for n in (1, 2, 3, 4, 0):
+            loads[n].start()
+
+    timeline.add(-2.0, load)
+    timeline.add(-2.0, clear)
+    for n in (1, 2, 3, 4, 0):
+        timeline.add(2.5 if n in (1, 2) else BACKWARD_US / 2, loads[n].wait)
 
     def owner(p, sums):
         part_rows = slice(p * step, (p + 1) * step)
         grad, column = input_gradient(
-            state[part_rows, :], gain[...], before[part_rows, :], sums
+            state[part_rows, :].astype(F32), gain[...], before[part_rows, :], sums
         )
         grad_out[part_rows, :] = grad
+        if final:
+            norm_sum[0:1, :] += column
+            return
         gnorm[0:1, :] += column
         low[part_rows, :] = grad.astype(BF16)
         cross = jnp.sum(low[part_rows, :].astype(F32) * raw[part_rows, :], axis=1, keepdims=True)
         cross_col[part_rows, :] = jnp.broadcast_to(cross, (step, LANES))
         begin(p)
 
-    reduce_rows(place, timeline, part, (far, near, mate), reduce_sems, owner, RATE)
-    for p in range(PIECES):
-        timeline.add(3.0 + RATE * (PIECES + 1 + p), functools.partial(forward, p))
-    block = pl.ds(pl.multiple_of(place.t * rows, rows), rows)
-    keep = pltpu.make_async_copy(low, top_all.at[block, :], local.at[0])
-    timeline.add(3.0 + RATE * PIECES, keep.start)
-    timeline.add(LATE, keep.wait)
-    timeline.add(LATE, finish)
-    per_row_steps(
-        place, timeline, scale_row, cross_col, stage, row_land, per_row, row_sems, inner_all,
-        3.0 + RATE * PIECES,
-    )
-    weight_scatter(place, timeline, grads, outs, lands, sems, bc_land, bc_sum, share_sems)
-    timeline.run()
-
-
-def turn_layer(line, inner_all, part, before, state, gain, raw, scale_row, grads):
-    rows, width = state.shape
-    inner = grads[0].shape[1]
+    roll_rows(
+        place, timeline, part, (far, near, mate), reduce_sems, owner, None if final else forward
+    )
+    timeline.add(
+        done + 2.2, lambda: late_dots(rows_all, ginner, gstep, gshared, dinner, dstep, dshared)
+    )
+    if not final:
+        block = pl.ds(pl.multiple_of(place.t * rows, rows), rows)
+        keep = pltpu.make_async_copy(low, top_all.at[block, :], local.at[0])
+        timeline.follow(5 + 3 * (PIECES - 1), lambda chunk: pl.when(place.t == chunk)(keep.start))
+        timeline.add(LATE, keep.wait)
+        timeline.add(LATE, finish)
+        per_row_steps(
+            place, timeline, scale_row, cross_col, stage, row_land, per_row, row_sems, inner_all, None
+        )
+    grads = (dout, dgate, dinner, dstep, dshared)
+    weight_scatter(
+        place, timeline, grads, far_side[1:3], outs, lands, sems, bc_land, bc_sum, share_sems, late
+    )
+    if final:
+
+        def pack():
+            small_sum[0:8, :] = small[...] + small_more[...]
+            small_sum[8:16, :] = small_top[...] + small_top_more[...]
+            bc_sums[0:8, :] = small_bc[...]
+            bc_sums[8:16, :] = bc_top[...]
+
+        timeline.add(done + 0.05, pack)
+        along = [place.partner(bit) for bit in bits]
+        across = [(place.dp, place.sibling), (place.dp, place.mate)]
+
+        def exchange(n, partner, group, start, end):
+            copies = [
+                remote(own, land.at[n], small_send.at[n, m], small_recv.at[n, m], partner)
+                for m, own, land in group
+            ]
+
+            def send():
+                for copy in copies:
+                    copy.start()
+
+            def take():
+                for copy, (_, own, land) in zip(copies, group):
+                    copy.wait()
+                    own[...] += land[n]
+
+            timeline.add(start, send)
+            timeline.add(end, take)
+
+        when = done + 17.0 + LAG
+        steps = [(len(bits), across[0], 3.0), (len(bits) + 1, across[1], 5.0)]
+        steps += [(n, along[n], 7.0) for n in range(len(bits))][::-1]
+        for n, partner, wait in steps:
+            group = [(0, bc_sums, bc_land_sums), (1, norm_sum, norm_land)]
+            if n < len(bits):
+                group.append((2, small_sum, small_land))
+            exchange(n, partner, group, when, when + wait)
+            when += wait + 0.01
+    hook, end = timeline.spread(chunks, SLOTS, BACKWARD_US, lambda n: chunks - 1 - n)
+    at = pl.ds(pl.multiple_of((chunks - 1 - chunk) * CHUNK, CHUNK), CHUNK)
+    mix_back_kernel(
+        *work,
+        part.at[at, :],
+        ginner.at[at, :],
+        gstep.at[at, :],
+        gshared.at[at, :],
+        small,
+        small_bc,
+        *scratch,
+        hook=hook,
+    )
+    end()
+
+
+def pull_layer(
+    line, inner_all, saved, gates, weights, layer_args, spread, aux, segrow, rows_all, dout, dgate,
+    before, state, gain, more, final,
+):
+    length, width = rows_all.shape
+    rows = state.shape[0]
+    inner = dout.shape[1]
+    dp = 2 * line
+    fine = width // (dp * TENSOR)
+    steps = dp.bit_length() - 1
     shape = jax.ShapeDtypeStruct
-    outs = [
-        shape((rows, width), F32),
-        shape((8, width), F32),
-        shape((8, rows * TENSOR), F32),
-        shape((rows * TENSOR, width), BF16),
-    ] + scatter_outputs(width, inner, 2 * line)
-    scratch = [pltpu.VMEM((rows, width), BF16)] * 3
+    _, iraw, iconv, sraw, sconv, step, mixed, sin = saved
+    far_side = (rows_all, dout, dgate, before, state)
+    whole = (gain, *more)
+    if final:
+        outs = [
+            shape((rows, width), F32),
+            shape((8, width), F32),
+            shape((16, inner), F32),
+            shape((16, 2 * N), F32),
+        ]
+        out_specs = [whole_spec(out.shape) for out in outs]
+    else:
+        outs = [
+            shape((rows, width), F32),
+            shape((8, width), F32),
+            shape((8, rows * TENSOR), F32),
+            shape((length, width), BF16),
+            shape((8, inner), F32),
+            shape((8, 2 * N), F32),
+        ]
+        out_specs = [whole_spec(out.shape) for out in outs]
+        out_specs[3] = ANY
+    tail_outs = scatter_outputs(width, inner, dp)
+    scratch = mix_back_scratch(inner)
+    scratch += [pltpu.VMEM(array.shape, array.dtype) for array in far_side]
+    scratch += [pltpu.SemaphoreType.DMA((5,))]
     scratch += [
-        pltpu.VMEM((3, 8, rows), F32),
-        pltpu.VMEM((rows, LANES), F32),
-        pltpu.VMEM((8, rows), F32),
-        pltpu.VMEM((rows, width), BF16),
+        pltpu.VMEM((length, width), BF16),
+        pltpu.VMEM((length, inner), BF16),
+        pltpu.VMEM((length, LANES), BF16),
+        pltpu.VMEM((length, 2 * N), BF16),
+        pltpu.VMEM((width, inner), BF16),
+        pltpu.VMEM((width, LANES), BF16),
+        pltpu.VMEM((dp, TENSOR, fine, 2 * N), BF16),
     ]
-    scratch += scatter_scratch(line, width, inner)
-    scratch += reduce_semaphores() + share_semaphores() + spread_semaphores()
-    scratch += [pltpu.SemaphoreType.DMA((1,))]
+    scratch += [pltpu.VMEM((rows, width), BF16)] * 3
+    scratch += scatter_scratch(line, width, inner) + reduce_semaphores()
+    if final:
+        scratch += [
+            pltpu.VMEM((8, inner), F32),
+            pltpu.VMEM((8, 2 * N), F32),
+            pltpu.VMEM((steps, 16, inner), F32),
+            pltpu.VMEM((steps + 2, 16, 2 * N), F32),
+            pltpu.VMEM((steps + 2, 8, width), F32),
+            pltpu.SemaphoreType.DMA((steps + 2, 3)),
+            pltpu.SemaphoreType.DMA((steps + 2, 3)),
+        ]
+    else:
+        scratch += [
+            pltpu.VMEM((3, 8, rows), F32),
+            pltpu.VMEM((rows, LANES), F32),
+            pltpu.VMEM((8, rows), F32),
+            pltpu.VMEM((rows, width), BF16),
+        ]
+        scratch += share_semaphores() + spread_semaphores() + [pltpu.SemaphoreType.DMA((1,))]
+    weights = weights[:4]
     return call_kernel(
-        functools.partial(turn_kernel, line, inner_all),
-        outs,
-        [IN_VMEM] * 11,
-        [IN_VMEM] * 3 + [ANY] + [IN_VMEM] * 5,
+        functools.partial(pull_kernel, line, inner_all, final),
+        outs + tail_outs,
+        mix_back_specs(length // CHUNK, inner, weights, layer_args, spread)
+        + [ANY] * 5
+        + [whole_spec(array.shape) for array in whole],
+        out_specs + [whole_spec(out.shape) for out in tail_outs],
         scratch,
-        3,
-        (part, before, state, gain, raw, scale_row, *grads),
-    )
-
-
-def end_kernel(line, part, before, state, gain, gnorm_top, small_a, small_b, bc_a, bc_b, *refs):
-    grads, refs = refs[:5], refs[5:]
-    grad_out, norm_sum, small_sum, bc_sums, refs = *refs[:4], refs[4:]
-    outs, refs = refs[:5], refs[5:]
-    far, near, mate = refs[:3]
-    lands, bc_land, bc_sum, sems, share_sems = refs[3:21], refs[21], refs[22], refs[23:29], refs[29:31]
-    refs = refs[31:]
-    reduce_sems, refs = refs[:6], refs[6:]
-    small_land, bc_land_sums, top_land, norm_land, norm_top, small_send, small_recv = refs
-    dp = 2 * line
-    bits = [1 << n for n in range(dp.bit_length() - 1)]
-    place = Place(line)
-    place.greet(far_bits=[bit for bit in bits if bit >= 4])
-    timeline = Timeline()
-    step = state.shape[0] // PIECES
-    norm_sum[...] = jnp.zeros_like(norm_sum)
-    norm_top[...] = gnorm_top[...]
-    small_sum[0:8, :] = small_a[...]
-    small_sum[8:16, :] = small_b[...]
-    bc_sums[0:8, :] = bc_a[...]
-    bc_sums[8:16, :] = bc_b[...]
-
-    def owner(p, sums):
-        part_rows = slice(p * step, (p + 1) * step)
-        grad, column = input_gradient(
-            state[part_rows, :], gain[...], before[part_rows, :], sums
-        )
-        grad_out[part_rows, :] = grad
-        norm_sum[0:1, :] += column
-
-    reduce_rows(place, timeline, part, (far, near, mate), reduce_sems, owner, RATE)
-    weight_scatter(place, timeline, grads, outs, lands, sems, bc_land, bc_sum, share_sems)
-    along = [place.partner(bit) for bit in bits]
-    across = [(place.dp, place.sibling), (place.dp, place.mate)]
-
-    def exchange(n, partner, group, start, end):
-        copies = [
-            remote(own, land.at[n], small_send.at[n, m], small_recv.at[n, m], partner)
-            for m, own, land in group
-        ]
-
-        def send():
-            for copy in copies:
-                copy.start()
-
-        def take():
-            for copy, (_, own, land) in zip(copies, group):
-                copy.wait()
-                own[...] += land[n]
-
-        timeline.add(start, send)
-        timeline.add(end, take)
-
-    early = -1.5
-    for n, partner in enumerate(along + across):
-        group = [(0, bc_sums, bc_land_sums), (1, norm_top, top_land)]
-        if n < len(bits):
-            group.append((2, small_sum, small_land))
-        later = 3.0 if n == 0 else early + 5.0
-        exchange(n, partner, group, early, later)
-        early = later + 0.01
-    late = 4.0 + RATE * PIECES
-    for n, partner in list(enumerate(along + across))[::-1]:
-        later = late + (3.5 if n >= len(bits) else 16.0)
-        exchange(n, partner, [(3, norm_sum, norm_land)], late, later)
-        late = later + 0.01
-    timeline.add(LATE + 1, lambda: norm_sum.__setitem__((slice(1, 2), slice(None)), norm_top[0:1, :]))
-    timeline.run()
-
-
-def end_layer(line, part, before, state, gain, gnorm_top, smalls, grads):
-    rows, width = state.shape
-    inner = grads[0].shape[1]
-    shape = jax.ShapeDtypeStruct
-    dp = 2 * line
-    steps = dp.bit_length() - 1
-    outs = [
-        shape((rows, width), F32),
-        shape((8, width), F32),
-        shape((16, inner), F32),
-        shape((16, 2 * N), F32),
-    ] + scatter_outputs(width, inner, dp)
-    scratch = [pltpu.VMEM((rows, width), BF16)] * 3 + scatter_scratch(line, width, inner)
-    scratch += reduce_semaphores()
-    scratch += [
-        pltpu.VMEM((steps, 16, inner), F32),
-        pltpu.VMEM((steps + 2, 16, 2 * N), F32),
-        pltpu.VMEM((steps + 2, 8, width), F32),
-        pltpu.VMEM((steps + 2, 8, width), F32),
-        pltpu.VMEM((8, width), F32),
-        pltpu.SemaphoreType.DMA((steps + 2, 4)),
-        pltpu.SemaphoreType.DMA((steps + 2, 4)),
-    ]
-    return call_kernel(
-        functools.partial(end_kernel, line),
-        outs,
-        [IN_VMEM] * 14,
-        [IN_VMEM] * 9,
-        scratch,
-        4,
-        (part, before, state, gain, gnorm_top, *smalls, *grads),
-    )
-
-
-def contract(left, right):
+        4 if final else 3,
+        (
+            iraw, iconv, sraw, sconv, step, mixed, sin, sin, *gates,
+            *weights, *layer_args, spread, aux, segrow, *far_side, *whole,
+        ),
+        (length // CHUNK,),
+    )
+
+
+def contract_wide(left, right):
     return lax.dot_general(
         left, right, (((0,), (0,)), ((), ())), preferred_element_type=F32
-    ).astype(BF16)
+    )
+
+
+def contract(left, right):
+    return contract_wide(left, right).astype(BF16)
 
 
 def on_device(
@@ -1694,36 +2013,25 @@
     part, sq, *saved_high = forward_layer(rows_high, weights_high, args[1], aux, segrow)
     hidden, per_row = top_layer(line, inner_all, part, sq, state, cotangent)
 
-    def weight_grads(rows_all, top_all, pulled):
-        ggate, ginner, gstep, gshared, outlow = pulled
-        return (
-            contract(top_all, outlow),
-            contract(rows_all, ggate),
-            contract(rows_all, ginner),
-            contract(rows_all, gstep),
-            contract(rows_all, gshared).reshape(dp, TENSOR, width // (dp * TENSOR), 2 * N),
-        )
-
-    part, *pulled, small_high, bc_high = backward_layer(
-        top_high, per_row, saved_high, weights_high, args[1], spread, aux, segrow
-    )
-    grads = weight_grads(rows_high, top_high, pulled)
-    grad_state, gnorm_high, per_row, top_low, *grads_high = turn_layer(
-        line, inner_all, part, cotangent, state, gains[1], raw, scale_row, grads
-    )
-    part, *pulled, small_low, bc_low = backward_layer(
-        top_low, per_row, saved_low, weights_low, args[0], spread, aux, segrow
-    )
-    grads = weight_grads(rows_low, top_low, pulled)
-    grad_resid, norm_sum, small, small_bc, *grads_low = end_layer(
-        line,
-        part,
-        grad_state,
-        resid.astype(F32),
-        gains[0],
-        gnorm_high,
-        (small_low, small_high, bc_low, bc_high),
-        grads,
+    def early_grads(rows_all, top_all, per_row, saved, weights, wide):
+        ggate, gout, outlow, small = gate_back(top_all, per_row, saved, weights[4], wide)
+        return (ggate, gout), contract(top_all, outlow), contract(rows_all, ggate), small
+
+    gates, dout, dgate, small_high_more = early_grads(
+        rows_high, top_high, per_row, saved_high, weights_high, args[1][3]
+    )
+    results = pull_layer(
+        line, inner_all, saved_high, gates, weights_high, args[1], spread, aux, segrow, rows_high,
+        dout, dgate, cotangent, state, gains[1], (raw, scale_row), False,
+    )
+    grad_state, gnorm_high, per_row, top_low, small_high, bc_high, *grads_high = results
+    gates, dout, dgate, small_low_more = early_grads(
+        rows_low, top_low, per_row, saved_low, weights_low, args[0][3]
+    )
+    more = (gnorm_high, small_low_more, small_high, small_high_more, bc_high)
+    grad_resid, norm_sum, small, small_bc, *grads_low = pull_layer(
+        line, inner_all, saved_low, gates, weights_low, args[0], spread, aux, segrow, rows_low,
+        dout, dgate, grad_state, resid, gains[0], more, True,
     )
     gout, gz, gx, gdt, gbc = [
         jnp.stack([low, high]) for low, high in zip(grads_low, grads_high)

time: 606 us -> 527 us (0.87)
  the two profiles are of different devices: /device:TPU:0 before, /device:TPU:9 now
where the time goes in v4:
time: 527 us; the launch traced here: 517 us
  Pallas kernels  461 us (87%)
  local copies, waits for them, and re-layouts  23.3 us (4%)
  matrix products  21.1 us (4%)
  other arithmetic  10.2 us (2%)
    pallas_call x5, Pallas kernels, call_kernel(): pl.pallas_call(kernel, grid=grid, out_shape=outs, in_specs=in_specs, out_...  413 us
    pallas_call x1, Pallas kernels, forward_layer(): pl.pallas_call(forward_kernel, grid=(length // CHUNK,), in_specs=forward_...  26.3 us
    pallas_call x2, Pallas kernels, gate_back(): pl.pallas_call(gate_back_kernel, grid=(length // CHUNK,), in_specs=[block...  21.6 us
    dot_general x4, matrix products, contract_wide(): lax.dot_general(left, right, (((0,), (0,)), ((), ())), preferred_element_...  21.1 us

profile of v4, /device:TPU:9, one launch (start us, length us, event | category | flops | bytes accessed | tf_op | source)
XLA Modules:
  0.0 516.8 jit_solution(14863273385546669638)
XLA Ops:
  0.7 0.8 exponential_negate_fusion
  1.4 0.8 fusion.18
  2.2 0.6 select_maximum_fusion
  2.8 0.8 slice_bitcast_fusion.12
  3.5 0.7 convert_element_type.50
  4.7 0.8 fusion.14
  5.8 0.6 pad_maximum_fusion.4
  6.6 0.8 fusion.6
  7.4 1.3 slice_bitcast_fusion.10
  8.7 1.4 fusion.13
  10.1 0.2 stack.133
  10.3 0.8 fusion.12
  11.1 1.3 slice_bitcast_fusion.8
  12.4 0.6 broadcast_in_dim.26.refs_11_.segrow_ref.refs_20_
  13.2 0.6 pad.25.refs_17_
  13.9 0.6 pad.22.refs_3_
  14.6 1.5 slice_bitcast_fusion.6
  16.1 0.8 fusion.refs_18_
  17.1 0.8 pad.24.refs_10_.aux_ref.refs_19_
  17.9 0.9 slice_bitcast_fusion
  18.8 1.0 slice_bitcast_fusion.1
  19.8 81.2 %shard_map.254 = (bf16[1536,768]{1,0:T(8,128)(2,1)}, bf16[1536,768]{1,0:T(8,128)(2,1)}, bf16[1536,768]{1,0:T(8,128)(2,1)}, bf16[1536,128]{1,0:T(8,128)(2,1)}, bf...) custom-call(bf16[256,1536]{1,0:T(8,128)(2,1)} %refs_25_.1, ...), custom_call_target="tpu_custom_call" | custom-call | tf_op jit(solution)/shard_map/pallas_call | solution.py:1381
  101.0 85.5 %shard_map.255 = (f32[1024,768]{1,0:T(8,128)}, bf16[1024,768]{1,0:T(8,128)(2,1)}, f32[1024,768]{1,0:T(8,128)}, f32[1024,256]{1,0:T(8,128)}, f32[1024,256]{1,0:T(...) custom-call(bf16[1024,1536]{1,0:T(8,128)(2,1)} %get-tuple-element.78, ...), custom_call_target="tpu_custom_call" | custom-call | tf_op jit(solution)/shard_map/pallas_call | solution.py:1381
  186.5 26.3 %shard_map.256 = (bf16[1024,1536]{1,0:T(8,128)(2,1)}, f32[8,1024]{1,0:T(8,128)}, f32[1024,768]{1,0:T(8,128)}, bf16[1024,768]{1,0:T(8,128)(2,1)}, f32[1024,768]{1...) custom-call(bf16[1024,1536]{1,0:T(8,128)(2,1)} %get-tuple-element.84, ...), custom_call_target="tpu_custom_call" | custom-call | flops 8455716864 | bytes 40000000 | tf_op jit(solution)/shard_map/pallas_call | solution.py:453
  212.8 29.2 %shard_map.257 = (f32[256,1536]{1,0:T(8,128)}, f32[8,1024]{1,0:T(8,128)}) custom-call(bf16[1024,1536]{1,0:T(8,128)(2,1)} %get-tuple-element.90.part, f32[8,1024]{1,0:T(8,128)} %get-tuple-element.91.sq, f32[256,1536]{1,0:T(8,128)} %get-tuple-element.92.state.refs_25_, f32[256,1536]{1,0:T(8,128)} %refs_24_.1), custom_call_target="tpu_custom_call" | custom-call | tf_op jit(solution)/shard_map/pallas_call | solution.py:1381
  242.0 10.8 %shard_map.258 = (bf16[1024,768]{1,0:T(8,128)(2,1)}, bf16[1024,768]{1,0:T(8,128)(2,1)}, bf16[1024,768]{1,0:T(8,128)(2,1)}, f32[8,768]{1,0:T(8,128)}) custom-call(bf16[1024,1536]{1,0:T(8,128)(2,1)} %get-tuple-element.108.top_ref, f32[8,1024]{1,0:T(8,128)} %get-tuple-element.109.sc_ref, f32[1024,768]{1,0:T(8,128)} %get-tuple-element.110.gate_ref, ...), custom_call_target="tpu_custom_call" | custom-call | tf_op jit(solution)/shard_map/pallas_call | solution.py:228
  252.8 6.6 %convolution_convert_fusion.3.refs_22_ = bf16[1536,768]{1,0:T(8,128)(2,1)} fusion(bf16[1024,1536]{1,0:T(8,128)(2,1)} %get-tuple-element.108.top_ref, bf16[1024,768]{1,0:T(8,128)(2,1)} %get-tuple-element.113), kind=kOutput, calls=%fused_computation.3 | convolution fusion | flops 2417098752 | bytes 7077888 | tf_op jit(solution)/shard_map/dot_general | solution.py:1950
  259.5 4.0 convolution_convert_fusion.2.refs_23_
  263.5 105.2 %shard_map.259 = (f32[256,1536]{1,0:T(8,128)}, f32[8,1536]{1,0:T(8,128)}, f32[8,1024]{1,0:T(8,128)}, bf16[1024,1536]{1,0:T(8,128)(2,1)}, f32[8,768]{1,0:T(8,128)...) custom-call(bf16[1024,768]{1,0:T(8,128)(2,1)} %get-tuple-element.101, ...), custom_call_target="tpu_custom_call" | custom-call | tf_op jit(solution)/shard_map/pallas_call | solution.py:1381
  368.6 10.8 %shard_map.260 = (bf16[1024,768]{1,0:T(8,128)(2,1)}, bf16[1024,768]{1,0:T(8,128)(2,1)}, bf16[1024,768]{1,0:T(8,128)(2,1)}, f32[8,768]{1,0:T(8,128)}) custom-call(bf16[1024,1536]{1,0:T(8,128)(2,1)} %get-tuple-element.116.top_ref, f32[8,1024]{1,0:T(8,128)} %get-tuple-element.117.sc_ref, f32[1024,768]{1,0:T(8,128)} %get-tuple-element.118.gate_ref, ...), custom_call_target="tpu_custom_call" | custom-call | tf_op jit(solution)/shard_map/pallas_call | solution.py:228
  379.5 6.5 %convolution_convert_fusion.1.refs_22_ = bf16[1536,768]{1,0:T(8,128)(2,1)} fusion(bf16[1024,1536]{1,0:T(8,128)(2,1)} %get-tuple-element.116.top_ref, bf16[1024,768]{1,0:T(8,128)(2,1)} %get-tuple-element.121), kind=kOutput, calls=%fused_computation.1 | convolution fusion | flops 2417098752 | bytes 7077888 | tf_op jit(solution)/shard_map/dot_general | solution.py:1950
  386.0 4.0 convolution_convert_fusion.refs_23_
  390.0 112.3 %shard_map.261 = (f32[256,1536]{1,0:T(8,128)}, f32[8,1536]{1,0:T(8,128)}, f32[16,768]{1,0:T(8,128)}, f32[16,256]{1,0:T(8,128)}, f32[192,768]{1,0:T(8,128)}, /*in...) custom-call(bf16[1024,768]{1,0:T(8,128)(2,1)} %get-tuple-element.94.refs_0_, ...), custom_call_target="tpu_custom_call" | custom-call | tf_op jit(solution)/shard_map/pallas_call | solution.py:1381
  502.4 2.3 pad_maximum_fusion
  504.6 0.6 fusion.11
  505.2 0.6 slice.161
  505.8 1.4 slice.153
  507.2 0.6 slice.160
  507.9 0.6 copy.59
  508.5 0.7 reduce_sum.9
  509.2 0.6 pad_maximum_fusion.3
  509.9 0.7 copy.51
  510.6 1.1 pad_maximum_fusion.1
  511.7 1.1 maximum_bitcast_fusion
  512.8 0.7 copy-done.4
  513.5 1.1 copy.62
  514.7 0.8 copy-done.5
  515.5 1.1 copy.63
  (63 shorter events, 1.7 us)
Async XLA Ops:
  0.6 17.3 %copy-start.6 = (bf16[2,768,192]{1,2,0:T(8,128)(2,1)S(1)}, bf16[2,768,192]{1,2,0:T(8,128)(2,1)}, u32[]{:S(2)}) copy-start(bf16[2,768,192]{1,2,0:T(8,128)(2,1)} %param.22) | copy-start | bytes 1769476
  14.6 4.2 copy-start.7
  14.6 4.2 copy-start.8
  252.8 6.6 %copy-start.1 = (bf16[1024,1536]{1,0:T(8,128)(2,1)S(1)}, bf16[1024,1536]{1,0:T(8,128)(2,1)}, u32[]{:S(2)}) copy-start(bf16[1024,1536]{1,0:T(8,128)(2,1)} %get-tuple-element.84.rows_ref.refs_21_) | copy-start | bytes 9437188
  252.8 6.6 %copy-start.3 = (bf16[1024,768]{1,0:T(8,128)(2,1)S(1)}, bf16[1024,768]{1,0:T(8,128)(2,1)}, u32[]{:S(2)}) copy-start(bf16[1024,768]{1,0:T(8,128)(2,1)} %get-tuple-element.111.refs_8_) | copy-start | bytes 4718596
  379.5 6.6 %copy-start = (bf16[1024,1536]{1,0:T(8,128)(2,1)S(1)}, bf16[1024,1536]{1,0:T(8,128)(2,1)}, u32[]{:S(2)}) copy-start(bf16[1024,1536]{1,0:T(8,128)(2,1)} %get-tuple-element.78.refs_0_.refs_21_) | copy-start | bytes 9437188
  379.5 6.6 %copy-start.2 = (bf16[1024,768]{1,0:T(8,128)(2,1)S(1)}, bf16[1024,768]{1,0:T(8,128)(2,1)}, u32[]{:S(2)}) copy-start(bf16[1024,768]{1,0:T(8,128)(2,1)} %get-tuple-element.119.refs_8_) | copy-start | bytes 4718596
  390.0 112.3 %copy-start.11 = (f32[192,768]{1,0:T(8,128)S(1)}, f32[192,768]{1,0:T(8,128)}, u32[]{:S(2)}) copy-start(f32[192,768]{1,0:T(8,128)} %get-tuple-element.130) | copy-start | bytes 1769476
  502.3 2.4 copy-start.18
  502.3 2.9 copy-start.19
  502.3 6.9 %copy-start.16 = (f32[48,256]{1,0:T(8,128)S(1)}, f32[48,256]{1,0:T(8,128)}, u32[]{:S(2)}) copy-start(f32[48,256]{1,0:T(8,128)} %get-tuple-element.134) | copy-start | bytes 147460
  502.3 6.9 %copy-start.17 = (f32[48,256]{1,0:T(8,128)S(1)}, f32[48,256]{1,0:T(8,128)}, u32[]{:S(2)}) copy-start(f32[48,256]{1,0:T(8,128)} %get-tuple-element.133) | copy-start | bytes 147460
  502.3 7.5 %copy-start.14 = (f32[192,128]{1,0:T(8,128)S(1)}, f32[192,128]{1,0:T(8,128)}, u32[]{:S(2)}) copy-start(f32[192,128]{1,0:T(8,128)} %get-tuple-element.136) | copy-start | bytes 294916
  502.3 7.5 %copy-start.15 = (f32[192,128]{1,0:T(8,128)S(1)}, f32[192,128]{1,0:T(8,128)}, u32[]{:S(2)}) copy-start(f32[192,128]{1,0:T(8,128)} %get-tuple-element.135) | copy-start | bytes 294916
  502.4 8.2 %copy-start.10 = (f32[192,768]{1,0:T(8,128)S(1)}, f32[192,768]{1,0:T(8,128)}, u32[]{:S(2)}) copy-start(f32[192,768]{1,0:T(8,128)} %get-tuple-element.132) | copy-start | bytes 1769476
  502.4 8.2 %copy-start.13 = (f32[192,768]{1,0:T(8,128)S(1)}, f32[192,768]{1,0:T(8,128)}, u32[]{:S(2)}) copy-start(f32[192,768]{1,0:T(8,128)} %get-tuple-element.131) | copy-start | bytes 1769476
  509.2 2.5 copy-start.9
  509.2 2.5 copy-start.12
  511.7 1.8 copy-start.4
  513.5 2.0 copy-start.5

commit v5 on v4

--- a/solution.py
+++ b/solution.py
@@ -4,6 +4,7 @@
 
 import jax
 import jax.numpy as jnp
+import numpy as np
 from jax import lax
 from jax.experimental import pallas as pl
 from jax.experimental.pallas import tpu as pltpu
@@ -15,6 +16,7 @@
 CHUNK = 256
 LANES = 128
 TAPS = 4
+STEPS = 16
 
 highest = lax.Precision.HIGHEST
 epsilon = 1e-05
@@ -64,6 +66,11 @@
     decay_out = jnp.exp(last - cum) * aux[:, 5:6]
     decay_pass = jnp.exp(last) * aux[0:1, 6:7]
     return step, cum, decay_in, decay_out, decay_pass
+
+
+def step_weights(blocks):
+    joined = jnp.concatenate([blocks[n] for n in range(blocks.shape[0])], axis=1)
+    return jnp.concatenate([joined, jnp.zeros((LANES - STEPS, joined.shape[1]), BF16)], axis=0)
 
 
 def forward_kernel(
@@ -89,14 +96,15 @@
     step_ref,
     mixed_ref,
     sin_ref,
+    full_ref,
     ext_x,
     ext_bc,
     state,
     gg_ref,
-    hook=None,
+    gate_raw,
+    hook,
 ):
     inner = wx_ref.shape[1]
-    hook = hook or (lambda slot: None)
 
     @pl.when(pl.program_id(0) == 0)
     def _():
@@ -126,14 +134,14 @@
         iota2((CHUNK, CHUNK), 0) >= iota2((CHUNK, CHUNK), 1)
     )
     coupling = jnp.where(visible, mm_nt(query, keys), 0.0)
-    step_raw = mm(rows, wdt_ref[...])
+    step_raw = mm_nt(rows, step_weights(wdt_ref))
     step_ref[...] = step_raw
     step, cum, decay_in, decay_out, decay_pass = decays(
         step_raw + heads_ref[0:1, :], rate, aux
     )
     cum_t = jnp.transpose(cum)
     ext_x[8 : 8 + CHUNK, :] = mm(rows, wx_ref[...])
-    gate_ref[...] = mm(rows, wz_ref[...])
+    gate_raw[...] = mm(rows, wz_ref[...])
     hook(1)
     squares = jnp.zeros((CHUNK, LANES), F32)
     half = iota2((CHUNK, LANES), 1) < P_SIZE
@@ -163,8 +171,11 @@
         mixed_ref[:, cols] = mixed
         leaving = (scaled.astype(F32) * pair_of(decay_out, head)).astype(BF16)
         state[:, cols] = pair_of(decay_pass, head) * before + mm(keys_t, leaving)
-        gate = gate_ref[:, cols]
-        gated = (mixed + wide_ref[0:1, cols] * act) * (gate * sigmoid(gate))
+        gate = gate_raw[:, cols]
+        gate_ref[:, cols] = gate.astype(BF16)
+        full = mixed + wide_ref[0:1, cols] * act
+        full_ref[:, cols] = full.astype(BF16)
+        gated = full * (gate * sigmoid(gate))
         squares = squares + gated * gated
         gg_ref[:, cols] = (gated * wide_ref[1:2, cols]).astype(BF16)
         hook(2 + pair)
@@ -177,8 +188,7 @@
     top_ref,
     sc_ref,
     gate_ref,
-    iconv_ref,
-    mixed_ref,
+    full_ref,
     wout_ref,
     wide_ref,
     ggate_ref,
@@ -200,44 +210,40 @@
     for pair in range(inner // LANES):
         cols = slice(pair * LANES, (pair + 1) * LANES)
         gain = wide_ref[1:2, cols]
-        conv = iconv_ref[:, cols]
-        act = conv * sigmoid(conv)
-        gate = gate_ref[:, cols]
+        gate = gate_ref[:, cols].astype(F32)
         gate_sig = sigmoid(gate)
         gate_act = gate * gate_sig
-        full = mixed_ref[:, cols] + wide_ref[0:1, cols] * act
+        full = full_ref[:, cols].astype(F32)
         gated = full * gate_act
         gno = gno_ref[:, cols]
         gated_scaled = gated * scale
         small_ref[4:5, cols] += jnp.sum(gno * gated_scaled, axis=0, keepdims=True)
         outlow_ref[:, cols] = (gated_scaled * gain).astype(BF16)
         ggated = scale * (gno * gain) - gated * coef
-        gout_low = (ggated * gate_act).astype(BF16)
-        gout_ref[:, cols] = gout_low
+        gout_ref[:, cols] = (ggated * gate_act).astype(BF16)
         ggate_ref[:, cols] = (
             ggated * full * (gate_sig * (1.0 + gate * (1.0 - gate_sig)))
         ).astype(BF16)
-        small_ref[5:6, cols] += jnp.sum(gout_low.astype(F32) * act, axis=0, keepdims=True)
-
-
-def gate_back(top_all, per_row, saved, weight_out, wide):
+
+
+def gate_back(layer, top_all, per_row, saved, weight_out, wide):
     length, width = top_all.shape
     inner = weight_out.shape[1]
-    gate, iconv, mixed = saved[0], saved[2], saved[6]
+    gate, full = saved[0], saved[8]
     shape = jax.ShapeDtypeStruct
     return pl.pallas_call(
         gate_back_kernel,
         grid=(length // CHUNK,),
         in_specs=[block_rows(width), pl.BlockSpec((8, CHUNK), lambda i: (0, i))]
-        + [block_rows(inner)] * 3
-        + [whole_spec(weight_out.shape), whole_spec(wide.shape)],
+        + [block_rows(inner)] * 2
+        + [whole_spec(weight_out.shape), layer_spec(layer, wide.shape)],
         out_specs=[block_rows(inner)] * 3 + [pl.BlockSpec((8, inner), lambda i: (0, 0))],
         out_shape=[shape((length, inner), BF16)] * 3 + [shape((8, inner), F32)],
         scratch_shapes=[pltpu.VMEM((CHUNK, inner), F32)],
         compiler_params=pltpu.CompilerParams(
             dimension_semantics=("arbitrary",), vmem_limit_bytes=VMEM_LIMIT
         ),
-    )(top_all, per_row, gate, iconv, mixed, weight_out, wide)
+    )(top_all, per_row, gate, full, weight_out, wide)
 
 
 def mix_back_kernel(
@@ -319,6 +325,7 @@
         scaled = (act * step_pair).astype(BF16)
         gout_low = gout_ref[:, cols]
         gout = gout_low.astype(F32)
+        small_ref[5:6, cols] += jnp.sum(gout * act, axis=0, keepdims=True)
         zero = jnp.zeros_like(gout)
         parts = []
         for one, own in (
@@ -385,7 +392,7 @@
     gext_bc[CHUNK : CHUNK + 8, :] = gext_bc[0:8, :]
     hook(7)
     total = mm_nt(ggate_ref[...], wz_ref[...]) + mm_nt(ginner_ref[...], wx_ref[...])
-    total = total + mm_nt(gstep_ref[...], wdt_ref[...])
+    total = total + mm(gstep_ref[...], step_weights(wdt_ref))
     part_ref[...] = (total + mm_nt(gshared_ref[...], wbc_ref[...])).astype(BF16)
 
 
@@ -394,6 +401,14 @@
     return pl.BlockSpec(shape, lambda i: zeros, pipeline_mode=pl.Buffered(1))
 
 
+def layer_spec(layer, shape):
+    return pl.BlockSpec(
+        (None, *shape[1:]),
+        lambda i: (layer,) + (0,) * (len(shape) - 1),
+        pipeline_mode=pl.Buffered(1),
+    )
+
+
 VMEM_LIMIT = 62 * 1024 * 1024
 
 
@@ -401,11 +416,11 @@
     return pl.BlockSpec((CHUNK, cols), lambda i: (i, 0))
 
 
-def forward_in_specs(rows_all, weights, layer_args):
+def forward_in_specs(layer, rows_all, weights, layer_args):
     return (
         [block_rows(rows_all.shape[1])]
         + [whole_spec(w.shape) for w in weights]
-        + [whole_spec(w.shape) for w in layer_args]
+        + [layer_spec(layer, w.shape) for w in layer_args]
         + [block_rows(LANES), pl.BlockSpec((8, CHUNK), lambda i: (0, i))]
     )
 
@@ -420,13 +435,14 @@
         block_rows(LANES),
         block_rows(inner),
         pl.BlockSpec((1, N, inner), lambda i: (i, 0, 0)),
+        block_rows(inner),
     ]
 
 
 def saved_shapes(length, inner):
     shape = jax.ShapeDtypeStruct
     return [
-        shape((length, inner), F32),
+        shape((length, inner), BF16),
         shape((length, inner), BF16),
         shape((length, inner), F32),
         shape((length, 2 * N), F32),
@@ -434,6 +450,7 @@
         shape((length, LANES), F32),
         shape((length, inner), F32),
         shape((length // CHUNK, N, inner), F32),
+        shape((length, inner), BF16),
     ]
 
 
@@ -443,32 +460,11 @@
         pltpu.VMEM((CHUNK + 8, 2 * N), F32),
         pltpu.VMEM((N, inner), F32),
         pltpu.VMEM((CHUNK, inner), BF16),
+        pltpu.VMEM((CHUNK, inner), F32),
     ]
 
 
-def forward_layer(rows_all, weights, layer_args, aux, segrow):
-    length, width = rows_all.shape
-    inner = weights[1].shape[1]
-    shape = jax.ShapeDtypeStruct
-    return pl.pallas_call(
-        forward_kernel,
-        grid=(length // CHUNK,),
-        in_specs=forward_in_specs(rows_all, weights, layer_args),
-        out_specs=[block_rows(width), pl.BlockSpec((8, CHUNK), lambda i: (0, i))]
-        + saved_specs(inner),
-        out_shape=[shape((length, width), BF16), shape((8, length), F32)]
-        + saved_shapes(length, inner),
-        scratch_shapes=forward_scratch(inner),
-        compiler_params=pltpu.CompilerParams(
-            dimension_semantics=("arbitrary",), vmem_limit_bytes=VMEM_LIMIT
-        ),
-        cost_estimate=pl.CostEstimate(
-            flops=length * width * inner * 7, bytes_accessed=40_000_000, transcendentals=8_000_000
-        ),
-    )(rows_all, *weights, *layer_args, aux, segrow)
-
-
-def mix_back_specs(chunks, inner, weights, layer_args, spread):
+def mix_back_specs(layer, chunks, inner, weights, layer_args, spread):
     last = chunks - 1
 
     def turned(cols):
@@ -488,7 +484,7 @@
             turned(inner),
         ]
         + [whole_spec(w.shape) for w in weights]
-        + [whole_spec(w.shape) for w in layer_args]
+        + [layer_spec(layer, w.shape) for w in layer_args]
         + [
             whole_spec(spread.shape),
             turned(LANES),
@@ -534,18 +530,18 @@
     return aux, jnp.broadcast_to(seg[None, :], (8, length))
 
 
-def layer_parameters(layer, conv_x, conv_bc, a_log, dt_bias, d_skip, gated_gain):
+def layer_parameters(conv_x, conv_bc, a_log, dt_bias, d_skip, gated_gain):
     heads = a_log.shape[1]
-    pad = ((0, 0), (0, LANES - heads))
-    head_rows = jnp.pad(jnp.stack([dt_bias[layer], -jnp.exp(a_log[layer])]), pad)
-    wide = jnp.stack([jnp.repeat(d_skip[layer], P_SIZE), gated_gain[layer]])
-    return (conv_x[layer], conv_bc[layer], head_rows, wide)
+    pad = ((0, 0), (0, 0), (0, LANES - heads))
+    head_rows = jnp.pad(jnp.stack([dt_bias, -jnp.exp(a_log)], axis=1), pad)
+    wide = jnp.stack([jnp.repeat(d_skip, P_SIZE, axis=1), gated_gain], axis=1)
+    return (conv_x, conv_bc, head_rows, wide)
 
 
 def head_spread(inner):
-    return (
-        jnp.arange(inner)[:, None] // P_SIZE == jnp.arange(LANES)[None, :]
-    ).astype(BF16)
+    return jnp.asarray(
+        np.arange(inner)[:, None] // P_SIZE == np.arange(LANES)[None, :], dtype=BF16
+    )
 
 
 MESH = pl.DeviceIdType.MESH
@@ -554,9 +550,11 @@
 PIECES = 4
 TENSOR = 4
 LATE = 1e9
-LAG = 8.0
+LAG = 14.0
+EIGHTHS = 8
 BIG = 6.5
 SMALL = 1.1
+TINY = 0.2
 
 
 class Place:
@@ -609,8 +607,8 @@
         self.steps = []
         self.rolling = []
 
-    def follow(self, slot, step):
-        self.rolling.append((slot, step))
+    def follow(self, eighths, step):
+        self.rolling.append((eighths, step))
 
     def add(self, when, step):
         self.steps.append((when, len(self.steps), step))
@@ -622,12 +620,13 @@
         for _, _, step in self.ordered():
             step()
 
-    def spread(self, chunks, slots, chunk_us, order=lambda k: k):
+    def spread(self, chunks, slots, chunk_us, order=lambda k: k, lag=LAG):
         places = {}
-        for slot, step in self.rolling:
+        rolling = [(-(-offset * slots // EIGHTHS), step) for offset, step in self.rolling]
+        for slot, step in rolling:
             for k in range(chunks):
                 if (k + 1) * slots + slot >= chunks * slots:
-                    when = ((k + 1) * slots + slot) * chunk_us / slots + (LAG if slot > 3 else 0.0)
+                    when = ((k + 1) * slots + slot) * chunk_us / slots + (lag if 2 * slot > slots else 0.0)
                     self.add(when, functools.partial(step, order(k)))
         after = []
         for when, _, step in self.ordered():
@@ -638,7 +637,10 @@
                 after.append(step)
         now = pl.program_id(0)
 
-        def hook(slot):
+        def hook(place):
+            if place * slots % EIGHTHS:
+                return
+            slot = place * slots // EIGHTHS
             for chunk in range(chunks):
                 steps = places.get((slot, chunk))
                 if steps:
@@ -648,10 +650,10 @@
                         for step in steps:
                             step()
 
-            for offset, step in self.rolling:
+            for offset, step in rolling:
                 if offset % slots == slot:
-                    lag = 1 + offset // slots
-                    step(jnp.where(now >= lag, order(now - lag), -1))
+                    behind = 1 + offset // slots
+                    step(jnp.where(now >= behind, order(now - behind), -1))
 
         def end():
             @pl.when(now == chunks - 1)
@@ -828,11 +830,13 @@
         timeline.add(0.0, begin(i))
         if route == "xz":
             timeline.add(plan["side", i], side(i))
-        for k in range(1, line):
-            for way in (0, 1):
-                for column, xs in enumerate((place.x,) if route == "zx" else (place.x, place.other)):
+        for way in (0, 1):
+            for column, xs in enumerate((place.x,) if route == "zx" else (place.x, place.other)):
+                when = plan["side", i] if column else 0.0
+                for k in range(1, line):
+                    when = max(plan["hop", i, way, k, column], when + 0.01)
                     arrive, finish = hop(i, way, k, xs, route == "zx")
-                    timeline.add(plan["hop", i, way, k, column], arrive)
+                    timeline.add(when, arrive)
                     timeline.add(LATE, finish)
         if route == "zx":
             timeline.add(plan["side", i] + 1.0 if early else LATE, settle(i))
@@ -1059,22 +1063,29 @@
     plan = plan_scatter([item[4:] for item in items], line)
     for i, (_, _, _, _, route, _, ready) in enumerate(items):
         columns = (0,) if route == "xz" else (0, 1)
+        latest = ready
         for zz in scatter_order(line):
             if route == "xz":
                 timeline.add(ready, lambda i=i, zz=zz: side(i, zz).start())
                 timeline.add(plan["join", i, zz], join(i, zz))
+                latest = max(latest, plan["join", i, zz])
             for xs in columns:
                 for way, name in enumerate("rl"):
+                    when = plan.get(("join", i, zz), ready)
                     for h in range(zz if way == 0 else line - 1 - zz):
-                        timeline.add(plan["send", i, zz, name, xs, h], send(i, zz, way, xs, h))
+                        when = max(plan["send", i, zz, name, xs, h], when + 0.01)
+                        timeline.add(when, send(i, zz, way, xs, h))
+                    latest = max(latest, when)
                 timeline.add(LATE, end(i, zz, xs))
+        latest += 0.01
         if route == "xz":
-            timeline.add(plan["last", i], last(i))
+            timeline.add(max(plan["last", i], latest), last(i))
             continue
+        swaps = max(plan["swap", i], latest) + ADD_US
         for xs in columns:
-            timeline.add(plan["line", i, xs], gather_line(i, xs))
-        timeline.add(plan["swap", i] + ADD_US, lambda i=i: swap(i).start())
-        timeline.add(plan["last", i], swap_end(i))
+            timeline.add(max(plan["line", i, xs], latest), gather_line(i, xs))
+        timeline.add(swaps, lambda i=i: swap(i).start())
+        timeline.add(max(plan["last", i], swaps + 0.01), swap_end(i))
 
 
 def spread_semaphores():
@@ -1128,71 +1139,7 @@
     return [pltpu.SemaphoreType.DMA((PIECES,))] * 6
 
 
-def reduce_rows(place, timeline, part, lands, sems, owner, rate, start=0.0):
-    land_far, land_near, land_mate = lands
-    send_a, recv_a, send_b, recv_b, send_z, recv_z = sems
-    rows = land_far.shape[0]
-    step = rows // PIECES
-
-    def at(block, p):
-        return part.at[pl.ds(pl.multiple_of(block * rows, rows) + p * step, step), :]
-
-    def own(ref, p):
-        return ref.at[pl.ds(p * step, step), :]
-
-    def far(p):
-        return remote(
-            at(place.diagonal, p), own(land_far, p), send_a.at[p], recv_a.at[p], (place.dp, place.sibling)
-        )
-
-    def near(p):
-        return remote(
-            at(place.sibling, p), own(land_near, p), send_b.at[p], recv_b.at[p], (place.dp, place.sibling)
-        )
-
-    def over(p):
-        return remote(
-            own(land_far, p), own(land_mate, p), send_z.at[p], recv_z.at[p], (place.dp, place.mate)
-        )
-
-    def begin():
-        for p in range(PIECES):
-            far(p).start()
-        for p in range(PIECES):
-            near(p).start()
-
-    def middle(p):
-        def run():
-            far(p).wait_recv()
-            mine = own(land_far, p)
-            mine[...] = (mine[...].astype(F32) + at(place.mate, p)[...].astype(F32)).astype(BF16)
-            over(p).start()
-
-        return run
-
-    def final(p):
-        def run():
-            near(p).wait_recv()
-            over(p).wait_recv()
-            sums = at(place.t, p)[...].astype(F32) + own(land_near, p)[...].astype(F32)
-            owner(p, sums + own(land_mate, p)[...].astype(F32))
-
-        return run
-
-    def finish():
-        for p in range(PIECES):
-            far(p).wait_send()
-            near(p).wait_send()
-            over(p).wait_send()
-
-    timeline.add(start, begin)
-    for p in range(PIECES):
-        timeline.add(start + 1.0 * (p + 1), middle(p))
-        timeline.add(start + 2.0 + rate * (p + 1), final(p))
-    timeline.add(LATE, finish)
-
-
-def roll_rows(place, timeline, part, lands, sems, owner, forward):
+def roll_rows(place, timeline, part, lands, sems, owner, forward, slot=4):
     land_far, land_near, land_mate = lands
     send_a, recv_a, send_b, recv_b, send_z, recv_z = sems
     rows = land_far.shape[0]
@@ -1260,9 +1207,9 @@
     timeline.follow(0, begin)
     for p in range(PIECES):
         timeline.follow(1 + p // 2, functools.partial(middle, p))
-        timeline.follow(4 + 3 * p, functools.partial(final, p))
+        timeline.follow(slot + 3 * p, functools.partial(final, p))
         if forward:
-            timeline.follow(8 + 3 * p, functools.partial(pass_on, p))
+            timeline.follow(slot + 4 + 3 * p, functools.partial(pass_on, p))
     timeline.add(LATE, finish)
 
 
@@ -1303,14 +1250,15 @@
     bc_own, bc_all = refs[4], wholes[4]
     rows = refs[0].shape[0]
     head, tail = halves(rows)
-    pieces = [by_rows_piece(whole, rows) for whole in wholes[:4]]
+    pieces = [by_rows_piece(whole, rows) for whole in wholes[:3]]
+    step_all = wholes[3]
 
     def bc_piece(zz, xs):
         return bc_all.at[zz * 2 + xs, place.t]
 
     items = [
         (bc_own, bc_piece, "zx", SMALL / 2, True),
-        (refs[3], pieces[3], "zx", SMALL, False),
+        (refs[3], lambda zz, xs: step_all.at[zz * 2 + xs], "zx", TINY, False),
         (refs[1], pieces[1], "zx", BIG, False),
         (refs[0], pieces[0], "zx", BIG, False),
         (refs[2].at[pl.ds(0, head), :], by_rows_piece(wholes[2], rows, 0, head), "xz", BIG / 2, False),
@@ -1334,7 +1282,7 @@
         shape((width, inner), BF16),
         shape((width, inner), BF16),
         shape((width, inner), BF16),
-        shape((width, LANES), BF16),
+        shape((dp, STEPS, width // dp), BF16),
         shape((dp, TENSOR, width // (dp * TENSOR), 2 * N), BF16),
     ]
 
@@ -1351,6 +1299,7 @@
     place = Place(line)
     place.greet()
     timeline = Timeline()
+    own = [ref.at[0] for ref in own]
     weight_gather(place, timeline, own, wholes, sems, share_sems, own_sems)
     rows = normed.shape[0]
     block = pl.ds(pl.multiple_of(place.t * rows, rows), rows)
@@ -1361,7 +1310,7 @@
 
     def prepare():
         state = resid[...].astype(F32)
-        normed[...] = (state * row_norm(state) * gain[...]).astype(BF16)
+        normed[...] = (state * row_norm(state) * gain[0:1, :]).astype(BF16)
         low[...] = cotangent[...].astype(BF16)
         for copy in local_copies:
             copy.start()
@@ -1393,7 +1342,7 @@
 
 def start_layer(line, resid, cotangent, gain, own):
     rows, width = resid.shape
-    inner = own[0].shape[1]
+    inner = own[0].shape[2]
     shape = jax.ShapeDtypeStruct
     outs = gather_outputs(line, width, inner, 2 * line) + [
         shape((rows * TENSOR, width), BF16),
@@ -1412,41 +1361,51 @@
     )
 
 
-def scale_steps(place, timeline, sq, land, scale_row, scale_col, sems, inner_all, start=0.0):
+def scale_steps(place, timeline, sq, land, scale_row, scale_col, sems, inner_all):
     rows = scale_col.shape[0]
 
     def at(owner):
         return sq.at[:, pl.ds(pl.multiple_of(owner * rows, rows), rows)]
 
+    peers = (place.sibling, place.mate, place.diagonal)
     copies = share_blocks(place, at, lambda n: land.at[n], sems)
 
-    def arrive():
+    def begin(chunk):
+        for peer, copy in zip(peers, copies):
+            pl.when(peer == chunk)(copy.start)
+
+    def arrive(chunk):
+        @pl.when(place.t == chunk)
+        def _():
+            for copy in copies:
+                copy.wait_recv()
+            squares = at(place.t)[...] + land[0] + land[1] + land[2]
+            scale = lax.rsqrt(squares / inner_all + epsilon)
+            scale_row[...] = scale
+            scale_col[...] = jnp.transpose(scale)
+
+    def finish():
         for copy in copies:
-            copy.wait()
-        squares = at(place.t)[...] + land[0] + land[1] + land[2]
-        scale = lax.rsqrt(squares / inner_all + epsilon)
-        scale_row[...] = scale
-        scale_col[...] = jnp.transpose(scale)
-
-    timeline.add(start - 0.5, lambda: [copy.start() for copy in copies] and None)
-    timeline.add(start + 1.5, arrive)
-
-
-RATE_SHARED = 8.8
-RATE = 4.4
-
-
-SLOTS = 8
+            copy.wait_send()
+
+    timeline.follow(0, begin)
+    timeline.follow(FORWARD_SLOT - 1, arrive)
+    timeline.add(LATE, finish)
+
+
+FORWARD_SLOTS = 8
+BACKWARD_SLOTS = 8
 FORWARD_US = 6.7
+FORWARD_SLOT = 8
 
 
 def middle_kernel(line, inner_all, *refs):
     work, refs = refs[:12], refs[12:]
     (resid, gain), own, refs = refs[:2], refs[2:7], refs[7:]
-    saved, refs = refs[:8], refs[8:]
+    saved, refs = refs[:9], refs[9:]
     state_out, raw_out, scale_row, rows_all, refs = *refs[:4], refs[4:]
     wholes, refs = refs[:5], refs[5:]
-    scratch, refs = refs[:4], refs[4:]
+    scratch, refs = refs[:5], refs[5:]
     part, sq, far, near, mate, land, scale_col, normed = refs[:8]
     refs = refs[8:]
     sems, share_sems, own_sems = refs[:5], refs[5:7], refs[7]
@@ -1456,8 +1415,7 @@
     place = Place(line)
     pl.when(chunk == 0)(place.greet)
     timeline = Timeline()
-    done = FORWARD_US * chunks + 1.0
-    scale_steps(place, timeline, sq, land, scale_row, scale_col, sq_sems, inner_all, done)
+    scale_steps(place, timeline, sq, land, scale_row, scale_col, sq_sems, inner_all)
     rows = normed.shape[0]
     step = rows // PIECES
     begin, forward, finish = spread_rows(place, normed, rows_all, rows_sems)
@@ -1467,19 +1425,20 @@
         raw_out[part_rows, :] = sums
         state = resid[part_rows, :].astype(F32) + sums * scale_col[part_rows, 0:1]
         state_out[part_rows, :] = state
-        normed[part_rows, :] = (state * row_norm(state) * gain[...]).astype(BF16)
+        normed[part_rows, :] = (state * row_norm(state) * gain[1:2, :]).astype(BF16)
         begin(p)
 
-    reduce_rows(place, timeline, part, (far, near, mate), reduce_sems, owner, RATE, done)
+    roll_rows(
+        place, timeline, part, (far, near, mate), reduce_sems, owner, forward, FORWARD_SLOT
+    )
+    own = [ref.at[1] for ref in own]
     weight_gather(place, timeline, own, wholes, sems, share_sems, own_sems)
-    for p in range(PIECES):
-        timeline.add(done + 3.0 + RATE * (PIECES + 1 + p), functools.partial(forward, p))
     block = pl.ds(pl.multiple_of(place.t * rows, rows), rows)
     keep = pltpu.make_async_copy(normed, rows_all.at[block, :], local.at[0])
-    timeline.add(done + 3.0 + RATE * PIECES, keep.start)
+    timeline.add(LATE, keep.start)
+    timeline.add(LATE, finish)
     timeline.add(LATE, keep.wait)
-    timeline.add(LATE, finish)
-    hook, end = timeline.spread(chunks, SLOTS, FORWARD_US)
+    hook, end = timeline.spread(chunks, FORWARD_SLOTS, FORWARD_US)
     at = pl.multiple_of(chunk * CHUNK, CHUNK)
     forward_kernel(
         *work, part.at[pl.ds(at, CHUNK), :], sq.at[:, pl.ds(at, CHUNK)], *saved, *scratch, hook=hook
@@ -1487,10 +1446,22 @@
     end()
 
 
+def row_scratch(length, rows, width):
+    return [
+        pltpu.VMEM((length, width), BF16),
+        pltpu.VMEM((8, length), F32),
+        pltpu.VMEM((rows, width), BF16),
+        pltpu.VMEM((rows, width), BF16),
+        pltpu.VMEM((rows, width), BF16),
+        pltpu.VMEM((3, 8, rows), F32),
+        pltpu.VMEM((rows, 8), F32),
+    ]
+
+
 def middle_layer(line, inner_all, rows_all, weights, layer_args, aux, segrow, resid, gain, own):
     rows, width = resid.shape
     length = rows_all.shape[0]
-    inner = own[0].shape[1]
+    inner = own[0].shape[2]
     shape = jax.ShapeDtypeStruct
     outs = (
         saved_shapes(length, inner)
@@ -1502,16 +1473,14 @@
         ]
         + gather_outputs(line, width, inner, 2 * line)
     )
-    scratch = forward_scratch(inner)
-    scratch += [pltpu.VMEM((length, width), BF16), pltpu.VMEM((8, length), F32)]
-    scratch += [pltpu.VMEM((rows, width), BF16)] * 3
-    scratch += [pltpu.VMEM((3, 8, rows), F32), pltpu.VMEM((rows, 8), F32), pltpu.VMEM((rows, width), BF16)]
+    scratch = forward_scratch(inner) + row_scratch(length, rows, width)
+    scratch += [pltpu.VMEM((rows, width), BF16)]
     scratch += gather_scratch(line) + reduce_semaphores() + share_semaphores() + spread_semaphores()
     scratch += [pltpu.SemaphoreType.DMA((1,))]
     return call_kernel(
         functools.partial(middle_kernel, line, inner_all),
         outs,
-        forward_in_specs(rows_all, weights, layer_args)
+        forward_in_specs(0, rows_all, weights, layer_args)
         + [whole_spec(resid.shape), whole_spec(gain.shape)]
         + [ANY] * 5,
         saved_specs(inner)
@@ -1524,7 +1493,7 @@
     )
 
 
-def per_row_steps(place, timeline, scale_row, cross_col, stage, land, out, sems, inner_all, when):
+def per_row_steps(place, timeline, scale_row, cross_col, stage, land, out, sems, inner_all, slot):
     rows = cross_col.shape[0]
     copies = share_blocks(place, lambda peer: stage, lambda n: land.at[n], sems)
     peers = (place.sibling, place.mate, place.diagonal)
@@ -1546,20 +1515,21 @@
             copy.wait()
             out[:, pl.ds(pl.multiple_of(peer * rows, rows), rows)] = land[n]
 
-    if when is None:
-        timeline.follow(5 + 3 * (PIECES - 1), follow)
-    else:
-        timeline.add(when, send)
+    timeline.follow(slot + 1 + 3 * (PIECES - 1), follow)
     timeline.add(LATE, arrive)
 
 
-def top_kernel(
-    line, inner_all, part, sq, state, cotangent, hidden, per_row,
-    far, near, mate, sq_land, row_land, scale_col, scale_row, cross_col, stage, *refs
-):
-    reduce_sems, sq_sems, row_sems = refs[:6], refs[6:8], refs[8:10]
+def top_kernel(line, inner_all, *refs):
+    work, (state, cotangent), refs = refs[:12], refs[12:14], refs[14:]
+    saved, (hidden, per_row), refs = refs[:9], refs[9:11], refs[11:]
+    scratch, refs = refs[:5], refs[5:]
+    part, sq, far, near, mate, sq_land, scale_col = refs[:7]
+    row_land, scale_row, cross_col, stage = refs[7:11]
+    reduce_sems, sq_sems, row_sems = refs[11:17], refs[17:19], refs[19:21]
+    chunk = pl.program_id(0)
+    chunks = part.shape[0] // CHUNK
     place = Place(line)
-    place.greet(across=False)
+    pl.when(chunk == 0)(lambda: place.greet(across=False))
     timeline = Timeline()
     scale_steps(place, timeline, sq, sq_land, scale_row, scale_col, sq_sems, inner_all)
     step = cross_col.shape[0] // PIECES
@@ -1571,19 +1541,27 @@
         cross = jnp.sum(low * sums, axis=1, keepdims=True)
         cross_col[part_rows, :] = jnp.broadcast_to(cross, (step, LANES))
 
-    reduce_rows(place, timeline, part, (far, near, mate), reduce_sems, owner, RATE)
+    roll_rows(place, timeline, part, (far, near, mate), reduce_sems, owner, None, FORWARD_SLOT)
     per_row_steps(
-        place, timeline, scale_row, cross_col, stage, row_land, per_row, row_sems, inner_all, 1e3
-    )
-    timeline.run()
-
-
-def top_layer(line, inner_all, part, sq, state, cotangent):
+        place, timeline, scale_row, cross_col, stage, row_land, per_row, row_sems, inner_all,
+        FORWARD_SLOT,
+    )
+    hook, end = timeline.spread(chunks, FORWARD_SLOTS, FORWARD_US)
+    at = pl.multiple_of(chunk * CHUNK, CHUNK)
+    forward_kernel(
+        *work, part.at[pl.ds(at, CHUNK), :], sq.at[:, pl.ds(at, CHUNK)], *saved, *scratch, hook=hook
+    )
+    end()
+
+
+def top_layer(line, inner_all, rows_all, weights, layer_args, aux, segrow, state, cotangent):
     rows, width = state.shape
+    length = rows_all.shape[0]
+    inner = weights[0].shape[1]
     shape = jax.ShapeDtypeStruct
-    scratch = [pltpu.VMEM((rows, width), BF16)] * 3 + [pltpu.VMEM((3, 8, rows), F32)] * 2
+    scratch = forward_scratch(inner) + row_scratch(length, rows, width)
     scratch += [
-        pltpu.VMEM((rows, 8), F32),
+        pltpu.VMEM((3, 8, rows), F32),
         pltpu.VMEM((8, rows), F32),
         pltpu.VMEM((rows, LANES), F32),
         pltpu.VMEM((8, rows), F32),
@@ -1591,12 +1569,14 @@
     scratch += reduce_semaphores() + share_semaphores() * 2
     return call_kernel(
         functools.partial(top_kernel, line, inner_all),
-        [shape((rows, width), F32), shape((8, rows * TENSOR), F32)],
-        [IN_VMEM] * 4,
-        [IN_VMEM] * 2,
+        saved_shapes(length, inner) + [shape((rows, width), F32), shape((8, length), F32)],
+        forward_in_specs(1, rows_all, weights, layer_args)
+        + [whole_spec(state.shape), whole_spec(cotangent.shape)],
+        saved_specs(inner) + [whole_spec((rows, width)), whole_spec((8, length))],
         scratch,
         2,
-        (part, sq, state, cotangent),
+        (rows_all, *weights, *layer_args, aux, segrow, state, cotangent),
+        (length // CHUNK,),
     )
 
 
@@ -1605,7 +1585,13 @@
     return first, rows - first
 
 
+def thirds(rows):
+    first = max(rows // 64 * 16, 16)
+    return (first, *halves(rows - first))
+
+
 BACKWARD_US = 10.0
+END_LAG = 7.0
 DOTS_US = 6.0
 
 
@@ -1645,17 +1631,28 @@
     def shared(zz, xs):
         return bc_sum.at[zz * 2 + xs]
 
-    def step(ref):
-        return by_rows_piece(ref, rows)
+    def steps(zz, xs):
+        return grads[3].at[zz * 2 + xs]
+
+    count = thirds(rows)
+    starts = (0, count[0], count[0] + count[1])
+
+    def third(n):
+        return by_rows_piece(grads[2], rows, starts[n], count[n])
+
+    def inner_item(n, route):
+        out = outs[2].at[pl.ds(starts[n], count[n]), :]
+        return (third(n), third(n), lands[6 + 2 * n : 8 + 2 * n], out, route, BIG * count[n] / rows, late)
 
     items = [
         (low(grads[0]), low(early[0]), lands[0:2], outs[0].at[first, :], "zx", BIG / 2, 0.0),
         (high(grads[0]), high(early[0]), lands[2:4], outs[0].at[second, :], "xz", BIG / 2, 0.0),
-        (step(grads[1]), step(early[1]), lands[4:6], outs[1], "xz", BIG, 0.0),
-        (low(grads[2]), low(grads[2]), lands[6:8], outs[2].at[first, :], "xz", BIG / 2, late),
-        (high(grads[2]), high(grads[2]), lands[8:10], outs[2].at[second, :], "xz", BIG / 2, late),
-        (step(grads[3]), step(grads[3]), lands[10:12], outs[3], "xz", SMALL, late),
-        (shared, shared, lands[12:14], outs[4], "xz", SMALL / 2, bc_ready + 0.1),
+        (by_rows_piece(grads[1], rows), by_rows_piece(early[1], rows), lands[4:6], outs[1], "xz", BIG, 0.0),
+        inner_item(0, "zx"),
+        inner_item(1, "xz"),
+        inner_item(2, "xz"),
+        (steps, steps, lands[12:14], outs[3], "xz", TINY, late),
+        (shared, shared, lands[14:16], outs[4], "xz", SMALL / 2, bc_ready + 0.1),
     ]
     scatter_weights(place, timeline, items, sems)
 
@@ -1664,7 +1661,7 @@
     shape = jax.ShapeDtypeStruct
     rows = width // dp
     return [shape((rows, inner), F32)] * 3 + [
-        shape((rows, LANES), F32),
+        shape((STEPS, rows), F32),
         shape((rows // TENSOR, 2 * N), F32),
     ]
 
@@ -1678,13 +1675,20 @@
         pltpu.VMEM((1, head, inner), BF16),
         pltpu.VMEM((line + 1, 2, head, inner), BF16),
     ]
-    for count, cols in ((tail, inner), (rows, inner), (head, inner), (tail, inner), (rows, LANES), (fine, 2 * N)):
+    few, some, more = thirds(rows)
+    for count, cols in ((tail, inner), (rows, inner)):
+        scratch += [pltpu.VMEM((line, count, cols), BF16), pltpu.VMEM((line + 1, count, cols), BF16)]
+    scratch += [
+        pltpu.VMEM((1, few, inner), BF16),
+        pltpu.VMEM((line + 1, 2, few, inner), BF16),
+    ]
+    for count, cols in ((some, inner), (more, inner), (STEPS, rows), (fine, 2 * N)):
         scratch += [pltpu.VMEM((line, count, cols), BF16), pltpu.VMEM((line + 1, count, cols), BF16)]
     scratch += [
         pltpu.VMEM((3, dp, fine, 2 * N), BF16),
         pltpu.VMEM((dp, fine, 2 * N), BF16),
     ]
-    return scratch + scatter_semaphores(7, line) + share_semaphores()
+    return scratch + scatter_semaphores(8, line) + share_semaphores()
 
 
 def input_gradient(state, gain, before, sums):
@@ -1699,12 +1703,15 @@
     dp, tensor, fine, _ = dshared.shape
     tile = rows_all.shape[1] // 2
     per_tile = tile // (tensor * fine)
+    rows = tensor * fine
 
     def body(n, carry):
         part = pl.ds(pl.multiple_of(n * tile, tile), tile)
         left = rows_all[:, part]
         dinner[part, :] = contract(left, ginner[...])
-        dstep[part, :] = contract(left, gstep[...])
+        steps = contract_wide(gstep[...], left)[0:STEPS, :].astype(BF16)
+        for m in range(per_tile):
+            dstep[n * per_tile + m] = steps[:, m * rows : (m + 1) * rows]
         shared = contract_wide(left, gshared[...])
         for m in range(per_tile * tensor):
             block = shared[m * fine : (m + 1) * fine, :].astype(BF16)
@@ -1733,8 +1740,8 @@
     ]
     part, ginner, gstep, gshared, dinner, dstep, dshared = refs[:7]
     far, near, mate, refs = *refs[7:10], refs[10:]
-    lands, bc_land, bc_sum, sems, share_sems = refs[:14], refs[14], refs[15], refs[16:22], refs[22:24]
-    reduce_sems, refs = refs[24:30], refs[30:]
+    lands, bc_land, bc_sum, sems, share_sems = refs[:16], refs[16], refs[17], refs[18:24], refs[24:26]
+    reduce_sems, refs = refs[26:32], refs[32:]
     if final:
         small, small_bc, small_land, bc_land_sums, norm_land = refs[:5]
         small_send, small_recv = refs[5:]
@@ -1773,10 +1780,13 @@
     for n in (1, 2, 3, 4, 0):
         timeline.add(2.5 if n in (1, 2) else BACKWARD_US / 2, loads[n].wait)
 
+    def own_gain():
+        return gain[0:1, :] if final else gain[1:2, :]
+
     def owner(p, sums):
         part_rows = slice(p * step, (p + 1) * step)
         grad, column = input_gradient(
-            state[part_rows, :].astype(F32), gain[...], before[part_rows, :], sums
+            state[part_rows, :].astype(F32), own_gain(), before[part_rows, :], sums
         )
         grad_out[part_rows, :] = grad
         if final:
@@ -1801,7 +1811,7 @@
         timeline.add(LATE, keep.wait)
         timeline.add(LATE, finish)
         per_row_steps(
-            place, timeline, scale_row, cross_col, stage, row_land, per_row, row_sems, inner_all, None
+            place, timeline, scale_row, cross_col, stage, row_land, per_row, row_sems, inner_all, 4
         )
     grads = (dout, dgate, dinner, dstep, dshared)
     weight_scatter(
@@ -1837,7 +1847,7 @@
             timeline.add(start, send)
             timeline.add(end, take)
 
-        when = done + 17.0 + LAG
+        when = BACKWARD_US * (chunks + (4 + 3 * (PIECES - 1)) / EIGHTHS) + END_LAG + 0.5
         steps = [(len(bits), across[0], 3.0), (len(bits) + 1, across[1], 5.0)]
         steps += [(n, along[n], 7.0) for n in range(len(bits))][::-1]
         for n, partner, wait in steps:
@@ -1846,7 +1856,9 @@
                 group.append((2, small_sum, small_land))
             exchange(n, partner, group, when, when + wait)
             when += wait + 0.01
-    hook, end = timeline.spread(chunks, SLOTS, BACKWARD_US, lambda n: chunks - 1 - n)
+    hook, end = timeline.spread(
+        chunks, BACKWARD_SLOTS, BACKWARD_US, lambda n: chunks - 1 - n, END_LAG if final else LAG
+    )
     at = pl.ds(pl.multiple_of((chunks - 1 - chunk) * CHUNK, CHUNK), CHUNK)
     mix_back_kernel(
         *work,
@@ -1873,9 +1885,9 @@
     fine = width // (dp * TENSOR)
     steps = dp.bit_length() - 1
     shape = jax.ShapeDtypeStruct
-    _, iraw, iconv, sraw, sconv, step, mixed, sin = saved
+    _, iraw, iconv, sraw, sconv, step, mixed, sin, _ = saved
+    layer = 0 if final else 1
     far_side = (rows_all, dout, dgate, before, state)
-    whole = (gain, *more)
     if final:
         outs = [
             shape((rows, width), F32),
@@ -1905,7 +1917,7 @@
         pltpu.VMEM((length, LANES), BF16),
         pltpu.VMEM((length, 2 * N), BF16),
         pltpu.VMEM((width, inner), BF16),
-        pltpu.VMEM((width, LANES), BF16),
+        pltpu.VMEM((dp, STEPS, width // dp), BF16),
         pltpu.VMEM((dp, TENSOR, fine, 2 * N), BF16),
     ]
     scratch += [pltpu.VMEM((rows, width), BF16)] * 3
@@ -1932,15 +1944,16 @@
     return call_kernel(
         functools.partial(pull_kernel, line, inner_all, final),
         outs + tail_outs,
-        mix_back_specs(length // CHUNK, inner, weights, layer_args, spread)
+        mix_back_specs(layer, length // CHUNK, inner, weights, layer_args, spread)
         + [ANY] * 5
-        + [whole_spec(array.shape) for array in whole],
+        + [whole_spec(gain.shape)]
+        + [whole_spec(array.shape) for array in more],
         out_specs + [whole_spec(out.shape) for out in tail_outs],
         scratch,
         4 if final else 3,
         (
             iraw, iconv, sraw, sconv, step, mixed, sin, sin, *gates,
-            *weights, *layer_args, spread, aux, segrow, *far_side, *whole,
+            *weights, *layer_args, spread, aux, segrow, *far_side, gain, *more,
         ),
         (length // CHUNK,),
     )
@@ -1974,7 +1987,8 @@
     gated_gain,
 ):
     dp = lax.axis_size("dp")
-    assert lax.axis_size("tensor") == TENSOR and segment_ids.shape[0] == LEN and a_log.shape[0] == 2
+    assert lax.axis_size("tensor") == TENSOR and segment_ids.shape[0] == LEN
+    assert a_log.shape[0] == 2 and a_log.shape[1] <= STEPS
     line = dp // 2
     heads = a_log.shape[1]
     inner = heads * P_SIZE
@@ -1982,56 +1996,51 @@
     width = resid.shape[1]
     aux, segrow = row_masks(segment_ids)
     spread = head_spread(inner)
-    args = [
-        layer_parameters(layer, conv_x, conv_bc, a_log, dt_bias, d_skip, gated_gain)
-        for layer in range(2)
-    ]
-    own = [
-        (
-            w_z[layer],
-            w_x[layer],
-            jnp.transpose(w_out[layer]),
-            jnp.pad(w_dt[layer], ((0, 0), (0, LANES - heads))),
-            w_bc[layer],
-        )
-        for layer in range(2)
-    ]
-    gains = [norm_gain[layer : layer + 1] for layer in range(2)]
+    args = layer_parameters(conv_x, conv_bc, a_log, dt_bias, d_skip, gated_gain)
+    own = (
+        w_z,
+        w_x,
+        jnp.swapaxes(w_out, 1, 2),
+        jnp.pad(jnp.swapaxes(w_dt, 1, 2), ((0, 0), (0, STEPS - heads), (0, 0))),
+        w_bc,
+    )
+    gains = norm_gain
 
     def arranged(gathered):
         gate, inner_w, out_w, step_w, shared_w = gathered
         return gate, inner_w, shared_w.reshape(width, 2 * N), step_w, out_w
 
-    *gathered, rows_low, top_high = start_layer(line, resid, cotangent, gains[0], own[0])
+    *gathered, rows_low, top_high = start_layer(line, resid, cotangent, gains, own)
     weights_low = arranged(gathered)
     results = middle_layer(
-        line, inner_all, rows_low, weights_low, args[0], aux, segrow, resid, gains[1], own[1]
-    )
-    saved_low = results[:8]
-    state, raw, scale_row, rows_high, *gathered = results[8:]
+        line, inner_all, rows_low, weights_low, args, aux, segrow, resid, gains, own
+    )
+    saved_low = results[:9]
+    state, raw, scale_row, rows_high, *gathered = results[9:]
     weights_high = arranged(gathered)
-    part, sq, *saved_high = forward_layer(rows_high, weights_high, args[1], aux, segrow)
-    hidden, per_row = top_layer(line, inner_all, part, sq, state, cotangent)
-
-    def early_grads(rows_all, top_all, per_row, saved, weights, wide):
-        ggate, gout, outlow, small = gate_back(top_all, per_row, saved, weights[4], wide)
+    *saved_high, hidden, per_row = top_layer(
+        line, inner_all, rows_high, weights_high, args, aux, segrow, state, cotangent
+    )
+
+    def early_grads(layer, rows_all, top_all, per_row, saved, weights):
+        ggate, gout, outlow, small = gate_back(layer, top_all, per_row, saved, weights[4], args[3])
         return (ggate, gout), contract(top_all, outlow), contract(rows_all, ggate), small
 
     gates, dout, dgate, small_high_more = early_grads(
-        rows_high, top_high, per_row, saved_high, weights_high, args[1][3]
+        1, rows_high, top_high, per_row, saved_high, weights_high
     )
     results = pull_layer(
-        line, inner_all, saved_high, gates, weights_high, args[1], spread, aux, segrow, rows_high,
-        dout, dgate, cotangent, state, gains[1], (raw, scale_row), False,
+        line, inner_all, saved_high, gates, weights_high, args, spread, aux, segrow, rows_high,
+        dout, dgate, cotangent, state, gains, (raw, scale_row), False,
     )
     grad_state, gnorm_high, per_row, top_low, small_high, bc_high, *grads_high = results
     gates, dout, dgate, small_low_more = early_grads(
-        rows_low, top_low, per_row, saved_low, weights_low, args[0][3]
+        0, rows_low, top_low, per_row, saved_low, weights_low
     )
     more = (gnorm_high, small_low_more, small_high, small_high_more, bc_high)
     grad_resid, norm_sum, small, small_bc, *grads_low = pull_layer(
-        line, inner_all, saved_low, gates, weights_low, args[0], spread, aux, segrow, rows_low,
-        dout, dgate, grad_state, resid, gains[0], more, True,
+        line, inner_all, saved_low, gates, weights_low, args, spread, aux, segrow, rows_low,
+        dout, dgate, grad_state, resid, gains, more, True,
     )
     gout, gz, gx, gdt, gbc = [
         jnp.stack([low, high]) for low, high in zip(grads_low, grads_high)
@@ -2043,7 +2052,7 @@
         gz,
         gx,
         gbc,
-        gdt[:, :, :heads],
+        jnp.swapaxes(gdt[:, :heads], 1, 2),
         jnp.swapaxes(gout, 1, 2),
         norm_sum[:2],
         small[:, :TAPS],

time: 527 us -> 498 us (0.945)
  the two profiles are of different devices: /device:TPU:9 before, /device:TPU:0 now
where the time goes in v5:
time: 498 us; the launch traced here: 494 us
  Pallas kernels  448 us (90%)
  matrix products  21.2 us (4%)
  local copies, waits for them, and re-layouts  13 us (3%)
  other arithmetic  10.5 us (2%)
    pallas_call x5, Pallas kernels, call_kernel(): pl.pallas_call(kernel, grid=grid, out_shape=outs, in_specs=in_specs, out_...  431 us
    dot_general x4, matrix products, contract_wide(): lax.dot_general(left, right, (((0,), (0,)), ((), ())), preferred_element_...  21.2 us
    pallas_call x2, Pallas kernels, gate_back(): pl.pallas_call(gate_back_kernel, grid=(length // CHUNK,), in_specs=[block...  17.8 us

profile of v5, /device:TPU:0, one launch (start us, length us, event | category | flops | bytes accessed | tf_op | source)
XLA Modules:
  0.0 494.1 jit_solution(2951262452614349902)
XLA Ops:
  0.6 0.7 exponential_negate_fusion
  1.3 1.3 select_maximum_fusion.refs_8_.refs_16_
  2.6 0.7 convert_element_type.43
  3.3 0.1 slice.51
  3.4 0.1 compare_convert_fusion.2
  3.5 0.1 pad_maximum_fusion.5
  3.5 0.1 broadcast_bitcast_fusion.2
  3.6 0.1 broadcast_bitcast_fusion
  3.7 0.1 broadcast_bitcast_fusion.1
  3.8 0.7 stack.118
  4.5 0.1 fusion.10
  4.5 0.1 fusion.9
  4.6 0.1 fusion.11
  4.7 0.8 fusion.4
  5.5 0.2 stack.137
  5.7 0.7 copy.64
  6.4 0.6 pad.16.refs_3_.refs_17_
  7.0 0.7 broadcast_in_dim.17
  7.8 0.1 stack_reshape.4
  7.8 0.6 pad_maximum_fusion.4.refs_9_.wide_ref.refs_17_
  8.5 0.6 broadcast_in_dim.21.refs_11_.refs_20_
  9.1 0.2 copy.55
  9.3 0.8 pad.18.refs_10_.refs_19_
  10.1 81.1 %shard_map.263 = (bf16[1536,768]{1,0:T(8,128)(2,1)}, bf16[1536,768]{1,0:T(8,128)(2,1)}, bf16[1536,768]{1,0:T(8,128)(2,1)}, bf16[8,16,192]{2,1,0:T(8,128)(2,1)}, ...) custom-call(bf16[256,1536]{1,0:T(8,128)(2,1)} %refs_25_.1, ...), custom_call_target="tpu_custom_call" | custom-call | tf_op jit(solution)/shard_map/pallas_call | solution.py:1330
  91.2 86.9 %shard_map.264 = (bf16[1024,768]{1,0:T(8,128)(2,1)}, bf16[1024,768]{1,0:T(8,128)(2,1)}, f32[1024,768]{1,0:T(8,128)}, f32[1024,256]{1,0:T(8,128)}, f32[1024,256]{...) custom-call(bf16[1024,1536]{1,0:T(8,128)(2,1)} %get-tuple-element.78, ...), custom_call_target="tpu_custom_call" | custom-call | tf_op jit(solution)/shard_map/pallas_call | solution.py:1330
  178.1 57.3 %shard_map.265 = (bf16[1024,768]{1,0:T(8,128)(2,1)}, bf16[1024,768]{1,0:T(8,128)(2,1)}, f32[1024,768]{1,0:T(8,128)}, f32[1024,256]{1,0:T(8,128)}, f32[1024,256]{...) custom-call(bf16[1024,1536]{1,0:T(8,128)(2,1)} %get-tuple-element.84, ...), custom_call_target="tpu_custom_call" | custom-call | tf_op jit(solution)/shard_map/pallas_call | solution.py:1330
  235.4 8.9 %shard_map.266 = (bf16[1024,768]{1,0:T(8,128)(2,1)}, bf16[1024,768]{1,0:T(8,128)(2,1)}, bf16[1024,768]{1,0:T(8,128)(2,1)}, f32[8,768]{1,0:T(8,128)}) custom-call(bf16[1024,1536]{1,0:T(8,128)(2,1)} %get-tuple-element.106.top_ref, f32[8,1024]{1,0:T(8,128)} %get-tuple-element.107.sc_ref, bf16[1024,768]{1,0:T(8,128)(2,1)} %get-tuple-element.108.gate_ref, ...), custom_call_target="tpu_custom_call" | custom-call | tf_op jit(solution)/shard_map/pallas_call | solution.py:234
  244.3 6.6 %convolution_convert_fusion.3.refs_22_ = bf16[1536,768]{1,0:T(8,128)(2,1)} fusion(bf16[1024,1536]{1,0:T(8,128)(2,1)} %get-tuple-element.106.top_ref, bf16[1024,768]{1,0:T(8,128)(2,1)} %get-tuple-element.112), kind=kOutput, calls=%fused_computation.3 | convolution fusion | flops 2417098752 | bytes 7077888 | tf_op jit(solution)/shard_map/dot_general | solution.py:1963
  251.0 4.0 convolution_convert_fusion.2.refs_23_
  254.9 99.5 %shard_map.267 = (f32[256,1536]{1,0:T(8,128)}, f32[8,1536]{1,0:T(8,128)}, f32[8,1024]{1,0:T(8,128)}, bf16[1024,1536]{1,0:T(8,128)(2,1)}, f32[8,768]{1,0:T(8,128)...) custom-call(bf16[1024,768]{1,0:T(8,128)(2,1)} %get-tuple-element.99., ...), custom_call_target="tpu_custom_call" | custom-call | tf_op jit(solution)/shard_map/pallas_call | solution.py:1330
  354.4 8.9 %shard_map.268 = (bf16[1024,768]{1,0:T(8,128)(2,1)}, bf16[1024,768]{1,0:T(8,128)(2,1)}, bf16[1024,768]{1,0:T(8,128)(2,1)}, f32[8,768]{1,0:T(8,128)}) custom-call(bf16[1024,1536]{1,0:T(8,128)(2,1)} %get-tuple-element.115.top_ref, f32[8,1024]{1,0:T(8,128)} %get-tuple-element.116.sc_ref, bf16[1024,768]{1,0:T(8,128)(2,1)} %get-tuple-element.117.gate_ref, ...), custom_call_target="tpu_custom_call" | custom-call | tf_op jit(solution)/shard_map/pallas_call | solution.py:234
  363.3 6.6 %convolution_convert_fusion.1.refs_22_ = bf16[1536,768]{1,0:T(8,128)(2,1)} fusion(bf16[1024,1536]{1,0:T(8,128)(2,1)} %get-tuple-element.115.top_ref, bf16[1024,768]{1,0:T(8,128)(2,1)} %get-tuple-element.121), kind=kOutput, calls=%fused_computation.1 | convolution fusion | flops 2417098752 | bytes 7077888 | tf_op jit(solution)/shard_map/dot_general | solution.py:1963
  369.9 3.9 convolution_convert_fusion.refs_23_
  373.9 105.9 %shard_map.269 = (f32[256,1536]{1,0:T(8,128)}, f32[8,1536]{1,0:T(8,128)}, f32[16,768]{1,0:T(8,128)}, f32[16,256]{1,0:T(8,128)}, f32[192,768]{1,0:T(8,128)}, /*in...) custom-call(bf16[1024,768]{1,0:T(8,128)(2,1)} %get-tuple-element.92.refs_0_, ...), custom_call_target="tpu_custom_call" | custom-call | tf_op jit(solution)/shard_map/pallas_call | solution.py:1330
  479.9 2.9 pad_maximum_fusion
  482.8 0.6 fusion.8
  483.4 0.6 slice.65
  484.0 1.4 slice.57
  485.4 0.6 slice.64
  486.0 0.6 copy.65
  486.6 0.1 reshape_squeeze.3
  486.7 0.7 reduce_sum.9
  487.4 0.6 copy.57
  488.0 0.6 pad_maximum_fusion.2
  488.7 2.2 maximum_bitcast_fusion
  490.8 1.1 copy.68
  492.0 0.8 copy-done.4
  492.8 1.1 copy.69
  (36 shorter events, 0.1 us)
Async XLA Ops:
  244.3 6.7 %copy-start.1 = (bf16[1024,1536]{1,0:T(8,128)(2,1)S(1)}, bf16[1024,1536]{1,0:T(8,128)(2,1)}, u32[]{:S(2)}) copy-start(bf16[1024,1536]{1,0:T(8,128)(2,1)} %get-tuple-element.84.refs_0_.refs_21_) | copy-start | bytes 9437188
  244.3 6.6 %copy-start.5 = (bf16[1024,768]{1,0:T(8,128)(2,1)S(1)}, bf16[1024,768]{1,0:T(8,128)(2,1)}, u32[]{:S(2)}) copy-start(bf16[1024,768]{1,0:T(8,128)(2,1)} %get-tuple-element.110.refs_8_) | copy-start | bytes 4718596
  363.3 6.7 %copy-start = (bf16[1024,1536]{1,0:T(8,128)(2,1)S(1)}, bf16[1024,1536]{1,0:T(8,128)(2,1)}, u32[]{:S(2)}) copy-start(bf16[1024,1536]{1,0:T(8,128)(2,1)} %get-tuple-element.78.refs_0_.refs_21_) | copy-start | bytes 9437188
  363.3 6.7 %copy-start.2 = (bf16[1024,768]{1,0:T(8,128)(2,1)S(1)}, bf16[1024,768]{1,0:T(8,128)(2,1)}, u32[]{:S(2)}) copy-start(bf16[1024,768]{1,0:T(8,128)(2,1)} %get-tuple-element.119.refs_8_) | copy-start | bytes 4718596
  373.9 106.0 %copy-start.6 = (f32[192,768]{1,0:T(8,128)S(1)}, f32[192,768]{1,0:T(8,128)}, u32[]{:S(2)}) copy-start(f32[192,768]{1,0:T(8,128)} %get-tuple-element.130) | copy-start | bytes 1769476
  373.9 106.0 %copy-start.7 = (f32[192,768]{1,0:T(8,128)S(1)}, f32[192,768]{1,0:T(8,128)}, u32[]{:S(2)}) copy-start(f32[192,768]{1,0:T(8,128)} %get-tuple-element.132) | copy-start | bytes 1769476
  479.8 3.0 copy-start.11
  479.9 3.5 copy-start.14
  479.9 7.5 %copy-start.12 = (f32[16,192]{1,0:T(8,128)S(1)}, f32[16,192]{1,0:T(8,128)}, u32[]{:S(2)}) copy-start(f32[16,192]{1,0:T(8,128)} %get-tuple-element.136) | copy-start | bytes 36868
  479.9 7.5 %copy-start.13 = (f32[16,192]{1,0:T(8,128)S(1)}, f32[16,192]{1,0:T(8,128)}, u32[]{:S(2)}) copy-start(f32[16,192]{1,0:T(8,128)} %get-tuple-element.135) | copy-start | bytes 36868
  479.9 8.1 %copy-start.9 = (f32[48,256]{1,0:T(8,128)S(1)}, f32[48,256]{1,0:T(8,128)}, u32[]{:S(2)}) copy-start(f32[48,256]{1,0:T(8,128)} %get-tuple-element.134) | copy-start | bytes 147460
  479.9 8.1 %copy-start.10 = (f32[48,256]{1,0:T(8,128)S(1)}, f32[48,256]{1,0:T(8,128)}, u32[]{:S(2)}) copy-start(f32[48,256]{1,0:T(8,128)} %get-tuple-element.133) | copy-start | bytes 147460
  479.9 8.8 %copy-start.8 = (f32[192,768]{1,0:T(8,128)S(1)}, f32[192,768]{1,0:T(8,128)}, u32[]{:S(2)}) copy-start(f32[192,768]{1,0:T(8,128)} %get-tuple-element.138) | copy-start | bytes 1769476
  482.8 8.0 %copy-start.3 = (f32[256,1536]{1,0:T(8,128)S(1)}, f32[256,1536]{1,0:T(8,128)}, u32[]{:S(2)}) copy-start(f32[256,1536]{1,0:T(8,128)} %get-tuple-element.218) | copy-start | bytes 4718596
  490.8 2.0 copy-start.4

commit v6 on v5

--- a/solution.py
+++ b/solution.py
@@ -416,10 +416,10 @@
     return pl.BlockSpec((CHUNK, cols), lambda i: (i, 0))
 
 
-def forward_in_specs(layer, rows_all, weights, layer_args):
+def forward_in_specs(layer, rows_all, weight_specs, layer_args):
     return (
         [block_rows(rows_all.shape[1])]
-        + [whole_spec(w.shape) for w in weights]
+        + weight_specs
         + [layer_spec(layer, w.shape) for w in layer_args]
         + [block_rows(LANES), pl.BlockSpec((8, CHUNK), lambda i: (0, i))]
     )
@@ -464,7 +464,7 @@
     ]
 
 
-def mix_back_specs(layer, chunks, inner, weights, layer_args, spread):
+def mix_back_specs(layer, chunks, inner, weight_specs, layer_args, spread):
     last = chunks - 1
 
     def turned(cols):
@@ -483,7 +483,7 @@
             turned(inner),
             turned(inner),
         ]
-        + [whole_spec(w.shape) for w in weights]
+        + weight_specs
         + [layer_spec(layer, w.shape) for w in layer_args]
         + [
             whole_spec(spread.shape),
@@ -1406,6 +1406,12 @@
     state_out, raw_out, scale_row, rows_all, refs = *refs[:4], refs[4:]
     wholes, refs = refs[:5], refs[5:]
     scratch, refs = refs[:5], refs[5:]
+    near_weights, load_sems, refs = refs[:5], refs[5], refs[6:]
+    loads = [
+        pltpu.make_async_copy(source, target, load_sems.at[n])
+        for n, (source, target) in enumerate(zip(work[1:6], near_weights))
+    ]
+    work = (work[0], *near_weights, *work[6:])
     part, sq, far, near, mate, land, scale_col, normed = refs[:8]
     refs = refs[8:]
     sems, share_sems, own_sems = refs[:5], refs[5:7], refs[7]
@@ -1432,6 +1438,9 @@
         place, timeline, part, (far, near, mate), reduce_sems, owner, forward, FORWARD_SLOT
     )
     own = [ref.at[1] for ref in own]
+    for copy in loads:
+        timeline.add(-2.0, copy.start)
+        timeline.add(0.6, copy.wait)
     weight_gather(place, timeline, own, wholes, sems, share_sems, own_sems)
     block = pl.ds(pl.multiple_of(place.t * rows, rows), rows)
     keep = pltpu.make_async_copy(normed, rows_all.at[block, :], local.at[0])
@@ -1473,14 +1482,16 @@
         ]
         + gather_outputs(line, width, inner, 2 * line)
     )
-    scratch = forward_scratch(inner) + row_scratch(length, rows, width)
+    scratch = forward_scratch(inner)
+    scratch += [pltpu.VMEM(array.shape, array.dtype) for array in weights]
+    scratch += [pltpu.SemaphoreType.DMA((5,))] + row_scratch(length, rows, width)
     scratch += [pltpu.VMEM((rows, width), BF16)]
     scratch += gather_scratch(line) + reduce_semaphores() + share_semaphores() + spread_semaphores()
     scratch += [pltpu.SemaphoreType.DMA((1,))]
     return call_kernel(
         functools.partial(middle_kernel, line, inner_all),
         outs,
-        forward_in_specs(0, rows_all, weights, layer_args)
+        forward_in_specs(0, rows_all, [ANY] * 5, layer_args)
         + [whole_spec(resid.shape), whole_spec(gain.shape)]
         + [ANY] * 5,
         saved_specs(inner)
@@ -1570,7 +1581,7 @@
     return call_kernel(
         functools.partial(top_kernel, line, inner_all),
         saved_shapes(length, inner) + [shape((rows, width), F32), shape((8, length), F32)],
-        forward_in_specs(1, rows_all, weights, layer_args)
+        forward_in_specs(1, rows_all, [whole_spec(w.shape) for w in weights], layer_args)
         + [whole_spec(state.shape), whole_spec(cotangent.shape)],
         saved_specs(inner) + [whole_spec((rows, width)), whole_spec((8, length))],
         scratch,
@@ -1732,8 +1743,10 @@
         grad_out, gnorm, per_row, top_all, small, small_bc, refs = *refs[:6], refs[6:]
     outs, refs = refs[:5], refs[5:]
     scratch, refs = refs[:7], refs[7:]
-    near_side, load_sems, refs = refs[:5], refs[5], refs[6:]
-    rows_all, dout, dgate, before, state = near_side
+    near_side, load_sems, refs = refs[:9], refs[9], refs[10:]
+    rows_all, dout, dgate, before, state = near_side[:5]
+    far_side = (*far_side, *work[10:14])
+    work = (*work[:10], *near_side[5:], *work[14:])
     loads = [
         pltpu.make_async_copy(source, target, load_sems.at[n])
         for n, (source, target) in enumerate(zip(far_side, near_side))
@@ -1772,13 +1785,15 @@
             gnorm[...] = jnp.zeros_like(gnorm)
 
     def load():
-        for n in (1, 2, 3, 4, 0):
+        for n in (1, 2, 3, 4, 0, 5, 6, 7, 8):
             loads[n].start()
 
     timeline.add(-2.0, load)
     timeline.add(-2.0, clear)
     for n in (1, 2, 3, 4, 0):
         timeline.add(2.5 if n in (1, 2) else BACKWARD_US / 2, loads[n].wait)
+    for n in (5, 6, 7, 8):
+        timeline.add(BACKWARD_US * 0.8, loads[n].wait)
 
     def own_gain():
         return gain[0:1, :] if final else gain[1:2, :]
@@ -1909,8 +1924,9 @@
         out_specs[3] = ANY
     tail_outs = scatter_outputs(width, inner, dp)
     scratch = mix_back_scratch(inner)
-    scratch += [pltpu.VMEM(array.shape, array.dtype) for array in far_side]
-    scratch += [pltpu.SemaphoreType.DMA((5,))]
+    weights = weights[:4]
+    scratch += [pltpu.VMEM(array.shape, array.dtype) for array in (*far_side, *weights)]
+    scratch += [pltpu.SemaphoreType.DMA((9,))]
     scratch += [
         pltpu.VMEM((length, width), BF16),
         pltpu.VMEM((length, inner), BF16),
@@ -1940,11 +1956,10 @@
             pltpu.VMEM((rows, width), BF16),
         ]
         scratch += share_semaphores() + spread_semaphores() + [pltpu.SemaphoreType.DMA((1,))]
-    weights = weights[:4]
     return call_kernel(
         functools.partial(pull_kernel, line, inner_all, final),
         outs + tail_outs,
-        mix_back_specs(layer, length // CHUNK, inner, weights, layer_args, spread)
+        mix_back_specs(layer, length // CHUNK, inner, [ANY] * 4, layer_args, spread)
         + [ANY] * 5
         + [whole_spec(gain.shape)]
         + [whole_spec(array.shape) for array in more],

time: 498 us -> 493 us (0.990)
  no operation moved by 1% of the time
where the time goes in v6:
time: 493 us; the launch traced here: 490 us
  Pallas kernels  444 us (90%)
  matrix products  21.2 us (4%)
  local copies, waits for them, and re-layouts  13 us (3%)
  other arithmetic  10.5 us (2%)
    pallas_call x5, Pallas kernels, call_kernel(): pl.pallas_call(kernel, grid=grid, out_shape=outs, in_specs=in_specs, out_...  426 us
    dot_general x4, matrix products, contract_wide(): lax.dot_general(left, right, (((0,), (0,)), ((), ())), preferred_element_...  21.2 us
    pallas_call x2, Pallas kernels, gate_back(): pl.pallas_call(gate_back_kernel, grid=(length // CHUNK,), in_specs=[block...  17.8 us

profile of v6, /device:TPU:0, one launch (start us, length us, event | category | flops | bytes accessed | tf_op | source)
XLA Modules:
  0.0 489.7 jit_solution(6984004876277258843)
XLA Ops:
  0.6 0.7 exponential_negate_fusion
  1.3 1.3 select_maximum_fusion.refs_8_.refs_16_
  2.6 0.7 convert_element_type.43
  3.3 0.1 slice.51
  3.4 0.1 compare_convert_fusion.2
  3.5 0.1 pad_maximum_fusion.5
  3.5 0.1 broadcast_bitcast_fusion.2
  3.6 0.1 broadcast_bitcast_fusion
  3.7 0.1 broadcast_bitcast_fusion.1
  3.8 0.7 stack.118
  4.5 0.1 fusion.10
  4.5 0.1 fusion.9
  4.6 0.1 fusion.11
  4.7 0.8 fusion.4
  5.5 0.2 stack.137
  5.7 0.7 copy.64
  6.4 0.6 pad.16.refs_3_.refs_17_
  7.0 0.7 broadcast_in_dim.17
  7.8 0.1 stack_reshape.4
  7.8 0.6 pad_maximum_fusion.4.refs_9_.wide_ref.refs_17_
  8.5 0.6 broadcast_in_dim.21.refs_11_.refs_20_
  9.1 0.2 copy.55
  9.3 0.8 pad.18.refs_10_.refs_19_
  10.1 81.1 %shard_map.263 = (bf16[1536,768]{1,0:T(8,128)(2,1)}, bf16[1536,768]{1,0:T(8,128)(2,1)}, bf16[1536,768]{1,0:T(8,128)(2,1)}, bf16[8,16,192]{2,1,0:T(8,128)(2,1)}, ...) custom-call(bf16[256,1536]{1,0:T(8,128)(2,1)} %refs_25_.1, ...), custom_call_target="tpu_custom_call" | custom-call | tf_op jit(solution)/shard_map/pallas_call | solution.py:1330
  91.2 86.1 %shard_map.264 = (bf16[1024,768]{1,0:T(8,128)(2,1)}, bf16[1024,768]{1,0:T(8,128)(2,1)}, f32[1024,768]{1,0:T(8,128)}, f32[1024,256]{1,0:T(8,128)}, f32[1024,256]{...) custom-call(bf16[1024,1536]{1,0:T(8,128)(2,1)} %get-tuple-element.78, ...), custom_call_target="tpu_custom_call" | custom-call | tf_op jit(solution)/shard_map/pallas_call | solution.py:1330
  177.2 58.0 %shard_map.265 = (bf16[1024,768]{1,0:T(8,128)(2,1)}, bf16[1024,768]{1,0:T(8,128)(2,1)}, f32[1024,768]{1,0:T(8,128)}, f32[1024,256]{1,0:T(8,128)}, f32[1024,256]{...) custom-call(bf16[1024,1536]{1,0:T(8,128)(2,1)} %get-tuple-element.84, ...), custom_call_target="tpu_custom_call" | custom-call | tf_op jit(solution)/shard_map/pallas_call | solution.py:1330
  235.3 8.9 %shard_map.266 = (bf16[1024,768]{1,0:T(8,128)(2,1)}, bf16[1024,768]{1,0:T(8,128)(2,1)}, bf16[1024,768]{1,0:T(8,128)(2,1)}, f32[8,768]{1,0:T(8,128)}) custom-call(bf16[1024,1536]{1,0:T(8,128)(2,1)} %get-tuple-element.106.top_ref, f32[8,1024]{1,0:T(8,128)} %get-tuple-element.107.sc_ref, bf16[1024,768]{1,0:T(8,128)(2,1)} %get-tuple-element.108.gate_ref, ...), custom_call_target="tpu_custom_call" | custom-call | tf_op jit(solution)/shard_map/pallas_call | solution.py:234
  244.2 6.6 %convolution_convert_fusion.3.refs_22_ = bf16[1536,768]{1,0:T(8,128)(2,1)} fusion(bf16[1024,1536]{1,0:T(8,128)(2,1)} %get-tuple-element.106.top_ref, bf16[1024,768]{1,0:T(8,128)(2,1)} %get-tuple-element.112), kind=kOutput, calls=%fused_computation.3 | convolution fusion | flops 2417098752 | bytes 7077888 | tf_op jit(solution)/shard_map/dot_general | solution.py:1978
  250.8 4.0 convolution_convert_fusion.2.refs_23_
  254.8 97.6 %shard_map.267 = (f32[256,1536]{1,0:T(8,128)}, f32[8,1536]{1,0:T(8,128)}, f32[8,1024]{1,0:T(8,128)}, bf16[1024,1536]{1,0:T(8,128)(2,1)}, f32[8,768]{1,0:T(8,128)...) custom-call(bf16[1024,768]{1,0:T(8,128)(2,1)} %get-tuple-element.99., ...), custom_call_target="tpu_custom_call" | custom-call | tf_op jit(solution)/shard_map/pallas_call | solution.py:1330
  352.4 8.9 %shard_map.268 = (bf16[1024,768]{1,0:T(8,128)(2,1)}, bf16[1024,768]{1,0:T(8,128)(2,1)}, bf16[1024,768]{1,0:T(8,128)(2,1)}, f32[8,768]{1,0:T(8,128)}) custom-call(bf16[1024,1536]{1,0:T(8,128)(2,1)} %get-tuple-element.115.top_ref, f32[8,1024]{1,0:T(8,128)} %get-tuple-element.116.sc_ref, bf16[1024,768]{1,0:T(8,128)(2,1)} %get-tuple-element.117.gate_ref, ...), custom_call_target="tpu_custom_call" | custom-call | tf_op jit(solution)/shard_map/pallas_call | solution.py:234
  361.3 6.6 %convolution_convert_fusion.1.refs_22_ = bf16[1536,768]{1,0:T(8,128)(2,1)} fusion(bf16[1024,1536]{1,0:T(8,128)(2,1)} %get-tuple-element.115.top_ref, bf16[1024,768]{1,0:T(8,128)(2,1)} %get-tuple-element.121), kind=kOutput, calls=%fused_computation.1 | convolution fusion | flops 2417098752 | bytes 7077888 | tf_op jit(solution)/shard_map/dot_general | solution.py:1978
  367.9 3.9 convolution_convert_fusion.refs_23_
  371.9 103.5 %shard_map.269 = (f32[256,1536]{1,0:T(8,128)}, f32[8,1536]{1,0:T(8,128)}, f32[16,768]{1,0:T(8,128)}, f32[16,256]{1,0:T(8,128)}, f32[192,768]{1,0:T(8,128)}, /*in...) custom-call(bf16[1024,768]{1,0:T(8,128)(2,1)} %get-tuple-element.92.refs_0_, ...), custom_call_target="tpu_custom_call" | custom-call | tf_op jit(solution)/shard_map/pallas_call | solution.py:1330
  475.5 2.9 pad_maximum_fusion
  478.4 0.6 fusion.8
  478.9 0.6 slice.65
  479.5 1.4 slice.57
  481.0 0.6 slice.64
  481.6 0.6 copy.65
  482.2 0.1 reshape_squeeze.3
  482.3 0.7 reduce_sum.9
  482.9 0.6 copy.57
  483.6 0.6 pad_maximum_fusion.2
  484.2 2.2 maximum_bitcast_fusion
  486.4 1.1 copy.68
  487.5 0.8 copy-done.4
  488.4 1.1 copy.69
  (36 shorter events, 0.1 us)
Async XLA Ops:
  244.2 6.7 %copy-start.1 = (bf16[1024,1536]{1,0:T(8,128)(2,1)S(1)}, bf16[1024,1536]{1,0:T(8,128)(2,1)}, u32[]{:S(2)}) copy-start(bf16[1024,1536]{1,0:T(8,128)(2,1)} %get-tuple-element.84.refs_0_.refs_21_) | copy-start | bytes 9437188
  244.2 6.6 %copy-start.5 = (bf16[1024,768]{1,0:T(8,128)(2,1)S(1)}, bf16[1024,768]{1,0:T(8,128)(2,1)}, u32[]{:S(2)}) copy-start(bf16[1024,768]{1,0:T(8,128)(2,1)} %get-tuple-element.110.refs_8_) | copy-start | bytes 4718596
  361.3 6.7 %copy-start = (bf16[1024,1536]{1,0:T(8,128)(2,1)S(1)}, bf16[1024,1536]{1,0:T(8,128)(2,1)}, u32[]{:S(2)}) copy-start(bf16[1024,1536]{1,0:T(8,128)(2,1)} %get-tuple-element.78.refs_0_.refs_21_) | copy-start | bytes 9437188
  361.3 6.7 %copy-start.2 = (bf16[1024,768]{1,0:T(8,128)(2,1)S(1)}, bf16[1024,768]{1,0:T(8,128)(2,1)}, u32[]{:S(2)}) copy-start(bf16[1024,768]{1,0:T(8,128)(2,1)} %get-tuple-element.119.refs_8_) | copy-start | bytes 4718596
  371.9 103.5 %copy-start.6 = (f32[192,768]{1,0:T(8,128)S(1)}, f32[192,768]{1,0:T(8,128)}, u32[]{:S(2)}) copy-start(f32[192,768]{1,0:T(8,128)} %get-tuple-element.130) | copy-start | bytes 1769476
  371.9 103.5 %copy-start.7 = (f32[192,768]{1,0:T(8,128)S(1)}, f32[192,768]{1,0:T(8,128)}, u32[]{:S(2)}) copy-start(f32[192,768]{1,0:T(8,128)} %get-tuple-element.132) | copy-start | bytes 1769476
  475.4 3.0 copy-start.11
  475.4 3.5 copy-start.14
  475.4 7.5 %copy-start.12 = (f32[16,192]{1,0:T(8,128)S(1)}, f32[16,192]{1,0:T(8,128)}, u32[]{:S(2)}) copy-start(f32[16,192]{1,0:T(8,128)} %get-tuple-element.136) | copy-start | bytes 36868
  475.4 7.5 %copy-start.13 = (f32[16,192]{1,0:T(8,128)S(1)}, f32[16,192]{1,0:T(8,128)}, u32[]{:S(2)}) copy-start(f32[16,192]{1,0:T(8,128)} %get-tuple-element.135) | copy-start | bytes 36868
  475.4 8.1 %copy-start.9 = (f32[48,256]{1,0:T(8,128)S(1)}, f32[48,256]{1,0:T(8,128)}, u32[]{:S(2)}) copy-start(f32[48,256]{1,0:T(8,128)} %get-tuple-element.134) | copy-start | bytes 147460
  475.4 8.1 %copy-start.10 = (f32[48,256]{1,0:T(8,128)S(1)}, f32[48,256]{1,0:T(8,128)}, u32[]{:S(2)}) copy-start(f32[48,256]{1,0:T(8,128)} %get-tuple-element.133) | copy-start | bytes 147460
  475.4 8.8 %copy-start.8 = (f32[192,768]{1,0:T(8,128)S(1)}, f32[192,768]{1,0:T(8,128)}, u32[]{:S(2)}) copy-start(f32[192,768]{1,0:T(8,128)} %get-tuple-element.138) | copy-start | bytes 1769476
  478.4 8.0 %copy-start.3 = (f32[256,1536]{1,0:T(8,128)S(1)}, f32[256,1536]{1,0:T(8,128)}, u32[]{:S(2)}) copy-start(f32[256,1536]{1,0:T(8,128)} %get-tuple-element.218) | copy-start | bytes 4718596
  486.4 2.0 copy-start.4

commit v7 on v6

--- a/solution.py
+++ b/solution.py
@@ -1863,8 +1863,8 @@
             timeline.add(end, take)
 
         when = BACKWARD_US * (chunks + (4 + 3 * (PIECES - 1)) / EIGHTHS) + END_LAG + 0.5
-        steps = [(len(bits), across[0], 3.0), (len(bits) + 1, across[1], 5.0)]
-        steps += [(n, along[n], 7.0) for n in range(len(bits))][::-1]
+        steps = [(len(bits), across[0], 2.5), (len(bits) + 1, across[1], 4.0)]
+        steps += [(n, along[n], 5.0) for n in range(len(bits))][::-1]
         for n, partner, wait in steps:
             group = [(0, bc_sums, bc_land_sums), (1, norm_sum, norm_land)]
             if n < len(bits):

time: 493 us -> 491 us (level)
  no operation moved by 1% of the time
where the time goes in v7:
time: 491 us; the launch traced here: 487 us
  Pallas kernels  442 us (90%)
  matrix products  21.2 us (4%)
  local copies, waits for them, and re-layouts  13 us (3%)
  other arithmetic  10.5 us (2%)
    pallas_call x5, Pallas kernels, call_kernel(): pl.pallas_call(kernel, grid=grid, out_shape=outs, in_specs=in_specs, out_...  424 us
    dot_general x4, matrix products, contract_wide(): lax.dot_general(left, right, (((0,), (0,)), ((), ())), preferred_element_...  21.2 us
    pallas_call x2, Pallas kernels, gate_back(): pl.pallas_call(gate_back_kernel, grid=(length // CHUNK,), in_specs=[block...  17.8 us

profile of v7, /device:TPU:0, one launch (start us, length us, event | category | flops | bytes accessed | tf_op | source)
XLA Modules:
  0.0 487.3 jit_solution(16308557039429340647)
XLA Ops:
  0.6 0.7 exponential_negate_fusion
  1.3 1.3 select_maximum_fusion.refs_8_.refs_16_
  2.6 0.7 convert_element_type.43
  3.3 0.1 slice.51
  3.4 0.1 compare_convert_fusion.2
  3.5 0.1 pad_maximum_fusion.5
  3.5 0.1 broadcast_bitcast_fusion.2
  3.6 0.1 broadcast_bitcast_fusion
  3.7 0.1 broadcast_bitcast_fusion.1
  3.8 0.7 stack.118
  4.5 0.1 fusion.10
  4.5 0.1 fusion.9
  4.6 0.1 fusion.11
  4.7 0.8 fusion.4
  5.5 0.2 stack.137
  5.7 0.7 copy.64
  6.4 0.6 pad.16.refs_3_.refs_17_
  7.0 0.7 broadcast_in_dim.17
  7.8 0.1 stack_reshape.4
  7.8 0.6 pad_maximum_fusion.4.refs_9_.wide_ref.refs_17_
  8.5 0.6 broadcast_in_dim.21.refs_11_.refs_20_
  9.1 0.2 copy.55
  9.3 0.8 pad.18.refs_10_.refs_19_
  10.1 81.1 %shard_map.263 = (bf16[1536,768]{1,0:T(8,128)(2,1)}, bf16[1536,768]{1,0:T(8,128)(2,1)}, bf16[1536,768]{1,0:T(8,128)(2,1)}, bf16[8,16,192]{2,1,0:T(8,128)(2,1)}, ...) custom-call(bf16[256,1536]{1,0:T(8,128)(2,1)} %refs_25_.1, ...), custom_call_target="tpu_custom_call" | custom-call | tf_op jit(solution)/shard_map/pallas_call | solution.py:1330
  91.2 86.1 %shard_map.264 = (bf16[1024,768]{1,0:T(8,128)(2,1)}, bf16[1024,768]{1,0:T(8,128)(2,1)}, f32[1024,768]{1,0:T(8,128)}, f32[1024,256]{1,0:T(8,128)}, f32[1024,256]{...) custom-call(bf16[1024,1536]{1,0:T(8,128)(2,1)} %get-tuple-element.78, ...), custom_call_target="tpu_custom_call" | custom-call | tf_op jit(solution)/shard_map/pallas_call | solution.py:1330
  177.2 58.0 %shard_map.265 = (bf16[1024,768]{1,0:T(8,128)(2,1)}, bf16[1024,768]{1,0:T(8,128)(2,1)}, f32[1024,768]{1,0:T(8,128)}, f32[1024,256]{1,0:T(8,128)}, f32[1024,256]{...) custom-call(bf16[1024,1536]{1,0:T(8,128)(2,1)} %get-tuple-element.84, ...), custom_call_target="tpu_custom_call" | custom-call | tf_op jit(solution)/shard_map/pallas_call | solution.py:1330
  235.3 8.9 %shard_map.266 = (bf16[1024,768]{1,0:T(8,128)(2,1)}, bf16[1024,768]{1,0:T(8,128)(2,1)}, bf16[1024,768]{1,0:T(8,128)(2,1)}, f32[8,768]{1,0:T(8,128)}) custom-call(bf16[1024,1536]{1,0:T(8,128)(2,1)} %get-tuple-element.106.top_ref, f32[8,1024]{1,0:T(8,128)} %get-tuple-element.107.sc_ref, bf16[1024,768]{1,0:T(8,128)(2,1)} %get-tuple-element.108.gate_ref, ...), custom_call_target="tpu_custom_call" | custom-call | tf_op jit(solution)/shard_map/pallas_call | solution.py:234
  244.2 6.6 %convolution_convert_fusion.3.refs_22_ = bf16[1536,768]{1,0:T(8,128)(2,1)} fusion(bf16[1024,1536]{1,0:T(8,128)(2,1)} %get-tuple-element.106.top_ref, bf16[1024,768]{1,0:T(8,128)(2,1)} %get-tuple-element.112), kind=kOutput, calls=%fused_computation.3 | convolution fusion | flops 2417098752 | bytes 7077888 | tf_op jit(solution)/shard_map/dot_general | solution.py:1978
  250.8 4.0 convolution_convert_fusion.2.refs_23_
  254.8 97.6 %shard_map.267 = (f32[256,1536]{1,0:T(8,128)}, f32[8,1536]{1,0:T(8,128)}, f32[8,1024]{1,0:T(8,128)}, bf16[1024,1536]{1,0:T(8,128)(2,1)}, f32[8,768]{1,0:T(8,128)...) custom-call(bf16[1024,768]{1,0:T(8,128)(2,1)} %get-tuple-element.99., ...), custom_call_target="tpu_custom_call" | custom-call | tf_op jit(solution)/shard_map/pallas_call | solution.py:1330
  352.4 8.9 %shard_map.268 = (bf16[1024,768]{1,0:T(8,128)(2,1)}, bf16[1024,768]{1,0:T(8,128)(2,1)}, bf16[1024,768]{1,0:T(8,128)(2,1)}, f32[8,768]{1,0:T(8,128)}) custom-call(bf16[1024,1536]{1,0:T(8,128)(2,1)} %get-tuple-element.115.top_ref, f32[8,1024]{1,0:T(8,128)} %get-tuple-element.116.sc_ref, bf16[1024,768]{1,0:T(8,128)(2,1)} %get-tuple-element.117.gate_ref, ...), custom_call_target="tpu_custom_call" | custom-call | tf_op jit(solution)/shard_map/pallas_call | solution.py:234
  361.3 6.6 %convolution_convert_fusion.1.refs_22_ = bf16[1536,768]{1,0:T(8,128)(2,1)} fusion(bf16[1024,1536]{1,0:T(8,128)(2,1)} %get-tuple-element.115.top_ref, bf16[1024,768]{1,0:T(8,128)(2,1)} %get-tuple-element.121), kind=kOutput, calls=%fused_computation.1 | convolution fusion | flops 2417098752 | bytes 7077888 | tf_op jit(solution)/shard_map/dot_general | solution.py:1978
  367.9 3.9 convolution_convert_fusion.refs_23_
  371.9 101.1 %shard_map.269 = (f32[256,1536]{1,0:T(8,128)}, f32[8,1536]{1,0:T(8,128)}, f32[16,768]{1,0:T(8,128)}, f32[16,256]{1,0:T(8,128)}, f32[192,768]{1,0:T(8,128)}, /*in...) custom-call(bf16[1024,768]{1,0:T(8,128)(2,1)} %get-tuple-element.92.refs_0_, ...), custom_call_target="tpu_custom_call" | custom-call | tf_op jit(solution)/shard_map/pallas_call | solution.py:1330
  473.1 2.9 pad_maximum_fusion
  476.0 0.6 fusion.8
  476.6 0.6 slice.65
  477.2 1.4 slice.57
  478.6 0.6 slice.64
  479.2 0.6 copy.65
  479.8 0.1 reshape_squeeze.3
  479.9 0.7 reduce_sum.9
  480.6 0.6 copy.57
  481.2 0.6 pad_maximum_fusion.2
  481.9 2.2 maximum_bitcast_fusion
  484.0 1.1 copy.68
  485.2 0.8 copy-done.4
  486.0 1.1 copy.69
  (36 shorter events, 0.1 us)
Async XLA Ops:
  244.2 6.7 %copy-start.1 = (bf16[1024,1536]{1,0:T(8,128)(2,1)S(1)}, bf16[1024,1536]{1,0:T(8,128)(2,1)}, u32[]{:S(2)}) copy-start(bf16[1024,1536]{1,0:T(8,128)(2,1)} %get-tuple-element.84.refs_0_.refs_21_) | copy-start | bytes 9437188
  244.2 6.6 %copy-start.5 = (bf16[1024,768]{1,0:T(8,128)(2,1)S(1)}, bf16[1024,768]{1,0:T(8,128)(2,1)}, u32[]{:S(2)}) copy-start(bf16[1024,768]{1,0:T(8,128)(2,1)} %get-tuple-element.110.refs_8_) | copy-start | bytes 4718596
  361.3 6.7 %copy-start = (bf16[1024,1536]{1,0:T(8,128)(2,1)S(1)}, bf16[1024,1536]{1,0:T(8,128)(2,1)}, u32[]{:S(2)}) copy-start(bf16[1024,1536]{1,0:T(8,128)(2,1)} %get-tuple-element.78.refs_0_.refs_21_) | copy-start | bytes 9437188
  361.3 6.7 %copy-start.2 = (bf16[1024,768]{1,0:T(8,128)(2,1)S(1)}, bf16[1024,768]{1,0:T(8,128)(2,1)}, u32[]{:S(2)}) copy-start(bf16[1024,768]{1,0:T(8,128)(2,1)} %get-tuple-element.119.refs_8_) | copy-start | bytes 4718596
  371.9 101.2 %copy-start.6 = (f32[192,768]{1,0:T(8,128)S(1)}, f32[192,768]{1,0:T(8,128)}, u32[]{:S(2)}) copy-start(f32[192,768]{1,0:T(8,128)} %get-tuple-element.130) | copy-start | bytes 1769476
  371.9 101.2 %copy-start.7 = (f32[192,768]{1,0:T(8,128)S(1)}, f32[192,768]{1,0:T(8,128)}, u32[]{:S(2)}) copy-start(f32[192,768]{1,0:T(8,128)} %get-tuple-element.132) | copy-start | bytes 1769476
  473.0 3.0 copy-start.11
  473.0 3.5 copy-start.14
  473.1 7.5 %copy-start.12 = (f32[16,192]{1,0:T(8,128)S(1)}, f32[16,192]{1,0:T(8,128)}, u32[]{:S(2)}) copy-start(f32[16,192]{1,0:T(8,128)} %get-tuple-element.136) | copy-start | bytes 36868
  473.1 7.5 %copy-start.13 = (f32[16,192]{1,0:T(8,128)S(1)}, f32[16,192]{1,0:T(8,128)}, u32[]{:S(2)}) copy-start(f32[16,192]{1,0:T(8,128)} %get-tuple-element.135) | copy-start | bytes 36868
  473.1 8.1 %copy-start.9 = (f32[48,256]{1,0:T(8,128)S(1)}, f32[48,256]{1,0:T(8,128)}, u32[]{:S(2)}) copy-start(f32[48,256]{1,0:T(8,128)} %get-tuple-element.134) | copy-start | bytes 147460
  473.1 8.1 %copy-start.10 = (f32[48,256]{1,0:T(8,128)S(1)}, f32[48,256]{1,0:T(8,128)}, u32[]{:S(2)}) copy-start(f32[48,256]{1,0:T(8,128)} %get-tuple-element.133) | copy-start | bytes 147460
  473.1 8.8 %copy-start.8 = (f32[192,768]{1,0:T(8,128)S(1)}, f32[192,768]{1,0:T(8,128)}, u32[]{:S(2)}) copy-start(f32[192,768]{1,0:T(8,128)} %get-tuple-element.138) | copy-start | bytes 1769476
  476.0 8.0 %copy-start.3 = (f32[256,1536]{1,0:T(8,128)S(1)}, f32[256,1536]{1,0:T(8,128)}, u32[]{:S(2)}) copy-start(f32[256,1536]{1,0:T(8,128)} %get-tuple-element.218) | copy-start | bytes 4718596
  484.0 2.0 copy-start.4
